TPU v7x, 32 devices: a whole 2x2x4 slice. The times are simulated.
32 devices in a mesh: rows: 16 (over z, y, core), ch: 2 (over x).
Axes of the slice: x: 2, y: 2, z: 4, core: 2. Of those that a mesh axis runs over, the one named last changes fastest.
Arguments:
- images: bfloat16 [4, 256, 64, 96], P(None, 'rows', None, 'ch'), may hold values from -6 to 6
- valid_h: int32 [4, 4], replicated, may hold values from 48 to 64
- valid_w: int32 [4, 4], replicated, may hold values from 32 to 64
- kernel_one: bfloat16 [3, 3, 96, 192], P(None, None, None, 'ch'), may hold values from -0.21875 to 0.21875
- kernel_two: bfloat16 [3, 3, 192, 192], P(None, None, None, 'ch'), may hold values from -0.15625 to 0.15625
- kernel_skip: bfloat16 [96, 192], P(None, 'ch'), may hold values from -0.625 to 0.625
- bias_one: bfloat16 [192], P('ch'), may hold values from -3 to 3
- bias_two: bfloat16 [192], P('ch'), may hold values from -3 to 3
- vector_one: float32 [192], P('ch'), may hold values from -6 to 6
- vector_two: float32 [192], P('ch'), may hold values from -6 to 6
- vector_skip: float32 [192], P('ch'), may hold values from -6 to 6
- cotangent: bfloat16 [4, 128, 32, 192], P(None, 'rows', None, 'ch'), may hold values from -6 to 6
Outputs:
- block_output: bfloat16 [4, 128, 32, 192], P(None, 'rows', None, 'ch')
- input_grad: bfloat16 [4, 256, 64, 96], P(None, 'rows', None, 'ch')
- grad_kernel_one: float32 [3, 3, 96, 192], P(None, None, None, 'ch')
- grad_kernel_two: float32 [3, 3, 192, 192], P(None, None, None, 'ch')
- grad_kernel_skip: float32 [96, 192], P(None, 'ch')
- grad_bias_one: float32 [192], P('ch')
- grad_bias_two: float32 [192], P('ch')
All inputs are finite; a program needn't handle non-finite values.
Results may differ from a plain program's by a relative error of at most 0.0056.
The roundings to bfloat16 on the way count: a program that leaves them out, or rounds other values in their place, can miss the bound.
Values may be sent and summed in bfloat16 or wider, within the bound.
A program may use at most 128 MiB of HBM per device.

v0:
```python
import jax
import jax.numpy as jnp
from jax import lax
from jax.sharding import PartitionSpec as P

IMG = 64
SHIFT = 40


EPS = 1e-06
HIGH = lax.Precision.HIGHEST


def extended(cells, sides, width):
    for axis, dim in sides:
        count = lax.axis_size(axis)
        head = lax.slice_in_dim(cells, 0, width, axis=dim)
        tail = lax.slice_in_dim(cells, cells.shape[dim] - width, cells.shape[dim], axis=dim)
        cells = jnp.concatenate(
            [
                lax.ppermute(tail, axis, [(i, (i + 1) % count) for i in range(count)]),
                cells,
                lax.ppermute(head, axis, [((i + 1) % count, i) for i in range(count)]),
            ],
            axis=dim,
        )
    return cells


def conv_rows(rim, kernel, taps):
    slab_rows = taps.shape[1]
    result = None
    for row_tap in range(3):
        part = lax.conv_general_dilated(
            rim[None, row_tap : row_tap + slab_rows],
            kernel[row_tap : row_tap + 1],
            (1, 1),
            ((0, 0), (1, 1)),
            dimension_numbers=("NHWC", "HWIO", "NHWC"),
            preferred_element_type=jnp.float32,
        )
        part = part[0] * taps[row_tap][:, None, None]
        result = part if result is None else result + part
    return result


def flipped(kernel):
    return jnp.transpose(kernel[::-1, ::-1], (0, 1, 3, 2))


def kernel_taps(rim, grad, taps_low):
    slab_rows = grad.shape[0]
    width = grad.shape[1]
    padded = jnp.pad(rim, ((0, 0), (1, 1), (0, 0)))
    stacked = []
    for row_tap in range(3):
        kept_grad = grad * taps_low[row_tap][:, None, None]
        line = []
        for col_tap in range(3):
            window = padded[row_tap : row_tap + slab_rows, col_tap : col_tap + width]
            line.append(
                jnp.einsum("rci,rco->io", window, kept_grad, preferred_element_type=jnp.float32)
            )
        stacked.append(jnp.stack(line))
    return jnp.stack(stacked)


def silu_slope(value):
    gate = jax.nn.sigmoid(value)
    return gate + value * gate * (1.0 - gate)


def shards(
    images,
    valid_h,
    valid_w,
    kernel_one,
    kernel_two,
    kernel_skip,
    bias_one,
    bias_two,
    vector_one,
    vector_two,
    vector_skip,
    cotangent,
):
    micros, rows_dev, width, in_local = images.shape
    out_local = kernel_one.shape[3]
    count_images = valid_h.shape[1]
    total_rows = rows_dev * lax.axis_size("rows")
    slab_start = lax.axis_index("rows") * rows_dev
    rim_global = slab_start - 1 + jnp.arange(rows_dev + 2, dtype=jnp.int32)
    placed = jnp.mod(rim_global - SHIFT, total_rows)
    image_of = placed // IMG
    row_of = placed % IMG
    taps = jnp.stack(
        [image_of[tap : tap + rows_dev] == image_of[1 : rows_dev + 1] for tap in range(3)]
    ).astype(jnp.float32)
    taps_low = taps.astype(jnp.bfloat16)
    owner = image_of[:, None] == jnp.arange(count_images, dtype=jnp.int32)[None, :]
    columns = jnp.arange(width)
    kern_one = kernel_one.astype(jnp.float32)
    kern_two = kernel_two.astype(jnp.float32)
    kern_skip = kernel_skip.astype(jnp.float32).reshape(1, 1, -1, out_local)
    part_one = jnp.einsum("hwio,o->hwi", kern_one, vector_one, precision=HIGH)
    part_two = jnp.einsum("hwio,o->hwi", kern_two, vector_two, precision=HIGH)
    part_skip = jnp.einsum("hwio,o->hwi", kern_skip, vector_skip, precision=HIGH)
    left_one, left_two, left_skip = lax.psum((part_one, part_two, part_skip), "ch")
    left_one = left_one * lax.rsqrt(jnp.sum(left_one * left_one) + EPS)
    left_two = left_two * lax.rsqrt(jnp.sum(left_two * left_two) + EPS)
    left_skip = left_skip * lax.rsqrt(jnp.sum(left_skip * left_skip) + EPS)
    image_one = jnp.einsum("hwio,hwi->o", kern_one, left_one, precision=HIGH)
    image_two = jnp.einsum("hwio,hwi->o", kern_two, left_two, precision=HIGH)
    image_skip = jnp.einsum("hwio,hwi->o", kern_skip, left_skip, precision=HIGH)
    square_one, square_two, square_skip = lax.psum(
        (
            jnp.sum(image_one * image_one),
            jnp.sum(image_two * image_two),
            jnp.sum(image_skip * image_skip),
        ),
        "ch",
    )
    scale_one = lax.rsqrt(square_one + EPS)
    scale_two = lax.rsqrt(square_two + EPS)
    scale_skip = lax.rsqrt(square_skip + EPS)
    right_one = image_one * scale_one
    right_two = image_two * scale_two
    right_skip = image_skip * scale_skip
    sigma_one = square_one * scale_one
    sigma_two = square_two * scale_two
    sigma_skip = square_skip * scale_skip
    eff_one = (kern_one / sigma_one).astype(jnp.bfloat16)
    eff_two = (kern_two / sigma_two).astype(jnp.bfloat16)
    eff_skip_full = (kern_skip / sigma_skip).astype(jnp.bfloat16)
    eff_skip = eff_skip_full[0, 0]
    bias_first = bias_one.astype(jnp.float32)
    bias_second = bias_two.astype(jnp.float32)
    back_two = flipped(eff_two)
    back_one = flipped(eff_one)
    outputs = []
    in_grads = []
    totals = None
    for micro in range(micros):
        height_rows = jnp.sum(jnp.where(owner, valid_h[micro][None, :], 0), axis=1)
        width_rows = jnp.sum(jnp.where(owner, valid_w[micro][None, :], 0), axis=1)
        mask_rim = (
            (row_of < height_rows)[:, None] & (columns[None, :] < width_rows[:, None])
        ).astype(jnp.float32)[:, :, None]
        mask_in = mask_rim[1:-1]
        input_rim = extended(images[micro], (("rows", 0),), 1)
        gathered = lax.all_gather(input_rim, "ch", axis=2, tiled=True)
        masked_rim = gathered * mask_rim.astype(jnp.bfloat16)
        act_in = jax.nn.silu(masked_rim.astype(jnp.float32)).astype(jnp.bfloat16)
        pre_one = conv_rows(act_in, eff_one, taps) + bias_first
        act_one = (jax.nn.silu(pre_one) * mask_in).astype(jnp.bfloat16)
        hidden_rim = extended(act_one, (("rows", 0),), 1)
        hidden_all = lax.all_gather(hidden_rim, "ch", axis=2, tiled=True)
        skip_in = masked_rim[1:-1]
        total = conv_rows(hidden_all, eff_two, taps) + bias_second
        total = total + jnp.einsum(
            "rci,io->rco", skip_in, eff_skip, preferred_element_type=jnp.float32
        )
        pooled = jnp.mean(total.reshape(rows_dev // 2, 2, width // 2, 2, out_local), axis=(1, 3))
        outputs.append(pooled.astype(jnp.bfloat16))
        quarter = cotangent[micro] * 0.25
        grad_total = jnp.broadcast_to(
            quarter[:, None, :, None, :], (rows_dev // 2, 2, width // 2, 2, out_local)
        ).reshape(rows_dev, width, out_local)
        grad_rim = extended(grad_total, (("rows", 0),), 1)
        partial_hidden = conv_rows(grad_rim, back_two, taps)
        grad_act_one = lax.psum_scatter(partial_hidden, "ch", scatter_dimension=2, tiled=True)
        grad_pre_one = (grad_act_one * mask_in * silu_slope(pre_one)).astype(jnp.bfloat16)
        pre_rim = extended(grad_pre_one, (("rows", 0),), 1)
        partial_act = conv_rows(pre_rim, back_one, taps)
        partial_skip = jnp.einsum(
            "rco,io->rci", grad_total, eff_skip, preferred_element_type=jnp.float32
        )
        grad_act_in, grad_skip_in = (
            lax.psum_scatter(partial_act, "ch", scatter_dimension=2, tiled=True),
            lax.psum_scatter(partial_skip, "ch", scatter_dimension=2, tiled=True),
        )
        own_input = images[micro].astype(jnp.float32)
        in_grads.append(
            (mask_in * (silu_slope(own_input) * grad_act_in + grad_skip_in)).astype(jnp.bfloat16)
        )
        grad_one = kernel_taps(act_in, grad_pre_one, taps_low)
        grad_two = kernel_taps(hidden_all, grad_total, taps_low)
        grad_skip = jnp.einsum(
            "rci,rco->io", skip_in, grad_total, preferred_element_type=jnp.float32
        )
        grad_first = jnp.sum(grad_pre_one.astype(jnp.float32), axis=(0, 1))
        grad_second = jnp.sum(grad_total.astype(jnp.float32), axis=(0, 1))
        current = (grad_one, grad_two, grad_skip, grad_first, grad_second)
        if totals is None:
            totals = current
        else:
            totals = tuple((acc + new for acc, new in zip(totals, current)))
    summed = lax.psum((totals[0], totals[1], totals[2], totals[3], totals[4]), "rows")
    sum_one, sum_two, sum_skip, sum_first, sum_second = summed
    sum_skip = sum_skip.reshape(1, 1, -1, out_local)
    dot_one, dot_two, dot_skip = lax.psum(
        (jnp.sum(sum_one * kern_one), jnp.sum(sum_two * kern_two), jnp.sum(sum_skip * kern_skip)),
        "ch",
    )
    final_one = (
        sum_one / sigma_one - dot_one / (sigma_one * sigma_one) * left_one[..., None] * right_one
    )
    final_two = (
        sum_two / sigma_two - dot_two / (sigma_two * sigma_two) * left_two[..., None] * right_two
    )
    final_skip = (
        sum_skip / sigma_skip
        - dot_skip / (sigma_skip * sigma_skip) * left_skip[..., None] * right_skip
    )
    return (
        jnp.stack(outputs),
        jnp.stack(in_grads),
        final_one,
        final_two,
        final_skip[0, 0],
        sum_first,
        sum_second,
    )


def solution(mesh):
    in_specs = (
        P(None, "rows", None, "ch"),
        P(),
        P(),
        P(None, None, None, "ch"),
        P(None, None, None, "ch"),
        P(None, "ch"),
        P("ch"),
        P("ch"),
        P("ch"),
        P("ch"),
        P("ch"),
        P(None, "rows", None, "ch"),
    )
    out_specs = (
        P(None, "rows", None, "ch"),
        P(None, "rows", None, "ch"),
        P(None, None, None, "ch"),
        P(None, None, None, "ch"),
        P(None, "ch"),
        P("ch"),
        P("ch"),
    )
    return jax.shard_map(shards, mesh=mesh, in_specs=in_specs, out_specs=out_specs, check_vma=False)
```

profile of v0, /device:TPU:0, one launch (start us, length us, event | category | flops | bytes accessed | tf_op | source)
XLA Modules:
  0.0 752.3 jit_solution(6537862448741138620)
XLA Ops:
  11.0 5.0 collective-permute-start.17
  17.7 4.5 collective-permute-start.5
  24.5 8.7 %all-reduce.12 = (f32[3,3,96]{2,1,0:T(4,128)S(1)}, f32[3,3,192]{2,1,0:T(4,128)S(1)}) all-reduce(f32[3,3,96]{2,1,0:T(4,128)S(1)} %bitcast.1328, f32[3,3,192]{2,1,0:T(4,128)S(1)} %bitcast.1327), channel_id=1, replica_groups=mesh['rows'=16,'ch'=2] {'ch'}, use_global_device_ids=true, to_apply=%region_2.3 | all-reduce | flops 2592 | bytes 20736 | tf_op jit(solution)/shard_map/psum | solution.py:108
  37.9 5.6 all-reduce.11
  48.3 1.5 convolution_select_fusion.7
  50.2 1.5 convolution_select_fusion.4
  52.0 1.5 convolution_select_fusion.1
  72.7 4.4 collective-permute-start.9
  77.9 6.7 all_gather.26
  84.7 1.9 copy.688
  90.9 8.6 %all_gather.28 = bf16[18,64,96]{1,2,0:T(8,128)(2,1)} all-gather(bf16[18,64,48]{1,2,0:T(8,128)(2,1)S(1)} %pad_maximum_fusion.24), channel_id=1, replica_groups=mesh['rows'=16,'ch'=2] {'ch'}, dimensions={2}, use_global_device_ids=true | all-gather | bytes 331776 | tf_op jit(solution)/shard_map/all_gather | solution.py:151
  99.5 1.9 copy.723
  114.3 4.4 collective-permute-start.25
  121.2 4.5 collective-permute-start.13
  130.6 4.7 collective-permute-start.1
  138.7 3.2 fusion.21
  142.0 2.3 copy.935
  146.4 11.0 %all_gather.30 = bf16[18,64,96]{1,2,0:T(8,128)(2,1)S(1)} all-gather(bf16[18,64,48]{1,2,0:T(8,128)(2,1)S(1)} %pad_maximum_fusion.25), channel_id=1, replica_groups=mesh['rows'=16,'ch'=2] {'ch'}, dimensions={2}, use_global_device_ids=true | all-gather | bytes 331776 | tf_op jit(solution)/shard_map/all_gather | solution.py:151
  184.0 6.6 all_gather.24
  201.1 2.0 fusion.14
  213.4 4.8 convert_reduce_fusion.1
  245.7 2.8 convert_reduce_fusion.3
  259.3 58.4 %all-reduce.8 = (f32[96,96]{1,0:T(8,128)S(1)}, f32[96]{0:T(128)}, f32[96]{0:T(128)}) all-reduce(f32[96,96]{1,0:T(8,128)S(1)} %copy-done.235, f32[96]{0:T(128)S(1)} %add_add_fusion.1, f32[96]{0:T(128)S(1)} %copy-done.252), channel_id=1, replica_groups=mesh['rows'=16,'ch'=2] {'rows'}, use_global_device_ids=true, to_apply=%region_42.43 | all-reduce | flops 9408 | bytes 75264 | tf_op jit(solution)/shard_map/psum | solution.py:198
  319.6 4.4 collective-permute-start.15
  325.0 4.4 collective-permute-start.11
  341.0 4.4 collective-permute-start.7
  345.8 12.0 %all_gather.31 = bf16[18,64,192]{1,0,2:T(8,128)(2,1)S(1)} all-gather(bf16[18,64,96]{1,0,2:T(8,128)(2,1)S(1)} %copy.774), channel_id=1, replica_groups=mesh['rows'=16,'ch'=2] {'ch'}, dimensions={2}, use_global_device_ids=true | all-gather | bytes 663552 | tf_op jit(solution)/shard_map/all_gather | solution.py:157
  367.9 4.8 collective-permute-start.3
  373.8 11.9 %all_gather.29 = bf16[18,64,192]{1,0,2:T(8,128)(2,1)S(1)} all-gather(bf16[18,64,96]{1,0,2:T(8,128)(2,1)S(1)} %copy.739), channel_id=1, replica_groups=mesh['rows'=16,'ch'=2] {'ch'}, dimensions={2}, use_global_device_ids=true | all-gather | bytes 663552 | tf_op jit(solution)/shard_map/all_gather | solution.py:157
  395.7 5.1 collective-permute-start.31
  401.3 11.3 %all_gather.27 = bf16[18,64,192]{1,0,2:T(8,128)(2,1)S(1)} all-gather(bf16[18,64,96]{1,0,2:T(8,128)(2,1)S(1)} %copy.704), channel_id=1, replica_groups=mesh['rows'=16,'ch'=2] {'ch'}, dimensions={2}, use_global_device_ids=true | all-gather | bytes 663552 | tf_op jit(solution)/shard_map/all_gather | solution.py:157
  422.7 5.4 collective-permute-start.27
  428.5 11.0 %all_gather.25 = bf16[18,64,192]{1,0,2:T(8,128)(2,1)S(1)} all-gather(bf16[18,64,96]{1,0,2:T(8,128)(2,1)S(1)} %copy.669), channel_id=1, replica_groups=mesh['rows'=16,'ch'=2] {'ch'}, dimensions={2}, use_global_device_ids=true | all-gather | bytes 663552 | tf_op jit(solution)/shard_map/all_gather | solution.py:157
  440.6 1.9 convolution_bitcast_fusion.11
  442.5 2.0 convolution_bitcast_fusion.34
  444.5 2.0 convolution_bitcast_fusion.35
  446.5 2.0 convolution_bitcast_fusion.10
  448.4 2.0 convolution_bitcast_fusion.9
  450.4 2.0 convolution_bitcast_fusion.33
  452.4 5.7 collective-permute-start.23
  460.6 1.9 convolution_bitcast_fusion.32
  462.6 4.8 collective-permute-start.19
  469.7 2.0 convolution_bitcast_fusion.31
  474.0 2.0 convolution_bitcast_fusion.30
  481.0 3.7 fusion.179
  484.7 2.3 copy.821
  496.7 2.6 convolution_select_fusion.23
  507.0 1.5 convolution_select_fusion.21
  509.7 2.5 convolution_select_fusion.20
  522.0 2.5 convolution_select_fusion.17
  531.7 1.4 convolution_select_fusion.15
  536.1 46.8 %all-reduce.15.cloned.1.call-done = (f32[3,3,96,96]{3,2,1,0:T(8,128)}, f32[3,3,192,96]{3,2,1,0:T(8,128)}) async-done(((f32[3,3,96,96]{3,2,1,0:T(8,128)}, f32[3,3,192,96]{3,2,1,0:T(8,128)}), (f32[3,3,96,96]{3,2,1,0:T(8,128)}, f32[3,3,192,96]{3,2,1,0:T(8,128)})) %all-reduce.15.cloned.1.call-update) | async-done | bytes 995344 | tf_op jit(solution)/shard_map/psum | solution.py:198
  583.0 1.7 fusion.280
  584.7 2.0 fusion.36
  586.7 5.6 all-reduce.10
  614.0 2.9 convolution_add_fusion.3
  620.4 1.6 convolution_add_fusion.2
  630.7 11.1 %reduce-scatter.29.cloned.1.call-done = f32[16,64,48]{1,0,2:T(8,128)} async-done(((f32[16,64,96]{1,0,2:T(8,128)}), f32[16,64,48]{1,0,2:T(8,128)}) %reduce-scatter.29.cloned.1.call-update) | async-done | bytes 196624 | tf_op jit(solution)/shard_map/reduce_scatter | solution.py:179
  641.9 19.8 %reduce-scatter.33.cloned.1.call-done = f32[16,64,48]{1,0,2:T(8,128)} async-done(((f32[16,64,96]{1,0,2:T(8,128)}), f32[16,64,48]{1,0,2:T(8,128)}) %reduce-scatter.33.cloned.1.call-update) | async-done | bytes 196624 | tf_op jit(solution)/shard_map/reduce_scatter | solution.py:179
  661.7 20.1 %reduce-scatter.23.cloned.1.call-done = f32[16,64,48]{1,0,2:T(8,128)} async-done(((f32[16,64,96]{1,0,2:T(8,128)}), f32[16,64,48]{1,0,2:T(8,128)}) %reduce-scatter.23.cloned.1.call-update) | async-done | bytes 196624 | tf_op jit(solution)/shard_map/reduce_scatter | solution.py:180
  681.8 19.8 %reduce-scatter.27.cloned.1.call-done = f32[16,64,48]{1,0,2:T(8,128)} async-done(((f32[16,64,96]{1,0,2:T(8,128)}), f32[16,64,48]{1,0,2:T(8,128)}) %reduce-scatter.27.cloned.1.call-update) | async-done | bytes 196624 | tf_op jit(solution)/shard_map/reduce_scatter | solution.py:180
  701.7 19.6 %reduce-scatter.31.cloned.1.call-done = f32[16,64,48]{1,0,2:T(8,128)} async-done(((f32[16,64,96]{1,0,2:T(8,128)}), f32[16,64,48]{1,0,2:T(8,128)}) %reduce-scatter.31.cloned.1.call-update) | async-done | bytes 196624 | tf_op jit(solution)/shard_map/reduce_scatter | solution.py:180
  721.2 19.8 %reduce-scatter.35.cloned.1.call-done = f32[16,64,48]{1,0,2:T(8,128)} async-done(((f32[16,64,96]{1,0,2:T(8,128)}), f32[16,64,48]{1,0,2:T(8,128)}) %reduce-scatter.35.cloned.1.call-update) | async-done | bytes 196624 | tf_op jit(solution)/shard_map/reduce_scatter | solution.py:180
  741.1 3.1 fusion.698
  (1215 shorter events, 275.0 us)
Async XLA Ops:
  7.2 16.0 %copy-start = (f32[96]{0:T(128)S(1)}, f32[96]{0:T(128)}, u32[]{:S(2)}) copy-start(f32[96]{0:T(128)} %param.21) | copy-start | bytes 1156
  7.2 198.9 %reduce-scatter.39.cloned.1.call-start = ((), (), s32[]{:S(2)}) async-start(), calls=%async_computation.21 | async-start | bytes 1179648
  10.6 99.0 %collective-permute-start.16 = (bf16[1,64,96]{2,1,0:T(8,128)(2,1)}, bf16[1,64,96]{2,1,0:T(8,128)(2,1)}, u32[]{:S(2)}, u32[]{:S(2)}) collective-permute-start(bf16[1,64,96]{2,1,0:T(8,128)(2,1)} %get-tuple-element.135), channel_id=1, source_target_pairs={{0,2},{2,4},{4,6},{6,8},{8,10},{10,12},{12,14},{14,16},{16,18},{18... | collective-permute-start | bytes 36872 | tf_op jit(solution)/shard_map/ppermute | solution.py:21
  11.0 100.0 %collective-permute-start.17 = (bf16[1,64,96]{2,1,0:T(8,128)(2,1)}, bf16[1,64,96]{2,1,0:T(8,128)(2,1)}, u32[]{:S(2)}, u32[]{:S(2)}) collective-permute-start(bf16[1,64,96]{2,1,0:T(8,128)(2,1)} %get-tuple-element.136), channel_id=1, source_target_pairs={{2,0},{4,2},{6,4},{8,6},{10,8},{12,10},{14,12},{16,14},{18,16},{20... | collective-permute-start | bytes 36872 | tf_op jit(solution)/shard_map/ppermute | solution.py:23
  16.9 97.2 %collective-permute-start.20 = (bf16[1,64,96]{2,1,0:T(8,128)(2,1)}, bf16[1,64,96]{2,1,0:T(8,128)(2,1)}, u32[]{:S(2)}, u32[]{:S(2)}) collective-permute-start(bf16[1,64,96]{2,1,0:T(8,128)(2,1)} %get-tuple-element.131), channel_id=1, source_target_pairs={{0,2},{2,4},{4,6},{6,8},{8,10},{10,12},{12,14},{14,16},{16,18},{18... | collective-permute-start | bytes 36872 | tf_op jit(solution)/shard_map/ppermute | solution.py:21
  17.6 55.1 %collective-permute-start.4 = (bf16[1,64,48]{1,2,0:T(8,128)(2,1)}, bf16[1,64,48]{1,2,0:T(8,128)(2,1)}, u32[]{:S(2)}, u32[]{:S(2)}) collective-permute-start(bf16[1,64,48]{1,2,0:T(8,128)(2,1)} %get-tuple-element.63), channel_id=1, source_target_pairs={{0,2},{2,4},{4,6},{6,8},{8,10},{10,12},{12,14},{14,16},{16,18},{18... | collective-permute-start | bytes 18440 | tf_op jit(solution)/shard_map/ppermute | solution.py:21
  17.7 55.1 %collective-permute-start.5 = (bf16[1,64,48]{1,2,0:T(8,128)(2,1)}, bf16[1,64,48]{1,2,0:T(8,128)(2,1)}, u32[]{:S(2)}, u32[]{:S(2)}) collective-permute-start(bf16[1,64,48]{1,2,0:T(8,128)(2,1)} %get-tuple-element.62), channel_id=1, source_target_pairs={{2,0},{4,2},{6,4},{8,6},{10,8},{12,10},{14,12},{16,14},{18,16},{20... | collective-permute-start | bytes 18440 | tf_op jit(solution)/shard_map/ppermute | solution.py:23
  22.2 15.5 %copy-start.15 = (bf16[96,96]{1,0:T(8,128)(2,1)S(1)}, bf16[96,96]{1,0:T(8,128)(2,1)}, u32[]{:S(2)}) copy-start(bf16[96,96]{1,0:T(8,128)(2,1)} %param.17) | copy-start | bytes 55300
  22.2 15.5 %copy-start.261 = (f32[96]{0:T(128)S(1)}, f32[96]{0:T(128)}, u32[]{:S(2)}) copy-start(f32[96]{0:T(128)} %param.22) | copy-start | bytes 1156
  43.5 19.8 %copy-start.255 = (f32[1,1,96]{2,1,0:T(1,128)}, f32[1,1,96]{2,1,0:T(1,128)S(1)}, u32[]{:S(2)}) copy-start(f32[1,1,96]{2,1,0:T(1,128)S(1)} %get-tuple-element.40) | copy-start | bytes 1156
  72.7 16.9 %collective-permute-start.8 = (bf16[1,64,48]{1,2,0:T(8,128)(2,1)}, bf16[1,64,48]{1,2,0:T(8,128)(2,1)}, u32[]{:S(2)}, u32[]{:S(2)}) collective-permute-start(bf16[1,64,48]{1,2,0:T(8,128)(2,1)} %get-tuple-element.59), channel_id=1, source_target_pairs={{0,2},{2,4},{4,6},{6,8},{8,10},{10,12},{12,14},{14,16},{16,18},{18... | collective-permute-start | bytes 18440 | tf_op jit(solution)/shard_map/ppermute | solution.py:21
  72.7 16.9 %collective-permute-start.9 = (bf16[1,64,48]{1,2,0:T(8,128)(2,1)}, bf16[1,64,48]{1,2,0:T(8,128)(2,1)}, u32[]{:S(2)}, u32[]{:S(2)}) collective-permute-start(bf16[1,64,48]{1,2,0:T(8,128)(2,1)} %get-tuple-element.61), channel_id=1, source_target_pairs={{2,0},{4,2},{6,4},{8,6},{10,8},{12,10},{14,12},{16,14},{18,16},{20... | collective-permute-start | bytes 18440 | tf_op jit(solution)/shard_map/ppermute | solution.py:23
  89.6 29.1 %collective-permute-start.21 = (bf16[1,64,96]{2,1,0:T(8,128)(2,1)}, bf16[1,64,96]{2,1,0:T(8,128)(2,1)}, u32[]{:S(2)}, u32[]{:S(2)}) collective-permute-start(bf16[1,64,96]{2,1,0:T(8,128)(2,1)} %get-tuple-element.132), channel_id=1, source_target_pairs={{2,0},{4,2},{6,4},{8,6},{10,8},{12,10},{14,12},{16,14},{18,16},{20... | collective-permute-start | bytes 36872 | tf_op jit(solution)/shard_map/ppermute | solution.py:23
  89.6 31.6 %collective-permute-start.28 = (bf16[1,64,96]{2,1,0:T(8,128)(2,1)}, bf16[1,64,96]{2,1,0:T(8,128)(2,1)}, u32[]{:S(2)}, u32[]{:S(2)}) collective-permute-start(bf16[1,64,96]{2,1,0:T(8,128)(2,1)} %get-tuple-element.141), channel_id=1, source_target_pairs={{0,2},{2,4},{4,6},{6,8},{8,10},{10,12},{12,14},{14,16},{16,18},{18... | collective-permute-start | bytes 36872 | tf_op jit(solution)/shard_map/ppermute | solution.py:21
  109.6 16.1 %collective-permute-start.29 = (bf16[1,64,96]{2,1,0:T(8,128)(2,1)S(1)}, bf16[1,64,96]{2,1,0:T(8,128)(2,1)S(1)}, u32[]{:S(2)}, u32[]{:S(2)}) collective-permute-start(bf16[1,64,96]{2,1,0:T(8,128)(2,1)S(1)} %copy-done.248), channel_id=1, source_target_pairs={{2,0},{4,2},{6,4},{8,6},{10,8},{12,10},{14,12},{16,14},{18,16},{20... | collective-permute-start | bytes 36872 | tf_op jit(solution)/shard_map/ppermute | solution.py:23
  111.0 19.5 %collective-permute-start.24 = (bf16[1,64,96]{2,1,0:T(8,128)(2,1)S(1)}, bf16[1,64,96]{2,1,0:T(8,128)(2,1)S(1)}, u32[]{:S(2)}, u32[]{:S(2)}) collective-permute-start(bf16[1,64,96]{2,1,0:T(8,128)(2,1)S(1)} %copy-done.247), channel_id=1, source_target_pairs={{0,2},{2,4},{4,6},{6,8},{8,10},{10,12},{12,14},{14,16},{16,18},{18... | collective-permute-start | bytes 36872 | tf_op jit(solution)/shard_map/ppermute | solution.py:21
  114.3 21.0 %collective-permute-start.25 = (bf16[1,64,96]{2,1,0:T(8,128)(2,1)S(1)}, bf16[1,64,96]{2,1,0:T(8,128)(2,1)S(1)}, u32[]{:S(2)}, u32[]{:S(2)}) collective-permute-start(bf16[1,64,96]{2,1,0:T(8,128)(2,1)S(1)} %copy-done.246), channel_id=1, source_target_pairs={{2,0},{4,2},{6,4},{8,6},{10,8},{12,10},{14,12},{16,14},{18,16},{20... | collective-permute-start | bytes 36872 | tf_op jit(solution)/shard_map/ppermute | solution.py:23
  118.7 27.0 %collective-permute-start.12 = (bf16[1,64,48]{1,2,0:T(8,128)(2,1)}, bf16[1,64,48]{1,2,0:T(8,128)(2,1)}, u32[]{:S(2)}, u32[]{:S(2)}) collective-permute-start(bf16[1,64,48]{1,2,0:T(8,128)(2,1)} %get-tuple-element.60), channel_id=1, source_target_pairs={{0,2},{2,4},{4,6},{6,8},{8,10},{10,12},{12,14},{14,16},{16,18},{18... | collective-permute-start | bytes 18440 | tf_op jit(solution)/shard_map/ppermute | solution.py:21
  121.2 24.4 %collective-permute-start.13 = (bf16[1,64,48]{1,2,0:T(8,128)(2,1)}, bf16[1,64,48]{1,2,0:T(8,128)(2,1)}, u32[]{:S(2)}, u32[]{:S(2)}) collective-permute-start(bf16[1,64,48]{1,2,0:T(8,128)(2,1)} %get-tuple-element.66), channel_id=1, source_target_pairs={{2,0},{4,2},{6,4},{8,6},{10,8},{12,10},{14,12},{16,14},{18,16},{20... | collective-permute-start | bytes 18440 | tf_op jit(solution)/shard_map/ppermute | solution.py:23
  125.7 57.4 %collective-permute-start = (bf16[1,64,48]{1,2,0:T(8,128)(2,1)}, bf16[1,64,48]{1,2,0:T(8,128)(2,1)}, u32[]{:S(2)}, u32[]{:S(2)}) collective-permute-start(bf16[1,64,48]{1,2,0:T(8,128)(2,1)} %get-tuple-element.65), channel_id=1, source_target_pairs={{0,2},{2,4},{4,6},{6,8},{8,10},{10,12},{12,14},{14,16},{16,18},{18... | collective-permute-start | bytes 18440 | tf_op jit(solution)/shard_map/ppermute | solution.py:21
  130.6 52.6 %collective-permute-start.1 = (bf16[1,64,48]{1,2,0:T(8,128)(2,1)}, bf16[1,64,48]{1,2,0:T(8,128)(2,1)}, u32[]{:S(2)}, u32[]{:S(2)}) collective-permute-start(bf16[1,64,48]{1,2,0:T(8,128)(2,1)} %get-tuple-element.64), channel_id=1, source_target_pairs={{2,0},{4,2},{6,4},{8,6},{10,8},{12,10},{14,12},{16,14},{18,16},{20... | collective-permute-start | bytes 18440 | tf_op jit(solution)/shard_map/ppermute | solution.py:23
  145.6 12.1 %copy-start.193 = (bf16[18,64]{1,0:T(8,128)(2,1)S(1)}, bf16[18,64]{1,0:T(8,128)(2,1)}, u32[]{:S(2)}) copy-start(bf16[18,64]{1,0:T(8,128)(2,1)} %get-tuple-element.179) | copy-start | bytes 6916
  145.6 62.9 %reduce-scatter.41.cloned.1.call-start = ((), (), s32[]{:S(2)}) async-start(), calls=%async_computation.22 | async-start | bytes 1179648
  169.2 41.8 %reduce-scatter.43.cloned.1.call-start = ((), (), s32[]{:S(2)}) async-start(), calls=%async_computation.23 | async-start | bytes 1179648
  194.2 49.1 %reduce-scatter.37.cloned.1.call-start = ((), (), s32[]{:S(2)}) async-start(), calls=%async_computation.20 | async-start | bytes 1179648
  205.7 377.3 %all-reduce.15.cloned.1.call-start = ((), (), s32[]{:S(2)}) async-start(), calls=%async_computation.24 | async-start | bytes 2654208 | tf_op jit(solution)/shard_map/psum | solution.py:198
  218.2 113.0 %copy-start.18 = (bf16[16,64,96]{2,1,0:T(8,128)(2,1)}, bf16[16,64,96]{2,1,0:T(8,128)(2,1)S(1)}, u32[]{:S(2)}) copy-start(bf16[16,64,96]{2,1,0:T(8,128)(2,1)S(1)} %get-tuple-element.144) | copy-start | bytes 589828
  218.2 113.4 %copy-start.20 = (bf16[16,64,96]{2,1,0:T(8,128)(2,1)}, bf16[16,64,96]{2,1,0:T(8,128)(2,1)S(1)}, u32[]{:S(2)}) copy-start(bf16[16,64,96]{2,1,0:T(8,128)(2,1)S(1)} %get-tuple-element.50) | copy-start | bytes 589828
  218.2 115.0 %copy-start.22 = (bf16[16,64,96]{2,1,0:T(8,128)(2,1)}, bf16[16,64,96]{2,1,0:T(8,128)(2,1)S(1)}, u32[]{:S(2)}) copy-start(bf16[16,64,96]{2,1,0:T(8,128)(2,1)S(1)} %get-tuple-element.147) | copy-start | bytes 589828
  248.5 85.5 %copy-start.38 = (bf16[16,64,96]{2,1,0:T(8,128)(2,1)}, bf16[16,64,96]{2,1,0:T(8,128)(2,1)S(1)}, u32[]{:S(2)}) copy-start(bf16[16,64,96]{2,1,0:T(8,128)(2,1)S(1)} %get-tuple-element.47) | copy-start | bytes 589828
  254.0 63.6 %copy-start.16 = (bf16[96,96]{1,0:T(8,128)(2,1)S(1)}, bf16[96,96]{1,0:T(8,128)(2,1)}, u32[]{:S(2)}) copy-start(bf16[96,96]{1,0:T(8,128)(2,1)} %param.17) | copy-start | bytes 55300
  255.9 68.2 %copy-start.58 = (f32[16,64,96]{2,1,0:T(8,128)S(1)}, f32[16,64,96]{2,1,0:T(8,128)}, u32[]{:S(2)}) copy-start(f32[16,64,96]{2,1,0:T(8,128)} %get-tuple-element.51) | copy-start | bytes 1179652
  256.8 72.6 %copy-start.56 = (f32[16,64,96]{2,1,0:T(8,128)S(1)}, f32[16,64,96]{2,1,0:T(8,128)}, u32[]{:S(2)}) copy-start(f32[16,64,96]{2,1,0:T(8,128)} %get-tuple-element.145) | copy-start | bytes 1179652
  319.6 21.4 %collective-permute-start.14 = (bf16[1,64,96]{2,1,0:T(8,128)(2,1)S(1)}, bf16[1,64,96]{2,1,0:T(8,128)(2,1)S(1)}, u32[]{:S(2)}, u32[]{:S(2)}) collective-permute-start(bf16[1,64,96]{2,1,0:T(8,128)(2,1)S(1)} %get-tuple-element.137), channel_id=1, source_target_pairs={{0,2},{2,4},{4,6},{6,8},{8,10},{10,12},{12,14},{14,16},{16,18},{18... | collective-permute-start | bytes 36872 | tf_op jit(solution)/shard_map/ppermute | solution.py:21
  319.6 25.7 %collective-permute-start.15 = (bf16[1,64,96]{2,1,0:T(8,128)(2,1)S(1)}, bf16[1,64,96]{2,1,0:T(8,128)(2,1)S(1)}, u32[]{:S(2)}, u32[]{:S(2)}) collective-permute-start(bf16[1,64,96]{2,1,0:T(8,128)(2,1)S(1)} %get-tuple-element.138), channel_id=1, source_target_pairs={{2,0},{4,2},{6,4},{8,6},{10,8},{12,10},{14,12},{16,14},{18,16},{20... | collective-permute-start | bytes 36872 | tf_op jit(solution)/shard_map/ppermute | solution.py:23
  325.0 42.9 %collective-permute-start.10 = (bf16[1,64,96]{2,1,0:T(8,128)(2,1)}, bf16[1,64,96]{2,1,0:T(8,128)(2,1)S(1)}, u32[]{:S(2)}, u32[]{:S(2)}) collective-permute-start(bf16[1,64,96]{2,1,0:T(8,128)(2,1)} %get-tuple-element.119), channel_id=1, source_target_pairs={{0,2},{2,4},{4,6},{6,8},{8,10},{10,12},{12,14},{14,16},{16,18},{18... | collective-permute-start | bytes 36872 | tf_op jit(solution)/shard_map/ppermute | solution.py:21
  325.0 47.7 %collective-permute-start.11 = (bf16[1,64,96]{2,1,0:T(8,128)(2,1)}, bf16[1,64,96]{2,1,0:T(8,128)(2,1)}, u32[]{:S(2)}, u32[]{:S(2)}) collective-permute-start(bf16[1,64,96]{2,1,0:T(8,128)(2,1)} %get-tuple-element.120), channel_id=1, source_target_pairs={{2,0},{4,2},{6,4},{8,6},{10,8},{12,10},{14,12},{16,14},{18,16},{20... | collective-permute-start | bytes 36872 | tf_op jit(solution)/shard_map/ppermute | solution.py:23
  330.3 65.4 %collective-permute-start.6 = (bf16[1,64,96]{2,1,0:T(8,128)(2,1)}, bf16[1,64,96]{2,1,0:T(8,128)(2,1)S(1)}, u32[]{:S(2)}, u32[]{:S(2)}) collective-permute-start(bf16[1,64,96]{2,1,0:T(8,128)(2,1)} %get-tuple-element.121), channel_id=1, source_target_pairs={{0,2},{2,4},{4,6},{6,8},{8,10},{10,12},{12,14},{14,16},{16,18},{18... | collective-permute-start | bytes 36872 | tf_op jit(solution)/shard_map/ppermute | solution.py:21
  341.0 59.9 %collective-permute-start.7 = (bf16[1,64,96]{2,1,0:T(8,128)(2,1)}, bf16[1,64,96]{2,1,0:T(8,128)(2,1)S(1)}, u32[]{:S(2)}, u32[]{:S(2)}) collective-permute-start(bf16[1,64,96]{2,1,0:T(8,128)(2,1)} %get-tuple-element.122), channel_id=1, source_target_pairs={{2,0},{4,2},{6,4},{8,6},{10,8},{12,10},{14,12},{16,14},{18,16},{20... | collective-permute-start | bytes 36872 | tf_op jit(solution)/shard_map/ppermute | solution.py:23
  345.4 77.3 %collective-permute-start.2 = (bf16[1,64,96]{2,1,0:T(8,128)(2,1)}, bf16[1,64,96]{2,1,0:T(8,128)(2,1)S(1)}, u32[]{:S(2)}, u32[]{:S(2)}) collective-permute-start(bf16[1,64,96]{2,1,0:T(8,128)(2,1)} %get-tuple-element.123), channel_id=1, source_target_pairs={{0,2},{2,4},{4,6},{6,8},{8,10},{10,12},{12,14},{14,16},{16,18},{18... | collective-permute-start | bytes 36872 | tf_op jit(solution)/shard_map/ppermute | solution.py:21
  367.9 60.2 %collective-permute-start.3 = (bf16[1,64,96]{2,1,0:T(8,128)(2,1)S(1)}, bf16[1,64,96]{2,1,0:T(8,128)(2,1)S(1)}, u32[]{:S(2)}, u32[]{:S(2)}) collective-permute-start(bf16[1,64,96]{2,1,0:T(8,128)(2,1)S(1)} %copy-done.250), channel_id=1, source_target_pairs={{2,0},{4,2},{6,4},{8,6},{10,8},{12,10},{14,12},{16,14},{18,16},{20... | collective-permute-start | bytes 36872 | tf_op jit(solution)/shard_map/ppermute | solution.py:23
  372.7 79.7 %collective-permute-start.30 = (bf16[1,64,96]{2,1,0:T(8,128)(2,1)}, bf16[1,64,96]{2,1,0:T(8,128)(2,1)}, u32[]{:S(2)}, u32[]{:S(2)}) collective-permute-start(bf16[1,64,96]{2,1,0:T(8,128)(2,1)} %get-tuple-element.109), channel_id=1, source_target_pairs={{0,2},{2,4},{4,6},{6,8},{8,10},{10,12},{12,14},{14,16},{16,18},{18... | collective-permute-start | bytes 36872 | tf_op jit(solution)/shard_map/ppermute | solution.py:21
  395.7 62.4 %collective-permute-start.31 = (bf16[1,64,96]{2,1,0:T(8,128)(2,1)}, bf16[1,64,96]{2,1,0:T(8,128)(2,1)}, u32[]{:S(2)}, u32[]{:S(2)}) collective-permute-start(bf16[1,64,96]{2,1,0:T(8,128)(2,1)} %get-tuple-element.110), channel_id=1, source_target_pairs={{2,0},{4,2},{6,4},{8,6},{10,8},{12,10},{14,12},{16,14},{18,16},{20... | collective-permute-start | bytes 36872 | tf_op jit(solution)/shard_map/ppermute | solution.py:23
  400.8 61.7 %collective-permute-start.26 = (bf16[1,64,96]{2,1,0:T(8,128)(2,1)}, bf16[1,64,96]{2,1,0:T(8,128)(2,1)}, u32[]{:S(2)}, u32[]{:S(2)}) collective-permute-start(bf16[1,64,96]{2,1,0:T(8,128)(2,1)} %get-tuple-element.105), channel_id=1, source_target_pairs={{0,2},{2,4},{4,6},{6,8},{8,10},{10,12},{12,14},{14,16},{16,18},{18... | collective-permute-start | bytes 36872 | tf_op jit(solution)/shard_map/ppermute | solution.py:21
  422.7 44.7 %collective-permute-start.27 = (bf16[1,64,96]{2,1,0:T(8,128)(2,1)}, bf16[1,64,96]{2,1,0:T(8,128)(2,1)}, u32[]{:S(2)}, u32[]{:S(2)}) collective-permute-start(bf16[1,64,96]{2,1,0:T(8,128)(2,1)} %get-tuple-element.106), channel_id=1, source_target_pairs={{2,0},{4,2},{6,4},{8,6},{10,8},{12,10},{14,12},{16,14},{18,16},{20... | collective-permute-start | bytes 36872 | tf_op jit(solution)/shard_map/ppermute | solution.py:23
  428.1 43.5 %collective-permute-start.22 = (bf16[1,64,96]{2,1,0:T(8,128)(2,1)}, bf16[1,64,96]{2,1,0:T(8,128)(2,1)}, u32[]{:S(2)}, u32[]{:S(2)}) collective-permute-start(bf16[1,64,96]{2,1,0:T(8,128)(2,1)} %get-tuple-element.101), channel_id=1, source_target_pairs={{0,2},{2,4},{4,6},{6,8},{8,10},{10,12},{12,14},{14,16},{16,18},{18... | collective-permute-start | bytes 36872 | tf_op jit(solution)/shard_map/ppermute | solution.py:21
  452.4 19.3 %collective-permute-start.23 = (bf16[1,64,96]{2,1,0:T(8,128)(2,1)S(1)}, bf16[1,64,96]{2,1,0:T(8,128)(2,1)S(1)}, u32[]{:S(2)}, u32[]{:S(2)}) collective-permute-start(bf16[1,64,96]{2,1,0:T(8,128)(2,1)S(1)} %copy-done.249), channel_id=1, source_target_pairs={{2,0},{4,2},{6,4},{8,6},{10,8},{12,10},{14,12},{16,14},{18,16},{20... | collective-permute-start | bytes 36872 | tf_op jit(solution)/shard_map/ppermute | solution.py:23
  458.2 18.8 %collective-permute-start.18 = (bf16[1,64,96]{2,1,0:T(8,128)(2,1)S(1)}, bf16[1,64,96]{2,1,0:T(8,128)(2,1)S(1)}, u32[]{:S(2)}, u32[]{:S(2)}) collective-permute-start(bf16[1,64,96]{2,1,0:T(8,128)(2,1)S(1)} %copy-done.245), channel_id=1, source_target_pairs={{0,2},{2,4},{4,6},{6,8},{8,10},{10,12},{12,14},{14,16},{16,18},{18... | collective-permute-start | bytes 36872 | tf_op jit(solution)/shard_map/ppermute | solution.py:21
  462.6 14.4 %collective-permute-start.19 = (bf16[1,64,96]{2,1,0:T(8,128)(2,1)S(1)}, bf16[1,64,96]{2,1,0:T(8,128)(2,1)S(1)}, u32[]{:S(2)}, u32[]{:S(2)}) collective-permute-start(bf16[1,64,96]{2,1,0:T(8,128)(2,1)S(1)} %copy-done.244), channel_id=1, source_target_pairs={{2,0},{4,2},{6,4},{8,6},{10,8},{12,10},{14,12},{16,14},{18,16},{20... | collective-permute-start | bytes 36872 | tf_op jit(solution)/shard_map/ppermute | solution.py:23
  492.6 138.1 %reduce-scatter.21.cloned.1.call-start = ((), (), s32[]{:S(2)}) async-start(), calls=%async_computation.12 | async-start | bytes 1179648 | tf_op jit(solution)/shard_map/reduce_scatter | solution.py:179
  496.5 134.2 %reduce-scatter.25.cloned.1.call-start = ((), (), s32[]{:S(2)}) async-start(), calls=%async_computation.14 | async-start | bytes 1179648 | tf_op jit(solution)/shard_map/reduce_scatter | solution.py:179
  509.7 132.2 %reduce-scatter.29.cloned.1.call-start = ((), (), s32[]{:S(2)}) async-start(), calls=%async_computation.16 | async-start | bytes 1179648 | tf_op jit(solution)/shard_map/reduce_scatter | solution.py:179
  521.7 140.0 %reduce-scatter.33.cloned.1.call-start = ((), (), s32[]{:S(2)}) async-start(), calls=%async_computation.18 | async-start | bytes 1179648 | tf_op jit(solution)/shard_map/reduce_scatter | solution.py:179
  534.6 48.3 %copy-start.76 = (bf16[3,3,96,96]{3,2,1,0:T(8,128)(2,1)S(1)}, bf16[3,3,96,96]{3,2,1,0:T(8,128)(2,1)}, u32[]{:S(2)}) copy-start(bf16[3,3,96,96]{3,2,1,0:T(8,128)(2,1)} %param.15) | copy-start | bytes 497668
  534.6 50.1 %copy-start.7 = (bf16[3,3,192,96]{3,2,1,0:T(8,128)(2,1)S(1)}, bf16[3,3,192,96]{3,2,1,0:T(8,128)(2,1)}, u32[]{:S(2)}) copy-start(bf16[3,3,192,96]{3,2,1,0:T(8,128)(2,1)} %param.16) | copy-start | bytes 995332
  534.7 147.2 %reduce-scatter.23.cloned.1.call-start = ((), (), s32[]{:S(2)}) async-start(), calls=%async_computation.13 | async-start | bytes 1179648 | tf_op jit(solution)/shard_map/reduce_scatter | solution.py:180
  536.1 57.5 %copy-start.17 = (bf16[96,96]{1,0:T(8,128)(2,1)S(1)}, bf16[96,96]{1,0:T(8,128)(2,1)}, u32[]{:S(2)}) copy-start(bf16[96,96]{1,0:T(8,128)(2,1)} %param.17) | copy-start | bytes 55300
  596.3 105.3 %reduce-scatter.27.cloned.1.call-start = ((), (), s32[]{:S(2)}) async-start(), calls=%async_computation.15 | async-start | bytes 1179648 | tf_op jit(solution)/shard_map/reduce_scatter | solution.py:180
  613.7 107.5 %reduce-scatter.31.cloned.1.call-start = ((), (), s32[]{:S(2)}) async-start(), calls=%async_computation.17 | async-start | bytes 1179648 | tf_op jit(solution)/shard_map/reduce_scatter | solution.py:180
  620.0 121.1 %reduce-scatter.35.cloned.1.call-start = ((), (), s32[]{:S(2)}) async-start(), calls=%async_computation.19 | async-start | bytes 1179648 | tf_op jit(solution)/shard_map/reduce_scatter | solution.py:180
  628.6 112.5 %copy-start.13 = (bf16[4,16,64,48]{2,3,1,0:T(8,128)(2,1)S(1)}, bf16[4,16,64,48]{2,3,1,0:T(8,128)(2,1)}, u32[]{:S(2)}) copy-start(bf16[4,16,64,48]{2,3,1,0:T(8,128)(2,1)} %param.12) | copy-start | bytes 1179652
  628.6 112.5 %copy-start.143 = (f32[16,64]{1,0:T(8,128)S(1)}, f32[16,64]{1,0:T(8,128)}, u32[]{:S(2)}) copy-start(f32[16,64]{1,0:T(8,128)} %slice.1030) | copy-start | bytes 12292
  628.6 112.5 %copy-start.145 = (f32[16,64]{1,0:T(8,128)S(1)}, f32[16,64]{1,0:T(8,128)}, u32[]{:S(2)}) copy-start(f32[16,64]{1,0:T(8,128)} %slice.1051) | copy-start | bytes 12292
  628.6 112.5 %copy-start.147 = (f32[16,64]{1,0:T(8,128)S(1)}, f32[16,64]{1,0:T(8,128)}, u32[]{:S(2)}) copy-start(f32[16,64]{1,0:T(8,128)} %slice.985) | copy-start | bytes 12292
  (266 other events, 575.2 us)
Sparse Core Ops, SparseCore 0:
  145.7 15.9 reduce-scatter.38
  169.3 15.5 reduce-scatter.40
  194.3 13.4 reduce-scatter.42
  210.0 17.4 reduce-scatter.36
  492.7 90.1 all-reduce.14
  585.1 17.2 reduce-scatter.20
  604.7 17.4 reduce-scatter.24
  624.4 17.4 reduce-scatter.28
  644.2 17.4 reduce-scatter.32
  664.4 17.4 reduce-scatter.22
  684.2 17.4 reduce-scatter.26
  703.8 17.4 reduce-scatter.30
  723.5 17.4 reduce-scatter.34
where the time goes:
time: 763 us; the launch traced here: 752 us
  blocking collectives  157 us (21%)
  waiting for transfers between devices  157 us (21%)
  local copies, waits for them, and re-layouts  146 us (19%)
  matrix products  136 us (18%)
  starting transfers between devices  71 us (9%)
  other arithmetic  56.5 us (7%)
  between operations  27.2 us (4%)
    reduce_scatter x4, waiting for transfers between devices, shards(): lax.psum_scatter(partial_skip, 'ch', scatter_dimension=2, tiled=True)  79.3 us
    dot_general x72, matrix products, kernel_taps(): jnp.einsum('rci,rco->io', window, kept_grad, preferred_element_type=jnp.f...  78 us
    ppermute x16, starting transfers between devices, extended(): lax.ppermute(head, axis, [((i + 1) % count, i) for i in range(count)])  68 us
    psum x1, blocking collectives, shards(): lax.psum((totals[0], totals[1], totals[2], totals[3], totals[4]), 'rows')  58.4 us
    unnamed x634, local copies, waits for them, and re-layouts  57 us
    psum x1, waiting for transfers between devices, shards(): lax.psum((totals[0], totals[1], totals[2], totals[3], totals[4]), 'rows')  46.8 us
    all_gather x4, blocking collectives, shards(): hidden_all = lax.all_gather(hidden_rim, 'ch', axis=2, tiled=True)  46.2 us
    conv_general_dilated x180, local copies, waits for them, and re-layouts, conv_rows(): lax.conv_general_dilated(rim[None, row_tap:row_tap + slab_rows], kernel[r...  43.3 us
  transfers between devices with their start and end apart: 45, of which 7 were waited for; matrix products, arithmetic and copies ran while one was open for 37% of the time, Pallas kernels for 0%

commit v1 on v0

--- a/solution.py
+++ b/solution.py
@@ -1,6 +1,10 @@
+import functools
+
 import jax
 import jax.numpy as jnp
 from jax import lax
+from jax.experimental import pallas as pl
+from jax.experimental.pallas import tpu as pltpu
 from jax.sharding import PartitionSpec as P
 
 IMG = 64
@@ -223,6 +227,770 @@
     )
 
 
+F32 = jnp.float32
+BF16 = jnp.bfloat16
+MESH = pl.DeviceIdType.MESH
+TILE = 128
+NT = (((1,), (1,)), ((), ()))
+TN = (((0,), (0,)), ((), ()))
+NN = (((1,), (0,)), ((), ()))
+
+
+def fits(n_rows, n_ch, arrays):
+    images, kernel_one = arrays[0], arrays[3]
+    micros, rows_dev, width, in_local = images.shape
+    out_local = kernel_one.shape[3]
+    return (
+        n_ch == 2
+        and micros % 2 == 0
+        and n_rows % 2 == 0
+        and n_rows >= 4
+        and rows_dev % 8 == 0
+        and SHIFT % rows_dev == rows_dev // 2
+        and IMG % rows_dev == 0
+        and 2 * width == TILE
+        and in_local % 16 == 0
+        and 2 * in_local < TILE
+        and out_local % 32 == 0
+        and TILE < 2 * out_local <= 2 * TILE
+    )
+
+
+def dot(left, right, dims=NN):
+    return lax.dot_general(left, right, dims, preferred_element_type=F32)
+
+
+def iota(shape, dim):
+    return lax.broadcasted_iota(jnp.int32, shape, dim)
+
+
+def pieces(row):
+    first = row.astype(BF16).astype(F32)
+    rest = row - first
+    second = rest.astype(BF16).astype(F32)
+    third = rest - second
+    at = iota((16, row.shape[1]), 0)
+    zero = jnp.zeros((16, row.shape[1]), F32)
+    stacked = jnp.where(at == 0, first, jnp.where(at == 1, second, jnp.where(at == 2, third, zero)))
+    return stacked.astype(BF16)
+
+
+def total(value):
+    return jnp.sum(jnp.sum(value, axis=0, keepdims=True), axis=1, keepdims=True)
+
+
+def power(vector_row, kernel):
+    left = jnp.sum(dot(pieces(vector_row), kernel, NT), axis=0, keepdims=True)
+    left = left * lax.rsqrt(total(left * left) + EPS)
+    image = jnp.sum(dot(pieces(left), kernel), axis=0, keepdims=True)
+    square = total(image * image)
+    scale = lax.rsqrt(square + EPS)
+    return left, image * scale, square * scale
+
+
+def slope(value):
+    gate = 1.0 / (1.0 + jnp.exp(-value))
+    return gate + value * gate * (1.0 - gate)
+
+
+def fused_kernel(names, n_rows, dims, *refs):
+    micros, rows, width, ci, co, lanes_two, lanes_one = dims
+    ref = dict(zip(names, refs))
+    half = width // 2
+    per = micros // 2
+    pairs = rows // 2
+    cut = rows // 2
+    seg_slots = cut + 3
+    seg_out = cut + 1
+    pairs_a = cut // 2 + 1
+    n_chips = n_rows // 2
+    cin, cout = 2 * ci, 2 * co
+    op = 2 * TILE
+    total_rows = rows * n_rows
+
+    img, cot = ref["img"], ref["cot"]
+    ssem, rsem = ref["ssem"], ref["rsem"]
+    me = lax.axis_index("rows")
+    c = lax.axis_index("ch")
+    o = 1 - c
+    core = lax.rem(me, 2)
+    mate = me + 1 - 2 * core
+    chip = me // 2
+    up = lax.rem(me + n_rows - 1, n_rows)
+    down = lax.rem(me + 1, n_rows)
+    my_id = c * n_chips + chip
+    far = []
+    for delta in range(1, 2 * n_chips):
+        other = lax.rem(my_id + delta, 2 * n_chips)
+        far.append((2 * lax.rem(other, n_chips) + core, other // n_chips))
+    near = [(me, o), (mate, c), (up, c), (up, o), (down, c), (down, o)]
+
+    barrier = pltpu.get_barrier_semaphore()
+    for device in near + far:
+        pl.semaphore_signal(barrier, inc=1, device_id=device, device_id_type=MESH)
+
+    count = [0]
+
+    def remote(src, dst, device):
+        at = count[0]
+        count[0] += 1
+        return pltpu.make_async_remote_copy(
+            src_ref=src,
+            dst_ref=dst,
+            send_sem=ssem.at[at],
+            recv_sem=rsem.at[at],
+            device_id=device,
+            device_id_type=MESH,
+        )
+
+    imgr, sendp = ref["imgr"], ref["sendp"]
+
+    def pack(p, carry):
+        for j in range(per):
+            for mine in (True, False):
+                m = (c if mine else o) * per + j
+                pair = jnp.concatenate([img[m, 2 * p], img[m, 2 * p + 1]], axis=1)
+                if mine:
+                    imgr[j, c, p + 1] = pair
+                else:
+                    sendp[j, p] = pair
+        return carry
+
+    lax.fori_loop(0, pairs, pack, 0)
+    vec = ref["vec"]
+    vec[c] = jnp.zeros(vec.shape[1:], F32)
+    for i, name in enumerate(("q1", "q2", "q0", "b1", "b2")):
+        vec[c, i : i + 1, 0:co] = ref[name][...].astype(F32)
+
+    pl.semaphore_wait(barrier, len(near) + len(far))
+
+    k1h, k2h, k0h, cotr = ref["k1h"], ref["k2h"], ref["k0h"], ref["cotr"]
+    k1, k2, k0 = ref["k1"], ref["k2"], ref["k0"]
+    n1, n2 = k1.shape[0] // 2, k2.shape[0] // 2
+    part1, part2 = pl.ds(core * n1, n1), pl.ds(core * n2, n2)
+    sends = []
+
+    def begin(*args):
+        copy = remote(*args)
+        copy.start()
+        sends.append(copy)
+        return copy
+
+    k1_x = begin(k1.at[part1], k1h.at[part1], (me, o))
+    vec_x = begin(vec.at[c], vec.at[c], (me, o))
+    img_x = [begin(sendp.at[j], imgr.at[j, c, pl.ds(1, pairs)], (me, o)) for j in range(per)]
+    mine_c, mine_o = pl.ds(c * per, per), pl.ds(o * per, per)
+    img_halo = [
+        begin(imgr.at[:, c, 1], imgr.at[:, c, pairs + 1], (up, c)),
+        begin(sendp.at[:, 0], imgr.at[:, c, pairs + 1], (up, o)),
+        begin(imgr.at[:, c, pairs], imgr.at[:, c, 0], (down, c)),
+        begin(sendp.at[:, pairs - 1], imgr.at[:, c, 0], (down, o)),
+    ]
+    cot_x = begin(cot.at[mine_o], cotr.at[:, c, pl.ds(1, pairs)], (me, o))
+    cot_halo = [
+        begin(cot.at[mine_c, 0], cotr.at[:, c, pairs + 1], (up, c)),
+        begin(cot.at[mine_o, 0], cotr.at[:, c, pairs + 1], (up, o)),
+        begin(cot.at[mine_c, pairs - 1], cotr.at[:, c, 0], (down, c)),
+        begin(cot.at[mine_o, pairs - 1], cotr.at[:, c, 0], (down, o)),
+    ]
+    k2_x = begin(k2.at[part2], k2h.at[part2], (me, o))
+    k0_x = begin(k0, k0h, (me, o))
+
+    perm_in, perm_x = ref["perm_in"], ref["perm_x"]
+    shape = (8 * half, TILE)
+    at, lane = iota(shape, 0), iota(shape, 1)
+    column = 2 * lax.rem(at, half) + lax.rem(at // half, 4) - 1
+    hit = (lane - at // (4 * half) * width == column) & (column >= 0) & (column < width)
+    perm_in[...] = jnp.where(hit, 1.0, 0.0).astype(BF16)
+    shape = (4 * half, TILE)
+    at, lane = iota(shape, 0), iota(shape, 1)
+    source = at // (2 * half) * width + 2 * lax.rem(at, half) + lax.rem(at // half, 2)
+    perm_x[0 : 4 * half] = jnp.where(lane == source, 1.0, 0.0).astype(BF16)
+    shape = (half, TILE)
+    at, lane = iota(shape, 0), iota(shape, 1)
+    perm_x[4 * half : 5 * half] = jnp.where(lax.rem(lane, width) // 2 == at, 1.0, 0.0).astype(BF16)
+
+    def rem_pos(value, by):
+        return lax.rem(lax.rem(value, by) + by, by)
+
+    first_a = rem_pos(me * rows - SHIFT, total_rows)
+    first_b = rem_pos(me * rows + cut - SHIFT, total_rows)
+    base = [lax.rem(first_a, IMG), lax.rem(first_b, IMG) - cut]
+    image_a, image_b = first_a // IMG, first_b // IMG
+    keep = jnp.where(base[1] < 0, 0.0, 1.0).astype(F32)
+    vh, vw = ref["vh"], ref["vw"]
+    high = [[vh[c * per + j, image] for image in (image_a, image_b)] for j in range(per)]
+    wide = [[vw[c * per + j, image] for image in (image_a, image_b)] for j in range(per)]
+
+    w1, w2, w0 = ref["w1"], ref["w2"], ref["w0"]
+
+    def place(dst, row, own_part, other_part, padded):
+        size = own_part.shape[0]
+        first = jnp.where(c == 0, own_part, other_part)
+        second = jnp.where(c == 0, other_part, own_part)
+        line = jnp.concatenate([first, second, jnp.zeros((size, op - cout), BF16)], axis=1)
+        dst[pl.ds(row, size), :] = line
+        if padded > size:
+            dst[pl.ds(row + size, padded - size), :] = jnp.zeros((padded - size, op), BF16)
+
+    vec_x.wait_recv()
+
+    def row_of(i):
+        return jnp.concatenate(
+            [vec[0, i : i + 1, 0:co], vec[1, i : i + 1, 0:co], jnp.zeros((1, op - cout), F32)], axis=1
+        )
+
+    k1_x.wait_recv()
+    k1_m = begin(k1h.at[part1], k1h.at[part1], (mate, c))
+    k1_m.wait_recv()
+    for tap in range(9):
+        rows_at = slice(tap * cin, (tap + 1) * cin)
+        place(w1, tap * TILE, k1[rows_at], k1h[rows_at], TILE)
+    left1, right1, sigma1 = power(row_of(0), w1[...])
+    scale1 = 1.0 / sigma1
+    bias1 = row_of(3)
+    bias2 = row_of(4)
+    left1_ref = ref["left1"]
+    left1_ref[0:1] = left1
+
+    for copy in img_x + img_halo:
+        copy.wait_recv()
+    b_in, xp, xb = ref["b_in"], ref["xp"], ref["xb"]
+    ones = jnp.where(iota((TILE - cin, TILE), 0) == 0, 1.0, 0.0).astype(F32)
+
+    def prepare(p, carry):
+        seg = (p >= pairs_a).astype(jnp.int32)
+        lane = iota((1, TILE), 1)
+        row = 2 * p - 2 + lane // width
+        column = lax.rem(lane, width)
+        acts, plain = [], []
+        for j in range(per):
+            first = jnp.where(seg == 0, base[0], base[1])
+            tall = jnp.where(seg == 0, high[j][0], high[j][1])
+            broad = jnp.where(seg == 0, wide[j][0], wide[j][1])
+            mask = jnp.where((first + row < tall) & (column < broad), 1.0, 0.0)
+            x = jnp.concatenate([imgr[j, 0, p], imgr[j, 1, p]], axis=0).astype(F32) * mask
+            act = x / (1.0 + jnp.exp(-x))
+            acts += [act.astype(BF16), ones.astype(BF16)]
+            plain += [x.astype(BF16), ones.astype(BF16)]
+        spread = dot(perm_in[...], jnp.concatenate(acts, axis=0), NT).astype(BF16)
+        slot = 2 * p + 2 * seg
+        for j in range(per):
+            for a in range(2):
+                for t in range(4):
+                    b_in[j, slot + a, :, t * TILE : (t + 1) * TILE] = spread[
+                        (4 * a + t) * half : (4 * a + t + 1) * half, j * TILE : (j + 1) * TILE
+                    ]
+        spread = dot(perm_x[...], jnp.concatenate(plain, axis=0), NT).astype(BF16)
+        for j in range(per):
+            part = spread[:, j * TILE : (j + 1) * TILE]
+            xp[j, p] = part[0 : 4 * half]
+            xb[j, p] = part[4 * half : 5 * half]
+        return carry
+
+    lax.fori_loop(0, pairs + 2, prepare, 0)
+    for j in range(per):
+        b_in[j, seg_slots - 1] = (b_in[j, seg_slots + 1].astype(F32) * keep).astype(BF16)
+        b_in[j, seg_slots] = (b_in[j, seg_slots - 2].astype(F32) * keep).astype(BF16)
+
+    raw1, grad1 = ref["raw1"], ref["grad1"]
+
+    def conv_one(step, carry):
+        j, seg = step // 2, lax.rem(step, 2)
+        parts = []
+        for b in range(2):
+            taps = [
+                b_in[j, pl.ds(seg * seg_slots + u, seg_out), :, b * TILE : (b + 3) * TILE].reshape(
+                    seg_out * half, 3 * TILE
+                )
+                for u in range(3)
+            ]
+            parts.append(jnp.concatenate(taps, axis=1))
+        result = dot(jnp.concatenate(parts, axis=0), w1[...])
+        for b in range(2):
+            raw1[j, b, pl.ds(seg * seg_out, seg_out)] = result[
+                b * seg_out * half : (b + 1) * seg_out * half
+            ].reshape(seg_out, half, op)
+        return carry
+
+    lax.fori_loop(0, 2 * per, conv_one, 0)
+
+    cols = ref["cols"]
+    pixel = iota((half, op), 0)
+
+    def activate(step, carry):
+        j, i = step // (2 * seg_out), lax.rem(step, 2 * seg_out)
+        seg = (i >= seg_out).astype(jnp.int32)
+        first = jnp.where(seg == 0, base[0], base[1])
+        tall = jnp.where(seg == 0, jnp.where(j == 0, high[0][0], high[1][0]), jnp.where(j == 0, high[0][1], high[1][1]))
+        broad = jnp.where(seg == 0, jnp.where(j == 0, wide[0][0], wide[1][0]), jnp.where(j == 0, wide[0][1], wide[1][1]))
+        broad = jnp.where(first + i - 1 < tall, broad, 0)
+        acts = []
+        for b in range(2):
+            pre = raw1[j, b, i] * scale1 + bias1
+            gate = 1.0 / (1.0 + jnp.exp(-pre))
+            mask = 2 * pixel + b < broad
+            lift = pre * gate
+            grad1[j, b, i] = jnp.where(mask, gate + lift * (1.0 - gate), 0.0)
+            acts.append(jnp.where(mask, lift, 0.0).astype(BF16).astype(F32))
+        even, odd = acts
+        before = jnp.where(pixel == 0, 0.0, pltpu.roll(odd, 1, 0))
+        after = jnp.where(pixel == half - 1, 0.0, pltpu.roll(even, half - 1, 0))
+        cols[j, 0, i] = before + even
+        cols[j, 1, i] = even + odd
+        cols[j, 2, i] = odd + after
+        return carry
+
+    lax.fori_loop(0, 2 * per * seg_out, activate, 0)
+
+    box = ref["box"]
+
+    def boxes(step, carry):
+        j, i = step // pairs, lax.rem(step, pairs)
+        above = jnp.where(i == cut // 2, keep, 1.0)
+        below = jnp.where(i == cut // 2 - 1, keep, 1.0)
+        for w in range(3):
+            lines = [cols[j, w, 2 * i + k] for k in range(4)]
+            for u in range(3):
+                one, two = lines[u], lines[u + 1]
+                if u == 0:
+                    one = one * above
+                if u == 2:
+                    two = two * below
+                tap = 3 * u + w
+                box[j, i, :, tap * op : (tap + 1) * op] = (one + two).astype(BF16)
+        return carry
+
+    lax.fori_loop(0, per * pairs, boxes, 0)
+
+    cot_x.wait_recv()
+    for copy in cot_halo:
+        copy.wait_recv()
+    quart = ref["quart"]
+
+    def quarter(step, carry):
+        j, i = step // (pairs + 2), lax.rem(step, pairs + 2)
+        inner = jnp.minimum(jnp.maximum(i - 1, 0), pairs - 1)
+        own = jnp.where((i == 0) | (i == pairs + 1), cotr[j, c, i], cot[c * per + j, inner])
+        other = cotr[j, o, i]
+        first = jnp.where(c == 0, own, other)
+        second = jnp.where(c == 0, other, own)
+        line = jnp.concatenate([first, second, jnp.zeros((half, op - cout), BF16)], axis=1)
+        quart[j, i] = (line.astype(F32) * 0.25).astype(BF16)
+        return carry
+
+    lax.fori_loop(0, per * (pairs + 2), quarter, 0)
+    own_px = pairs * half
+
+    def owned(j):
+        return quart[j, 1 : pairs + 1].reshape(own_px, op)
+
+    wire2, wire1 = ref["wire2"], ref["wire1"]
+    acc2 = ref["acc2"]
+    acc0 = ref["acc0"]
+    for j in range(per):
+        given = owned(j)[:, 0:cout]
+        value = dot(given, box[j].reshape(own_px, 9 * op), TN)
+        skip = dot(given, xb[j, 1 : pairs + 1].reshape(own_px, TILE), TN)
+        acc2[...] = value if j == 0 else acc2[...] + value
+        acc0[...] = skip if j == 0 else acc0[...] + skip
+    spare = lanes_two - 9 * cout - cin
+    for ch in range(2):
+        rows_at = slice(ch * co, (ch + 1) * co)
+        parts = [acc2[rows_at, tap * op : tap * op + cout] for tap in range(9)]
+        parts += [acc0[rows_at, 0:cin], jnp.zeros((co, spare), F32)]
+        wire2[ch] = jnp.concatenate(parts, axis=1).astype(BF16)
+
+    half_rows = co // 2
+    kept_rows = pl.ds(core * half_rows, half_rows)
+    mate_rows = pl.ds((1 - core) * half_rows, half_rows)
+
+    def sum_mate(wire, got):
+        return begin(wire.at[:, mate_rows], got, (mate, c))
+
+    def sum_far(copy, wire, got, shares, landing, mine):
+        copy.wait_recv()
+        share = shares.shape[-1]
+        for ch in range(2):
+            value = wire[ch, kept_rows].astype(F32) + got[ch].astype(F32)
+            for chip_at in range(n_chips):
+                shares[ch, chip_at] = value[:, chip_at * share : (chip_at + 1) * share].astype(BF16)
+                @pl.when(my_id == ch * n_chips + chip_at)
+                def _():
+                    mine[...] = value[:, chip_at * share : (chip_at + 1) * share]
+        copies = []
+        for delta in range(1, 2 * n_chips):
+            other = lax.rem(my_id + delta, 2 * n_chips)
+            copies.append(
+                begin(shares.at[other // n_chips, lax.rem(other, n_chips)], landing.at[delta - 1], far[delta - 1])
+            )
+        return copies
+
+    def gather_far(copies, landing, mine, result):
+        value = mine[...]
+        for delta in range(1, 2 * n_chips):
+            copies[delta - 1].wait_recv()
+            value = value + landing[delta - 1].astype(F32)
+        share = value.shape[1]
+        result[chip, kept_rows] = value.astype(BF16)
+        back = []
+        for delta in range(1, n_chips):
+            other = lax.rem(chip + delta, n_chips)
+            back.append(
+                begin(result.at[chip, kept_rows], result.at[chip, kept_rows], (2 * other + core, c))
+            )
+        return back
+
+    def gather_mate(copies, result):
+        for copy in copies:
+            copy.wait_recv()
+        return begin(result.at[:, kept_rows], result.at[:, kept_rows], (mate, c))
+
+    sum2 = sum_mate(wire2, ref["got2"])
+
+    k2_x.wait_recv()
+    k2_m = begin(k2h.at[part2], k2h.at[part2], (mate, c))
+    k0_x.wait_recv()
+    place(w0, 0, k0[...], k0h[...], TILE)
+    k2_m.wait_recv()
+    for tap in range(9):
+        rows_at = slice(tap * cout, (tap + 1) * cout)
+        place(w2, tap * op, k2[rows_at], k2h[rows_at], op)
+    left2, right2, sigma2 = power(row_of(1), w2[...])
+    left0, right0, sigma0 = power(row_of(2), w0[...])
+    scale2, scale0 = 1.0 / sigma2, 1.0 / sigma0
+    left2_ref, left0_ref = ref["left2"], ref["left0"]
+    left2_ref[0:1] = left2
+    left0_ref[0:1] = left0
+
+    taps_sum = ref["taps_sum"]
+    spot = iota(((pairs + 2) * half, op), 0)
+    at_left = lax.rem(spot, half) == 0
+    at_right = lax.rem(spot, half) == half - 1
+    all_px = (pairs + 2) * half
+    g_pre = ref["g_pre"]
+    dot1 = jnp.zeros((half, op), F32)
+    for j in range(per):
+        given = quart[j].reshape(all_px, op)
+        for u in range(3):
+            t0, t1, t2 = [
+                dot(given, w2[(3 * u + w) * op : (3 * u + w + 1) * op], NT) for w in range(3)
+            ]
+            even = t0 + t1 + jnp.where(at_left, 0.0, pltpu.roll(t2, 1, 0))
+            odd = t1 + t2 + jnp.where(at_right, 0.0, pltpu.roll(t0, all_px - 1, 0))
+            taps_sum[u, 0] = even.reshape(pairs + 2, half, op)
+            taps_sum[u, 1] = odd.reshape(pairs + 2, half, op)
+
+        def back_rows(i, carry):
+            hold = jnp.where(i == cut // 2, keep, 1.0)
+            for b in range(2):
+                upper, lower = taps_sum[2, b, i], taps_sum[0, b, i + 1]
+                even = lower + taps_sum[1, b, i + 1] + hold * upper
+                odd = taps_sum[1, b, i] + upper + hold * lower
+                even = (even * scale2 * grad1[j, b, 2 * i + 1]).astype(BF16)
+                odd = (odd * scale2 * grad1[j, b, 2 * i]).astype(BF16)
+                g_pre[j, b, 2 * i + 1] = even
+                g_pre[j, b, 2 * i] = odd
+                own_even = jnp.where(i < pairs, 1.0, 0.0)
+                own_odd = jnp.where(i > 0, 1.0, 0.0)
+                carry = carry + own_even * even.astype(F32) * raw1[j, b, 2 * i + 1]
+                carry = carry + own_odd * odd.astype(F32) * raw1[j, b, 2 * i]
+            return carry
+
+        dot1 = lax.fori_loop(0, pairs + 1, back_rows, dot1)
+
+    out_b, send_b, got_b = ref["out_b"], ref["send_b"], ref["got_b"]
+    dot2 = jnp.zeros((1, op), F32)
+    dot0 = jnp.zeros((1, op), F32)
+    for j in range(per):
+        main = dot(box[j].reshape(own_px, 9 * op), w2[...])
+        skip = dot(xb[j, 1 : pairs + 1].reshape(own_px, TILE), w0[...])
+        given = owned(j).astype(F32)
+        dot2 = dot2 + jnp.sum(given * main, axis=0, keepdims=True)
+        dot0 = dot0 + jnp.sum(given * skip, axis=0, keepdims=True)
+        value = (main * scale2 + skip * scale0) * 0.25 + bias2
+        value = value.astype(BF16)
+        first, second = value[:, 0:co], value[:, co:cout]
+        out_b[c * per + j] = jnp.where(c == 0, first, second).reshape(pairs, half, co)
+        send_b[j] = jnp.where(c == 0, second, first).reshape(pairs, half, co)
+    out_x = begin(send_b, got_b, (me, o))
+
+    far2 = sum_far(sum2, wire2, ref["got2"], ref["shares2"], ref["landing2"], ref["mine2"])
+
+    acc1 = ref["acc1"]
+
+    def kernel_one_grad(step, carry):
+        j, seg = step // 2, lax.rem(step, 2)
+        value = None
+        for b in range(2):
+            given = g_pre[j, b, pl.ds(seg * cut + 1, cut)].reshape(cut * half, op)[:, 0:cout]
+            taps = [
+                b_in[j, pl.ds(seg * (cut + 2) + 1 + u, cut), :, b * TILE : (b + 3) * TILE].reshape(
+                    cut * half, 3 * TILE
+                )
+                for u in range(3)
+            ]
+            part = dot(given, jnp.concatenate(taps, axis=1), TN)
+            value = part if value is None else value + part
+        acc1[...] = acc1[...] + value
+        return carry
+
+    acc1[...] = jnp.zeros_like(acc1)
+    lax.fori_loop(0, 2 * per, kernel_one_grad, 0)
+    spare = lanes_one - 9 * cin - 10
+    dots = [total(dot1), total(dot2), total(dot0)]
+
+    def pair_of(column):
+        high_part = column.astype(BF16).astype(F32)
+        return [high_part, column - high_part]
+
+    for ch in range(2):
+        rows_at = slice(ch * co, (ch + 1) * co)
+        parts = [acc1[rows_at, tap * TILE : tap * TILE + cin] for tap in range(9)]
+        parts += pair_of(acc1[rows_at, 4 * TILE + cin : 4 * TILE + cin + 1])
+        parts += pair_of(acc0[rows_at, cin : cin + 1])
+        for value in dots:
+            parts += pair_of(jnp.broadcast_to(value, (co, 1)))
+        parts.append(jnp.zeros((co, spare), F32))
+        wire1[ch] = jnp.concatenate(parts, axis=1).astype(BF16)
+    sum1 = sum_mate(wire1, ref["got1"])
+
+    taps_in, skip_back = ref["taps_in"], ref["skip_back"]
+    pixel_in = iota((half, TILE), 0)
+    out_g, send_g, got_g = ref["out_g"], ref["send_g"], ref["got_g"]
+    far1 = None
+    back2 = None
+    for j in range(per):
+        skip_back[...] = (dot(owned(j), w0[...], NT) * scale0).reshape(pairs, half, TILE)
+
+        def tap_products(step, carry):
+            b, part = step // 2, lax.rem(step, 2)
+            given = g_pre[j, b, pl.ds(part * seg_out, seg_out)].reshape(seg_out * half, op)
+            taps_in[b, pl.ds(part * seg_out, seg_out)] = dot(given, w1[...], NT).reshape(
+                seg_out, half, 9 * TILE
+            )
+            return carry
+
+        lax.fori_loop(0, 4, tap_products, 0)
+
+        def input_rows(p, carry):
+            lines = []
+            for a in range(2):
+                r = 2 * p + a
+                hold_up = jnp.where(r == cut - 1, keep, 1.0)
+                hold_down = jnp.where(r == cut, keep, 1.0)
+
+                def column_sum(w, s):
+                    def of(u, row):
+                        at = (3 * u + w) * TILE
+                        return taps_in[s, row, :, at : at + TILE]
+
+                    return of(0, r + 2) * hold_up + of(1, r + 1) + of(2, r) * hold_down
+
+                before = pltpu.roll(column_sum(2, 1), 1, 0)
+                after = pltpu.roll(column_sum(0, 0), half - 1, 0)
+                even = column_sum(0, 1) + column_sum(1, 0) + jnp.where(pixel_in == 0, 0.0, before)
+                odd = column_sum(1, 1) + column_sum(2, 0) + jnp.where(pixel_in == half - 1, 0.0, after)
+                seg = (r >= cut).astype(jnp.int32)
+                first = jnp.where(seg == 0, base[0], base[1])
+                tall = jnp.where(seg == 0, high[j][0], high[j][1])
+                broad = jnp.where(seg == 0, wide[j][0], wide[j][1])
+                broad = jnp.where(first + r < tall, broad, 0)
+                for b, value in ((0, even), (1, odd)):
+                    at = (2 * a + b) * half
+                    x = xp[j, p + 1, at : at + half].astype(F32)
+                    mask = 2 * pixel_in + b < broad
+                    value = slope(x) * (value * scale1) + skip_back[p]
+                    lines.append(jnp.where(mask, value, 0.0).astype(BF16))
+            line = dot(jnp.concatenate(lines, axis=0), perm_x[0 : 4 * half], TN).astype(BF16)
+            own = jnp.where(c == 0, line[0:ci], line[ci:cin])
+            other = jnp.where(c == 0, line[ci:cin], line[0:ci])
+            out_g[c * per + j, 2 * p] = own[:, 0:width]
+            out_g[c * per + j, 2 * p + 1] = own[:, width:TILE]
+            send_g[j, p] = other
+            return carry
+
+        lax.fori_loop(0, pairs, input_rows, 0)
+        copy = begin(send_g.at[j], got_g.at[j], (me, o))
+        if j == 0:
+            grad_x = [copy]
+            far1 = sum_far(sum1, wire1, ref["got1"], ref["shares1"], ref["landing1"], ref["mine1"])
+            back2 = gather_far(far2, ref["landing2"], ref["mine2"], ref["result2"])
+        else:
+            grad_x.append(copy)
+
+    last2 = gather_mate(back2, ref["result2"])
+    back1 = gather_far(far1, ref["landing1"], ref["mine1"], ref["result1"])
+    out_x.wait_recv()
+    out_b[mine_o] = got_b[...].reshape(per, pairs, half, co)
+
+    def unpack(p, carry):
+        for j in range(per):
+            out_g[o * per + j, 2 * p] = got_g[j, p, :, 0:width]
+            out_g[o * per + j, 2 * p + 1] = got_g[j, p, :, width:TILE]
+        return carry
+
+    for copy in grad_x:
+        copy.wait_recv()
+    lax.fori_loop(0, pairs, unpack, 0)
+
+    last1 = gather_mate(back1, ref["result1"])
+
+    def own_half(row):
+        return jnp.where(c == 0, row[:, 0:co], row[:, co:cout])
+
+    def column_of(row):
+        row = jnp.concatenate([own_half(row), jnp.zeros((1, TILE - co), F32)], axis=1)
+        return jnp.transpose(jnp.broadcast_to(row, (TILE, TILE)))[0:co]
+
+    def compact(row, size, padded):
+        return jnp.concatenate([row[:, t * padded : t * padded + size] for t in range(9)], axis=1)
+
+    def lines_of(result):
+        share = result.shape[2]
+        return [result[chip_at, :, 0:share].astype(F32) for chip_at in range(n_chips)]
+
+    last1.wait_recv()
+    flat1 = jnp.concatenate(lines_of(ref["result1"]), axis=1)
+    extra = flat1[:, 9 * cin : 9 * cin + 10]
+    dot_values = [extra[0:1, 4 + 2 * i : 5 + 2 * i] + extra[0:1, 5 + 2 * i : 6 + 2 * i] for i in range(3)]
+    biases = jnp.concatenate([extra, jnp.zeros((co, TILE - 10), F32)], axis=1)
+    biases = jnp.transpose(jnp.concatenate([biases, jnp.zeros((TILE - co, TILE), F32)], axis=0))
+    ref["out_b1"][...] = biases[0:1, 0:co] + biases[1:2, 0:co]
+    ref["out_b2"][...] = biases[2:3, 0:co] + biases[3:4, 0:co]
+
+    def finish(flat, left, right, scale, value, out):
+        columns = column_of(right) * (value * scale * scale)
+        size = flat.shape[1]
+        for at in range(0, size, TILE):
+            some = min(TILE, size - at)
+            part = flat[:, at : at + some] * scale - columns[:, 0:some] * left[:, at : at + some]
+            if some < TILE:
+                part = jnp.concatenate([part, jnp.zeros((co, TILE - some), F32)], axis=1)
+            part = jnp.concatenate([part, jnp.zeros((TILE - co, TILE), F32)], axis=0)
+            out[at : at + some] = jnp.transpose(part)[0:some, 0:co]
+
+    finish(flat1[:, 0 : 9 * cin], compact(left1_ref[0:1], cin, TILE), right1, scale1, dot_values[0], ref["out_k1"])
+    last2.wait_recv()
+    flat2 = jnp.concatenate(lines_of(ref["result2"]), axis=1)
+    finish(flat2[:, 0 : 9 * cout], compact(left2_ref[0:1], cout, op), right2, scale2, dot_values[1], ref["out_k2"])
+    finish(flat2[:, 9 * cout : 9 * cout + cin], left0_ref[0:1, 0:cin], right0, scale0, dot_values[2], ref["out_k0"])
+
+    for copy in sends:
+        copy.wait_send()
+
+
+def fused(n_rows, arrays):
+    (images, valid_h, valid_w, kernel_one, kernel_two, kernel_skip, bias_one, bias_two,
+     vector_one, vector_two, vector_skip, cotangent) = arrays
+    micros, rows, width, ci = images.shape
+    co = kernel_one.shape[3]
+    per, pairs, half = micros // 2, rows // 2, width // 2
+    op = 2 * TILE
+    n_chips = n_rows // 2
+    cin, cout = 2 * ci, 2 * co
+    step = TILE * n_chips
+    lanes_two = -(-(9 * cout + cin) // step) * step
+    lanes_one = -(-(9 * cin + 10) // step) * step
+    seg_out = rows // 2 + 1
+    inputs = {
+        "vh": valid_h,
+        "vw": valid_w,
+        "img": jnp.transpose(images, (0, 1, 3, 2)),
+        "k1": kernel_one.reshape(9 * cin, co),
+        "k2": kernel_two.reshape(9 * cout, co),
+        "k0": kernel_skip,
+        "b1": bias_one.reshape(1, co),
+        "b2": bias_two.reshape(1, co),
+        "q1": vector_one.reshape(1, co),
+        "q2": vector_two.reshape(1, co),
+        "q0": vector_skip.reshape(1, co),
+        "cot": cotangent,
+    }
+    outputs = {
+        "out_b": jax.ShapeDtypeStruct(cotangent.shape, BF16),
+        "out_g": jax.ShapeDtypeStruct((micros, rows, ci, width), BF16),
+        "out_k1": jax.ShapeDtypeStruct((9 * cin, co), F32),
+        "out_k2": jax.ShapeDtypeStruct((9 * cout, co), F32),
+        "out_k0": jax.ShapeDtypeStruct((cin, co), F32),
+        "out_b1": jax.ShapeDtypeStruct((1, co), F32),
+        "out_b2": jax.ShapeDtypeStruct((1, co), F32),
+    }
+    vm = pltpu.VMEM
+    scratch = {
+        "imgr": vm((per, 2, pairs + 2, ci, TILE), BF16),
+        "sendp": vm((per, pairs, ci, TILE), BF16),
+        "vec": vm((2, 8, TILE), F32),
+        "k1h": vm((9 * cin, co), BF16),
+        "k2h": vm((9 * cout, co), BF16),
+        "k0h": vm((cin, co), BF16),
+        "cotr": vm((per, 2, pairs + 2, half, co), BF16),
+        "perm_in": vm((8 * half, TILE), BF16),
+        "perm_x": vm((5 * half, TILE), BF16),
+        "w1": vm((9 * TILE, op), BF16),
+        "w2": vm((9 * op, op), BF16),
+        "w0": vm((TILE, op), BF16),
+        "left1": vm((8, 9 * TILE), F32),
+        "left2": vm((8, 9 * op), F32),
+        "left0": vm((8, TILE), F32),
+        "b_in": vm((per, 2 * (rows // 2 + 3), half, 4 * TILE), BF16),
+        "xp": vm((per, pairs + 2, 4 * half, TILE), BF16),
+        "xb": vm((per, pairs + 2, half, TILE), BF16),
+        "raw1": vm((per, 2, 2 * seg_out, half, op), F32),
+        "grad1": vm((per, 2, 2 * seg_out, half, op), F32),
+        "cols": vm((per, 3, 2 * seg_out, half, op), F32),
+        "box": vm((per, pairs, half, 9 * op), BF16),
+        "quart": vm((per, pairs + 2, half, op), BF16),
+        "acc2": vm((cout, 9 * op), F32),
+        "acc0": vm((cout, TILE), F32),
+        "acc1": vm((cout, 9 * TILE), F32),
+        "taps_sum": vm((3, 2, pairs + 2, half, op), F32),
+        "g_pre": vm((per, 2, 2 * seg_out, half, op), BF16),
+        "taps_in": vm((2, 2 * seg_out, half, 9 * TILE), F32),
+        "skip_back": vm((pairs, half, TILE), F32),
+        "send_b": vm((per, pairs, half, co), BF16),
+        "got_b": vm((per, pairs, half, co), BF16),
+        "send_g": vm((per, pairs, ci, TILE), BF16),
+        "got_g": vm((per, pairs, ci, TILE), BF16),
+    }
+    for name, lanes in (("1", lanes_one), ("2", lanes_two)):
+        share = lanes // n_chips
+        scratch["wire" + name] = vm((2, co, lanes), BF16)
+        scratch["got" + name] = vm((2, co // 2, lanes), BF16)
+        scratch["shares" + name] = vm((2, n_chips, co // 2, share), BF16)
+        scratch["landing" + name] = vm((2 * n_chips - 1, co // 2, share), BF16)
+        scratch["mine" + name] = vm((co // 2, share), F32)
+        scratch["result" + name] = vm((n_chips, co, share), BF16)
+    copies = 18 + per * 2 + 2 * (1 + 2 * n_chips - 1 + n_chips - 1 + 1)
+    scratch["ssem"] = pltpu.SemaphoreType.DMA((copies,))
+    scratch["rsem"] = pltpu.SemaphoreType.DMA((copies,))
+    names = list(inputs) + list(outputs) + list(scratch)
+    dims = (micros, rows, width, ci, co, lanes_two, lanes_one)
+    smem = pl.BlockSpec(memory_space=pltpu.SMEM)
+    vmem = pl.BlockSpec(memory_space=pltpu.VMEM)
+    results = pl.pallas_call(
+        functools.partial(fused_kernel, names, n_rows, dims),
+        out_shape=list(outputs.values()),
+        in_specs=[smem, smem] + [vmem] * (len(inputs) - 2),
+        out_specs=[vmem] * len(outputs),
+        scratch_shapes=list(scratch.values()),
+        compiler_params=pltpu.CompilerParams(
+            collective_id=0, has_side_effects=True, vmem_limit_bytes=60 * 1024 * 1024
+        ),
+        name="down_block",
+    )(*inputs.values())
+    out_b, out_g, out_k1, out_k2, out_k0, out_b1, out_b2 = results
+    return (
+        out_b,
+        jnp.transpose(out_g, (0, 1, 3, 2)),
+        out_k1.reshape(3, 3, cin, co),
+        out_k2.reshape(3, 3, cout, co),
+        out_k0,
+        out_b1.reshape(co),
+        out_b2.reshape(co),
+    )
+
+
 def solution(mesh):
     in_specs = (
         P(None, "rows", None, "ch"),
@@ -247,4 +1015,10 @@
         P("ch"),
         P("ch"),
     )
-    return jax.shard_map(shards, mesh=mesh, in_specs=in_specs, out_specs=out_specs, check_vma=False)
+
+    def step(*arrays):
+        if fits(mesh.shape["rows"], mesh.shape["ch"], arrays):
+            return fused(mesh.shape["rows"], arrays)
+        return shards(*arrays)
+
+    return jax.shard_map(step, mesh=mesh, in_specs=in_specs, out_specs=out_specs, check_vma=False)

time: 763 us -> 70.7 us (0.09); the launches traced: 752 us -> 69.6 us
  blocking collectives: 157 us -> 0 us
  waiting for transfers between devices: 157 us -> 0 us
  local copies, waits for them, and re-layouts: 146 us -> 7.28 us
  matrix products: 136 us -> 0 us
  starting transfers between devices: 71 us -> 0 us
  Pallas kernels: 0 us -> 61.7 us
  other arithmetic: 56.5 us -> 0 us
  between operations: 27.2 us -> 0.65 us
    reduce_scatter x8 -> x0, waiting for transfers between devices: 110 us -> none  [the longest x4 79.3 us: shards(): lax.psum_scatter(partial_skip, 'ch', scatter_dimension=2, tiled=True)]
    dot_general x90 -> x0, matrix products: 94.3 us -> none  [the longest x72 78 us: kernel_taps(): jnp.einsum('rci,rco->io', window, kept_grad, preferred_element_type=jnp.f...]
    all_gather x8 -> x0, blocking collectives: 79.1 us -> none  [the longest x4 46.2 us: shards(): hidden_all = lax.all_gather(hidden_rim, 'ch', axis=2, tiled=True)]
    psum x4 -> x0, blocking collectives: 78.3 us -> none  [the longest x1 58.4 us: shards(): lax.psum((totals[0], totals[1], totals[2], totals[3], totals[4]), 'rows')]
    ppermute x32 -> x0, starting transfers between devices: 69.2 us -> none  [the longest x16 68 us: extended(): lax.ppermute(head, axis, [((i + 1) % count, i) for i in range(count)])]
    pallas_call x0 -> x1, Pallas kernels: none -> 61.7 us  [fused(): pl.pallas_call(functools.partial(fused_kernel, names, n_rows, dims), out_...]
    unnamed x634 -> x17, local copies, waits for them, and re-layouts: 57 us -> 7.28 us
    psum x1 -> x0, waiting for transfers between devices: 46.8 us -> none  [shards(): lax.psum((totals[0], totals[1], totals[2], totals[3], totals[4]), 'rows')]
  transfers between devices with their start and end apart: 45 -> 0, of which waited for: 7 -> 0; matrix products, arithmetic and copies ran while one was open for 37% -> 0% of each run, Pallas kernels for 0% -> 0%
where the time goes in v1:
time: 70.7 us; the launch traced here: 69.6 us
  Pallas kernels  61.7 us (87%)
  local copies, waits for them, and re-layouts  7.28 us (10%)
    pallas_call x1, Pallas kernels, fused(): pl.pallas_call(functools.partial(fused_kernel, names, n_rows, dims), out_...  61.7 us
    unnamed x17, local copies, waits for them, and re-layouts  7.28 us

profile of v1, /device:TPU:0, one launch (start us, length us, event | category | flops | bytes accessed | tf_op | source)
XLA Modules:
  0.0 69.6 jit_solution(7726084214728347931)
XLA Ops:
  0.6 61.7 %down_block.1 = (bf16[4,8,32,96]{3,2,1,0:T(8,128)(2,1)}, bf16[4,16,48,64]{3,2,1,0:T(8,128)(2,1)}, f32[864,96]{1,0:T(8,128)}, f32[1728,96]{1,0:T(8,128)}, f32[96,...) custom-call(s32[4,4]{1,0:T(4,128)} %refs_0_.1, s32[4,4]{1,0:T(4,128)} %refs_1_.1, bf16[4,16,48,64]{3,2,1,0:T(8,128)(2,1)} %bitcast.14, ...), custom_call_target="tpu_custom_call" | custom-call | tf_op jit(solution)/shard_map/down_block/pallas_call | solution.py:971
  62.3 1.7 %copy.26 = bf16[4,8,32,96]{3,2,1,0:T(8,128)(2,1)} copy(bf16[4,8,32,96]{3,2,1,0:T(8,128)(2,1)} %get-tuple-element.28) | data formatting | bytes 393216
  64.0 0.0 copy-start.1
  64.0 0.0 copy-start
  64.0 2.2 %copy.27 = bf16[4,16,64,48]{2,3,1,0:T(8,128)(2,1)} copy(bf16[4,16,64,48]{2,3,1,0:T(8,128)(2,1)} %bitcast.15) | data formatting | bytes 786432
  66.2 0.0 copy-done.1
  66.2 0.8 %copy.28 = f32[3,3,96,96]{3,2,1,0:T(8,128)} copy(f32[3,3,96,96]{3,2,1,0:T(8,128)S(1)} %bitcast.17) | data formatting | bytes 663552
  66.9 0.0 copy-done
  66.9 0.0 copy-start.2
  67.0 0.9 %copy.29 = f32[3,3,192,96]{3,2,1,0:T(8,128)} copy(f32[3,3,192,96]{3,2,1,0:T(8,128)S(1)} %bitcast.13) | data formatting | bytes 1327104
  67.9 0.0 copy-done.2
  67.9 0.0 copy-start.4
  67.9 0.6 copy.30
  68.5 0.0 copy-done.4
  68.5 0.0 copy-start.3
  68.5 0.5 copy.31
  69.0 0.1 copy-done.3
  69.1 0.5 copy.32
Async XLA Ops:
  64.0 2.2 %copy-start.1 = (f32[864,96]{1,0:T(8,128)S(1)}, f32[864,96]{1,0:T(8,128)}, u32[]{:S(2)}) copy-start(f32[864,96]{1,0:T(8,128)} %get-tuple-element.16) | copy-start | bytes 995332
  64.0 2.9 %copy-start = (f32[1728,96]{1,0:T(8,128)S(1)}, f32[1728,96]{1,0:T(8,128)}, u32[]{:S(2)}) copy-start(f32[1728,96]{1,0:T(8,128)} %get-tuple-element.17) | copy-start | bytes 1990660
  66.9 0.9 %copy-start.2 = (f32[96,96]{1,0:T(8,128)S(1)}, f32[96,96]{1,0:T(8,128)}, u32[]{:S(2)}) copy-start(f32[96,96]{1,0:T(8,128)} %get-tuple-element.32) | copy-start | bytes 110596
  67.9 0.6 copy-start.4
  68.5 0.6 copy-start.3

commit v2 on v1

--- a/solution.py
+++ b/solution.py
@@ -294,7 +294,7 @@
 
 
 def fused_kernel(names, n_rows, dims, *refs):
-    micros, rows, width, ci, co, lanes_two, lanes_one = dims
+    micros, rows, width, ci, co, lanes_two, lanes_one, bits, share1, share2 = dims
     ref = dict(zip(names, refs))
     half = width // 2
     per = micros // 2
@@ -307,9 +307,10 @@
     cin, cout = 2 * ci, 2 * co
     op = 2 * TILE
     total_rows = rows * n_rows
-
-    img, cot = ref["img"], ref["cot"]
-    ssem, rsem = ref["ssem"], ref["rsem"]
+    own_px = pairs * half
+    all_px = (pairs + 2) * half
+
+    ssem, rsem, lsem = ref["ssem"], ref["rsem"], ref["lsem"]
     me = lax.axis_index("rows")
     c = lax.axis_index("ch")
     o = 1 - c
@@ -330,6 +331,7 @@
         pl.semaphore_signal(barrier, inc=1, device_id=device, device_id_type=MESH)
 
     count = [0]
+    sends = []
 
     def remote(src, dst, device):
         at = count[0]
@@ -343,58 +345,27 @@
             device_id_type=MESH,
         )
 
-    imgr, sendp = ref["imgr"], ref["sendp"]
-
-    def pack(p, carry):
-        for j in range(per):
-            for mine in (True, False):
-                m = (c if mine else o) * per + j
-                pair = jnp.concatenate([img[m, 2 * p], img[m, 2 * p + 1]], axis=1)
-                if mine:
-                    imgr[j, c, p + 1] = pair
-                else:
-                    sendp[j, p] = pair
-        return carry
-
-    lax.fori_loop(0, pairs, pack, 0)
-    vec = ref["vec"]
-    vec[c] = jnp.zeros(vec.shape[1:], F32)
-    for i, name in enumerate(("q1", "q2", "q0", "b1", "b2")):
-        vec[c, i : i + 1, 0:co] = ref[name][...].astype(F32)
-
-    pl.semaphore_wait(barrier, len(near) + len(far))
-
-    k1h, k2h, k0h, cotr = ref["k1h"], ref["k2h"], ref["k0h"], ref["cotr"]
-    k1, k2, k0 = ref["k1"], ref["k2"], ref["k0"]
-    n1, n2 = k1.shape[0] // 2, k2.shape[0] // 2
-    part1, part2 = pl.ds(core * n1, n1), pl.ds(core * n2, n2)
-    sends = []
-
     def begin(*args):
         copy = remote(*args)
         copy.start()
         sends.append(copy)
         return copy
 
-    k1_x = begin(k1.at[part1], k1h.at[part1], (me, o))
-    vec_x = begin(vec.at[c], vec.at[c], (me, o))
-    img_x = [begin(sendp.at[j], imgr.at[j, c, pl.ds(1, pairs)], (me, o)) for j in range(per)]
-    mine_c, mine_o = pl.ds(c * per, per), pl.ds(o * per, per)
-    img_halo = [
-        begin(imgr.at[:, c, 1], imgr.at[:, c, pairs + 1], (up, c)),
-        begin(sendp.at[:, 0], imgr.at[:, c, pairs + 1], (up, o)),
-        begin(imgr.at[:, c, pairs], imgr.at[:, c, 0], (down, c)),
-        begin(sendp.at[:, pairs - 1], imgr.at[:, c, 0], (down, o)),
-    ]
-    cot_x = begin(cot.at[mine_o], cotr.at[:, c, pl.ds(1, pairs)], (me, o))
-    cot_halo = [
-        begin(cot.at[mine_c, 0], cotr.at[:, c, pairs + 1], (up, c)),
-        begin(cot.at[mine_o, 0], cotr.at[:, c, pairs + 1], (up, o)),
-        begin(cot.at[mine_c, pairs - 1], cotr.at[:, c, 0], (down, c)),
-        begin(cot.at[mine_o, pairs - 1], cotr.at[:, c, 0], (down, o)),
-    ]
-    k2_x = begin(k2.at[part2], k2h.at[part2], (me, o))
-    k0_x = begin(k0, k0h, (me, o))
+    img, cot, k10, k2 = ref["img_v"], ref["cot_v"], ref["k10_v"], ref["k2_v"]
+    n1, n2 = 9 * cin, 9 * cout
+    loads = []
+    for i, (src, dst) in enumerate(
+        [
+            (ref["img"], img),
+            (ref["k1"], k10.at[0:n1]),
+            (ref["k0"], k10.at[n1 : n1 + cin]),
+            (ref["k2"], k2.at[0:n2]),
+            (ref["cot"], cot),
+        ]
+    ):
+        load = pltpu.make_async_copy(src, dst, lsem.at[i])
+        load.start()
+        loads.append(load)
 
     perm_in, perm_x = ref["perm_in"], ref["perm_x"]
     shape = (8 * half, TILE)
@@ -422,6 +393,86 @@
     high = [[vh[c * per + j, image] for image in (image_a, image_b)] for j in range(per)]
     wide = [[vw[c * per + j, image] for image in (image_a, image_b)] for j in range(per)]
 
+    def choose(seg, two):
+        return jnp.where(seg == 0, two[0], two[1])
+
+    vec = ref["vec"]
+    vec[c] = jnp.zeros(vec.shape[1:], F32)
+    for i, name in enumerate(("q1", "q2", "q0", "b1", "b2")):
+        vec[c, i : i + 1, 0:co] = ref[name][...].astype(F32)
+
+    imgr, sendp = ref["imgr"], ref["sendp"]
+    loads[0].wait()
+    for j in range(per):
+        for mine in (False, True):
+
+            def pack(p, carry, j=j, mine=mine):
+                m = (c if mine else o) * per + j
+                pair = jnp.concatenate([img[m, 2 * p], img[m, 2 * p + 1]], axis=1)
+                if mine:
+                    imgr[j, c, p + 1] = pair
+                else:
+                    sendp[j, p] = pair
+                return carry
+
+            lax.fori_loop(0, pairs, pack, 0, unroll=4)
+    for load in loads[1:]:
+        load.wait()
+
+    pl.semaphore_wait(barrier, len(near) + len(far))
+
+    k10h, k2h, cotr = ref["k10h"], ref["k2h"], ref["cotr"]
+    spots = [core] + [lax.rem(me // 2**b, 2) for b in range(1, bits)]
+    mates = [mate] + [me + 2**b * (1 - 2 * spots[b]) for b in range(1, bits)]
+
+    def piece(rows_each, level, depth):
+        first = 0
+        for b in range(depth - level):
+            first = first * 2 + spots[b]
+        return pl.ds(first * (2**level * rows_each), 2**level * rows_each)
+
+    class Shared:
+        def __init__(self, own, got, rows_each, depth):
+            self.got, self.rows_each, self.depth, self.level = got, rows_each, depth, 0
+            at = piece(rows_each, 0, depth)
+            self.copy = begin(own.at[at], got.at[at], (me, o))
+
+        def turn(self):
+            self.copy.wait_recv()
+            if self.level < self.depth:
+                at = piece(self.rows_each, self.level, self.depth)
+                device = (mates[self.depth - 1 - self.level], c)
+                self.copy = begin(self.got.at[at], self.got.at[at], device)
+            self.level += 1
+
+    mine_c, mine_o = pl.ds(c * per, per), pl.ds(o * per, per)
+    img_x, img_halo = [], []
+
+    def send_image(j):
+        img_x.append(begin(sendp.at[j], imgr.at[j, c, pl.ds(1, pairs)], (me, o)))
+        img_halo.append(
+            [
+                begin(sendp.at[j, 0], imgr.at[j, c, pairs + 1], (up, o)),
+                begin(sendp.at[j, pairs - 1], imgr.at[j, c, 0], (down, o)),
+                begin(imgr.at[j, c, 1], imgr.at[j, c, pairs + 1], (up, c)),
+                begin(imgr.at[j, c, pairs], imgr.at[j, c, 0], (down, c)),
+            ]
+        )
+
+    vec_x = begin(vec.at[c], vec.at[c], (me, o))
+    one = Shared(k10, k10h, share1, 2)
+    send_image(0)
+    two = Shared(k2, k2h, share2, bits)
+    for j in range(1, per):
+        send_image(j)
+    cot_x = begin(cot.at[mine_o], cotr.at[:, c, pl.ds(1, pairs)], (me, o))
+    cot_halo = [
+        begin(cot.at[mine_o, 0], cotr.at[:, c, pairs + 1], (up, o)),
+        begin(cot.at[mine_o, pairs - 1], cotr.at[:, c, 0], (down, o)),
+        begin(cot.at[mine_c, 0], cotr.at[:, c, pairs + 1], (up, c)),
+        begin(cot.at[mine_c, pairs - 1], cotr.at[:, c, 0], (down, c)),
+    ]
+
     w1, w2, w0 = ref["w1"], ref["w2"], ref["w0"]
 
     def place(dst, row, own_part, other_part, padded):
@@ -433,174 +484,141 @@
         if padded > size:
             dst[pl.ds(row + size, padded - size), :] = jnp.zeros((padded - size, op), BF16)
 
-    vec_x.wait_recv()
-
     def row_of(i):
         return jnp.concatenate(
             [vec[0, i : i + 1, 0:co], vec[1, i : i + 1, 0:co], jnp.zeros((1, op - cout), F32)], axis=1
         )
 
-    k1_x.wait_recv()
-    k1_m = begin(k1h.at[part1], k1h.at[part1], (mate, c))
-    k1_m.wait_recv()
-    for tap in range(9):
-        rows_at = slice(tap * cin, (tap + 1) * cin)
-        place(w1, tap * TILE, k1[rows_at], k1h[rows_at], TILE)
-    left1, right1, sigma1 = power(row_of(0), w1[...])
-    scale1 = 1.0 / sigma1
-    bias1 = row_of(3)
-    bias2 = row_of(4)
-    left1_ref = ref["left1"]
-    left1_ref[0:1] = left1
-
-    for copy in img_x + img_halo:
-        copy.wait_recv()
     b_in, xp, xb = ref["b_in"], ref["xp"], ref["xb"]
-    ones = jnp.where(iota((TILE - cin, TILE), 0) == 0, 1.0, 0.0).astype(F32)
-
-    def prepare(p, carry):
-        seg = (p >= pairs_a).astype(jnp.int32)
-        lane = iota((1, TILE), 1)
-        row = 2 * p - 2 + lane // width
-        column = lax.rem(lane, width)
-        acts, plain = [], []
-        for j in range(per):
-            first = jnp.where(seg == 0, base[0], base[1])
-            tall = jnp.where(seg == 0, high[j][0], high[j][1])
-            broad = jnp.where(seg == 0, wide[j][0], wide[j][1])
-            mask = jnp.where((first + row < tall) & (column < broad), 1.0, 0.0)
-            x = jnp.concatenate([imgr[j, 0, p], imgr[j, 1, p]], axis=0).astype(F32) * mask
-            act = x / (1.0 + jnp.exp(-x))
-            acts += [act.astype(BF16), ones.astype(BF16)]
-            plain += [x.astype(BF16), ones.astype(BF16)]
-        spread = dot(perm_in[...], jnp.concatenate(acts, axis=0), NT).astype(BF16)
-        slot = 2 * p + 2 * seg
-        for j in range(per):
-            for a in range(2):
-                for t in range(4):
-                    b_in[j, slot + a, :, t * TILE : (t + 1) * TILE] = spread[
-                        (4 * a + t) * half : (4 * a + t + 1) * half, j * TILE : (j + 1) * TILE
-                    ]
-        spread = dot(perm_x[...], jnp.concatenate(plain, axis=0), NT).astype(BF16)
-        for j in range(per):
-            part = spread[:, j * TILE : (j + 1) * TILE]
-            xp[j, p] = part[0 : 4 * half]
-            xb[j, p] = part[4 * half : 5 * half]
-        return carry
-
-    lax.fori_loop(0, pairs + 2, prepare, 0)
-    for j in range(per):
+    ones = jnp.where(iota((TILE - cin, TILE), 0) == 0, 1.0, 0.0).astype(BF16)
+
+    def prepare(j):
+        img_x[j].wait_recv()
+        for copy in img_halo[j]:
+            copy.wait_recv()
+
+        def two_pairs(step, carry):
+            lane = iota((1, TILE), 1)
+            column = lax.rem(lane, width)
+            acts, plain, slots = [], [], []
+            for k in range(2):
+                p = 2 * step + k
+                seg = (p >= pairs_a).astype(jnp.int32)
+                row = 2 * p - 2 + lane // width
+                mask = jnp.where(
+                    (choose(seg, base) + row < choose(seg, high[j])) & (column < choose(seg, wide[j])), 1.0, 0.0
+                )
+                x = jnp.concatenate([imgr[j, 0, p], imgr[j, 1, p]], axis=0).astype(F32) * mask
+                act = x / (1.0 + jnp.exp(-x))
+                acts += [act.astype(BF16), ones]
+                plain += [x.astype(BF16), ones]
+                slots.append(2 * p + 2 * seg)
+            spread = dot(perm_in[...], jnp.concatenate(acts, axis=0), NT).astype(BF16)
+            for k in range(2):
+                for a in range(2):
+                    for t in range(4):
+                        b_in[j, slots[k] + a, :, t * TILE : (t + 1) * TILE] = spread[
+                            (4 * a + t) * half : (4 * a + t + 1) * half, k * TILE : (k + 1) * TILE
+                        ]
+            spread = dot(perm_x[...], jnp.concatenate(plain, axis=0), NT).astype(BF16)
+            for k in range(2):
+                part = spread[:, k * TILE : (k + 1) * TILE]
+                xp[j, 2 * step + k] = part[0 : 4 * half]
+                xb[j, 2 * step + k] = part[4 * half : 5 * half]
+            return carry
+
+        lax.fori_loop(0, (pairs + 2) // 2, two_pairs, 0, unroll=True)
         b_in[j, seg_slots - 1] = (b_in[j, seg_slots + 1].astype(F32) * keep).astype(BF16)
         b_in[j, seg_slots] = (b_in[j, seg_slots - 2].astype(F32) * keep).astype(BF16)
 
     raw1, grad1 = ref["raw1"], ref["grad1"]
 
-    def conv_one(step, carry):
-        j, seg = step // 2, lax.rem(step, 2)
-        parts = []
-        for b in range(2):
-            taps = [
-                b_in[j, pl.ds(seg * seg_slots + u, seg_out), :, b * TILE : (b + 3) * TILE].reshape(
-                    seg_out * half, 3 * TILE
-                )
-                for u in range(3)
-            ]
-            parts.append(jnp.concatenate(taps, axis=1))
-        result = dot(jnp.concatenate(parts, axis=0), w1[...])
-        for b in range(2):
-            raw1[j, b, pl.ds(seg * seg_out, seg_out)] = result[
-                b * seg_out * half : (b + 1) * seg_out * half
-            ].reshape(seg_out, half, op)
-        return carry
-
-    lax.fori_loop(0, 2 * per, conv_one, 0)
+    def conv_one(j):
+        def segment(seg, carry):
+            parts = []
+            for b in range(2):
+                taps = [
+                    b_in[j, pl.ds(seg * seg_slots + u, seg_out), :, b * TILE : (b + 3) * TILE].reshape(
+                        seg_out * half, 3 * TILE
+                    )
+                    for u in range(3)
+                ]
+                parts.append(jnp.concatenate(taps, axis=1))
+            result = dot(jnp.concatenate(parts, axis=0), w1[...])
+            for b in range(2):
+                raw1[j, b, pl.ds(seg * seg_out, seg_out)] = result[
+                    b * seg_out * half : (b + 1) * seg_out * half
+                ].reshape(seg_out, half, op)
+            return carry
+
+        lax.fori_loop(0, 2, segment, 0)
 
     cols = ref["cols"]
     pixel = iota((half, op), 0)
 
-    def activate(step, carry):
-        j, i = step // (2 * seg_out), lax.rem(step, 2 * seg_out)
-        seg = (i >= seg_out).astype(jnp.int32)
-        first = jnp.where(seg == 0, base[0], base[1])
-        tall = jnp.where(seg == 0, jnp.where(j == 0, high[0][0], high[1][0]), jnp.where(j == 0, high[0][1], high[1][1]))
-        broad = jnp.where(seg == 0, jnp.where(j == 0, wide[0][0], wide[1][0]), jnp.where(j == 0, wide[0][1], wide[1][1]))
-        broad = jnp.where(first + i - 1 < tall, broad, 0)
-        acts = []
-        for b in range(2):
-            pre = raw1[j, b, i] * scale1 + bias1
-            gate = 1.0 / (1.0 + jnp.exp(-pre))
-            mask = 2 * pixel + b < broad
-            lift = pre * gate
-            grad1[j, b, i] = jnp.where(mask, gate + lift * (1.0 - gate), 0.0)
-            acts.append(jnp.where(mask, lift, 0.0).astype(BF16).astype(F32))
-        even, odd = acts
-        before = jnp.where(pixel == 0, 0.0, pltpu.roll(odd, 1, 0))
-        after = jnp.where(pixel == half - 1, 0.0, pltpu.roll(even, half - 1, 0))
-        cols[j, 0, i] = before + even
-        cols[j, 1, i] = even + odd
-        cols[j, 2, i] = odd + after
-        return carry
-
-    lax.fori_loop(0, 2 * per * seg_out, activate, 0)
+    def activate(j):
+        def line(i, carry):
+            seg = (i >= seg_out).astype(jnp.int32)
+            broad = jnp.where(choose(seg, base) + i - 1 < choose(seg, high[j]), choose(seg, wide[j]), 0)
+            acts = []
+            for b in range(2):
+                pre = raw1[j, b, i] * scale1 + bias1
+                gate = 1.0 / (1.0 + jnp.exp(-pre))
+                mask = 2 * pixel + b < broad
+                lift = pre * gate
+                grad1[j, b, i] = jnp.where(mask, gate + lift * (1.0 - gate), 0.0)
+                acts.append(jnp.where(mask, lift, 0.0).astype(BF16).astype(F32))
+            even, odd = acts
+            before = jnp.where(pixel == 0, 0.0, pltpu.roll(odd, 1, 0))
+            after = jnp.where(pixel == half - 1, 0.0, pltpu.roll(even, half - 1, 0))
+            cols[j, 0, i] = before + even
+            cols[j, 1, i] = even + odd
+            cols[j, 2, i] = odd + after
+            return carry
+
+        lax.fori_loop(0, 2 * seg_out, line, 0, unroll=2)
 
     box = ref["box"]
 
-    def boxes(step, carry):
-        j, i = step // pairs, lax.rem(step, pairs)
-        above = jnp.where(i == cut // 2, keep, 1.0)
-        below = jnp.where(i == cut // 2 - 1, keep, 1.0)
-        for w in range(3):
-            lines = [cols[j, w, 2 * i + k] for k in range(4)]
-            for u in range(3):
-                one, two = lines[u], lines[u + 1]
-                if u == 0:
-                    one = one * above
-                if u == 2:
-                    two = two * below
-                tap = 3 * u + w
-                box[j, i, :, tap * op : (tap + 1) * op] = (one + two).astype(BF16)
-        return carry
-
-    lax.fori_loop(0, per * pairs, boxes, 0)
-
-    cot_x.wait_recv()
-    for copy in cot_halo:
-        copy.wait_recv()
+    def boxes(j):
+        def line(i, carry):
+            above = jnp.where(i == cut // 2, keep, 1.0)
+            below = jnp.where(i == cut // 2 - 1, keep, 1.0)
+            for w in range(3):
+                lines = [cols[j, w, 2 * i + k] for k in range(4)]
+                for u in range(3):
+                    upper, lower = lines[u], lines[u + 1]
+                    if u == 0:
+                        upper = upper * above
+                    if u == 2:
+                        lower = lower * below
+                    tap = 3 * u + w
+                    box[j, i, :, tap * op : (tap + 1) * op] = (upper + lower).astype(BF16)
+            return carry
+
+        lax.fori_loop(0, pairs, line, 0, unroll=2)
+
     quart = ref["quart"]
 
-    def quarter(step, carry):
-        j, i = step // (pairs + 2), lax.rem(step, pairs + 2)
-        inner = jnp.minimum(jnp.maximum(i - 1, 0), pairs - 1)
-        own = jnp.where((i == 0) | (i == pairs + 1), cotr[j, c, i], cot[c * per + j, inner])
-        other = cotr[j, o, i]
-        first = jnp.where(c == 0, own, other)
-        second = jnp.where(c == 0, other, own)
-        line = jnp.concatenate([first, second, jnp.zeros((half, op - cout), BF16)], axis=1)
-        quart[j, i] = (line.astype(F32) * 0.25).astype(BF16)
-        return carry
-
-    lax.fori_loop(0, per * (pairs + 2), quarter, 0)
-    own_px = pairs * half
+    def quarter(j):
+        def put(i, own, other):
+            first = jnp.where(c == 0, own, other)
+            second = jnp.where(c == 0, other, own)
+            line = jnp.concatenate([first, second, jnp.zeros((half, op - cout), BF16)], axis=1)
+            quart[j, i] = (line.astype(F32) * 0.25).astype(BF16)
+
+        def inner(i, carry):
+            put(i + 1, cot[c * per + j, i], cotr[j, o, i + 1])
+            return carry
+
+        lax.fori_loop(0, pairs, inner, 0, unroll=4)
+        for i in (0, pairs + 1):
+            put(i, cotr[j, c, i], cotr[j, o, i])
 
     def owned(j):
         return quart[j, 1 : pairs + 1].reshape(own_px, op)
 
     wire2, wire1 = ref["wire2"], ref["wire1"]
-    acc2 = ref["acc2"]
-    acc0 = ref["acc0"]
-    for j in range(per):
-        given = owned(j)[:, 0:cout]
-        value = dot(given, box[j].reshape(own_px, 9 * op), TN)
-        skip = dot(given, xb[j, 1 : pairs + 1].reshape(own_px, TILE), TN)
-        acc2[...] = value if j == 0 else acc2[...] + value
-        acc0[...] = skip if j == 0 else acc0[...] + skip
-    spare = lanes_two - 9 * cout - cin
-    for ch in range(2):
-        rows_at = slice(ch * co, (ch + 1) * co)
-        parts = [acc2[rows_at, tap * op : tap * op + cout] for tap in range(9)]
-        parts += [acc0[rows_at, 0:cin], jnp.zeros((co, spare), F32)]
-        wire2[ch] = jnp.concatenate(parts, axis=1).astype(BF16)
-
     half_rows = co // 2
     kept_rows = pl.ds(core * half_rows, half_rows)
     mate_rows = pl.ds((1 - core) * half_rows, half_rows)
@@ -614,10 +632,13 @@
         for ch in range(2):
             value = wire[ch, kept_rows].astype(F32) + got[ch].astype(F32)
             for chip_at in range(n_chips):
-                shares[ch, chip_at] = value[:, chip_at * share : (chip_at + 1) * share].astype(BF16)
+                part = value[:, chip_at * share : (chip_at + 1) * share]
+                shares[ch, chip_at] = part.astype(BF16)
+
                 @pl.when(my_id == ch * n_chips + chip_at)
                 def _():
-                    mine[...] = value[:, chip_at * share : (chip_at + 1) * share]
+                    mine[...] = part
+
         copies = []
         for delta in range(1, 2 * n_chips):
             other = lax.rem(my_id + delta, 2 * n_chips)
@@ -631,7 +652,6 @@
         for delta in range(1, 2 * n_chips):
             copies[delta - 1].wait_recv()
             value = value + landing[delta - 1].astype(F32)
-        share = value.shape[1]
         result[chip, kept_rows] = value.astype(BF16)
         back = []
         for delta in range(1, n_chips):
@@ -646,31 +666,70 @@
             copy.wait_recv()
         return begin(result.at[:, kept_rows], result.at[:, kept_rows], (mate, c))
 
+    one.turn()
+    prepare(0)
+    one.turn()
+    two.turn()
+    one.turn()
+    vec_x.wait_recv()
+    for tap in range(9):
+        rows_at = slice(tap * cin, (tap + 1) * cin)
+        place(w1, tap * TILE, k10[rows_at], k10h[rows_at], TILE)
+    rows_at = slice(n1, n1 + cin)
+    place(w0, 0, k10[rows_at], k10h[rows_at], TILE)
+    left1, right1, sigma1 = power(row_of(0), w1[...])
+    left0, right0, sigma0 = power(row_of(2), w0[...])
+    scale1, scale0 = 1.0 / sigma1, 1.0 / sigma0
+    bias1, bias2 = row_of(3), row_of(4)
+    left1_ref, left2_ref, left0_ref = ref["left1"], ref["left2"], ref["left0"]
+    left1_ref[0:1] = left1
+    left0_ref[0:1] = left0
+    conv_one(0)
+    activate(0)
+    two.turn()
+    boxes(0)
+    for j in range(1, per):
+        prepare(j)
+        conv_one(j)
+        if j == 1:
+            two.turn()
+        activate(j)
+        boxes(j)
+    cot_x.wait_recv()
+    for copy in cot_halo:
+        copy.wait_recv()
+    for j in range(per):
+        quarter(j)
+
+    acc0 = ref["acc0"]
+    given = jnp.concatenate([owned(j) for j in range(per)], axis=0)[:, 0:cout]
+    value = dot(given, box[...].reshape(per * own_px, 9 * op), TN)
+    skip = dot(given, xb[:, 1 : pairs + 1].reshape(per * own_px, TILE), TN)
+    acc0[...] = skip
+    spare = lanes_two - 9 * cout - cin
+    for ch in range(2):
+        rows_at = slice(ch * co, (ch + 1) * co)
+        parts = [value[rows_at, tap * op : tap * op + cout] for tap in range(9)]
+        parts += [skip[rows_at, 0:cin], jnp.zeros((co, spare), F32)]
+        wire2[ch] = jnp.concatenate(parts, axis=1).astype(BF16)
     sum2 = sum_mate(wire2, ref["got2"])
 
-    k2_x.wait_recv()
-    k2_m = begin(k2h.at[part2], k2h.at[part2], (mate, c))
-    k0_x.wait_recv()
-    place(w0, 0, k0[...], k0h[...], TILE)
-    k2_m.wait_recv()
+    for turn in range(two.level, bits + 1):
+        two.turn()
     for tap in range(9):
         rows_at = slice(tap * cout, (tap + 1) * cout)
         place(w2, tap * op, k2[rows_at], k2h[rows_at], op)
     left2, right2, sigma2 = power(row_of(1), w2[...])
-    left0, right0, sigma0 = power(row_of(2), w0[...])
-    scale2, scale0 = 1.0 / sigma2, 1.0 / sigma0
-    left2_ref, left0_ref = ref["left2"], ref["left0"]
+    scale2 = 1.0 / sigma2
     left2_ref[0:1] = left2
-    left0_ref[0:1] = left0
 
     taps_sum = ref["taps_sum"]
-    spot = iota(((pairs + 2) * half, op), 0)
+    spot = iota((all_px, op), 0)
     at_left = lax.rem(spot, half) == 0
     at_right = lax.rem(spot, half) == half - 1
-    all_px = (pairs + 2) * half
     g_pre = ref["g_pre"]
-    dot1 = jnp.zeros((half, op), F32)
-    for j in range(per):
+
+    def back_two(j, dot1):
         given = quart[j].reshape(all_px, op)
         for u in range(3):
             t0, t1, t2 = [
@@ -681,8 +740,10 @@
             taps_sum[u, 0] = even.reshape(pairs + 2, half, op)
             taps_sum[u, 1] = odd.reshape(pairs + 2, half, op)
 
-        def back_rows(i, carry):
+        def line(i, carry):
             hold = jnp.where(i == cut // 2, keep, 1.0)
+            own_even = jnp.where(i < pairs, 1.0, 0.0)
+            own_odd = jnp.where(i > 0, 1.0, 0.0)
             for b in range(2):
                 upper, lower = taps_sum[2, b, i], taps_sum[0, b, i + 1]
                 even = lower + taps_sum[1, b, i + 1] + hold * upper
@@ -691,13 +752,16 @@
                 odd = (odd * scale2 * grad1[j, b, 2 * i]).astype(BF16)
                 g_pre[j, b, 2 * i + 1] = even
                 g_pre[j, b, 2 * i] = odd
-                own_even = jnp.where(i < pairs, 1.0, 0.0)
-                own_odd = jnp.where(i > 0, 1.0, 0.0)
                 carry = carry + own_even * even.astype(F32) * raw1[j, b, 2 * i + 1]
                 carry = carry + own_odd * odd.astype(F32) * raw1[j, b, 2 * i]
             return carry
 
-        dot1 = lax.fori_loop(0, pairs + 1, back_rows, dot1)
+        return lax.fori_loop(0, pairs + 1, line, dot1, unroll=3)
+
+    dot1 = back_two(0, jnp.zeros((half, op), F32))
+    far2 = sum_far(sum2, wire2, ref["got2"], ref["shares2"], ref["landing2"], ref["mine2"])
+    for j in range(1, per):
+        dot1 = back_two(j, dot1)
 
     out_b, send_b, got_b = ref["out_b"], ref["send_b"], ref["got_b"]
     dot2 = jnp.zeros((1, op), F32)
@@ -713,9 +777,6 @@
         first, second = value[:, 0:co], value[:, co:cout]
         out_b[c * per + j] = jnp.where(c == 0, first, second).reshape(pairs, half, co)
         send_b[j] = jnp.where(c == 0, second, first).reshape(pairs, half, co)
-    out_x = begin(send_b, got_b, (me, o))
-
-    far2 = sum_far(sum2, wire2, ref["got2"], ref["shares2"], ref["landing2"], ref["mine2"])
 
     acc1 = ref["acc1"]
 
@@ -754,16 +815,16 @@
         parts.append(jnp.zeros((co, spare), F32))
         wire1[ch] = jnp.concatenate(parts, axis=1).astype(BF16)
     sum1 = sum_mate(wire1, ref["got1"])
+    out_x = begin(send_b, got_b, (me, o))
 
     taps_in, skip_back = ref["taps_in"], ref["skip_back"]
     pixel_in = iota((half, TILE), 0)
     out_g, send_g, got_g = ref["out_g"], ref["send_g"], ref["got_g"]
-    far1 = None
-    back2 = None
-    for j in range(per):
+
+    def back_products(j):
         skip_back[...] = (dot(owned(j), w0[...], NT) * scale0).reshape(pairs, half, TILE)
 
-        def tap_products(step, carry):
+        def some(step, carry):
             b, part = step // 2, lax.rem(step, 2)
             given = g_pre[j, b, pl.ds(part * seg_out, seg_out)].reshape(seg_out * half, op)
             taps_in[b, pl.ds(part * seg_out, seg_out)] = dot(given, w1[...], NT).reshape(
@@ -771,9 +832,10 @@
             )
             return carry
 
-        lax.fori_loop(0, 4, tap_products, 0)
-
-        def input_rows(p, carry):
+        lax.fori_loop(0, 4, some, 0)
+
+    def input_rows(j):
+        def two_rows(p, carry):
             lines = []
             for a in range(2):
                 r = 2 * p + a
@@ -792,10 +854,7 @@
                 even = column_sum(0, 1) + column_sum(1, 0) + jnp.where(pixel_in == 0, 0.0, before)
                 odd = column_sum(1, 1) + column_sum(2, 0) + jnp.where(pixel_in == half - 1, 0.0, after)
                 seg = (r >= cut).astype(jnp.int32)
-                first = jnp.where(seg == 0, base[0], base[1])
-                tall = jnp.where(seg == 0, high[j][0], high[j][1])
-                broad = jnp.where(seg == 0, wide[j][0], wide[j][1])
-                broad = jnp.where(first + r < tall, broad, 0)
+                broad = jnp.where(choose(seg, base) + r < choose(seg, high[j]), choose(seg, wide[j]), 0)
                 for b, value in ((0, even), (1, odd)):
                     at = (2 * a + b) * half
                     x = xp[j, p + 1, at : at + half].astype(F32)
@@ -810,31 +869,25 @@
             send_g[j, p] = other
             return carry
 
-        lax.fori_loop(0, pairs, input_rows, 0)
-        copy = begin(send_g.at[j], got_g.at[j], (me, o))
-        if j == 0:
-            grad_x = [copy]
-            far1 = sum_far(sum1, wire1, ref["got1"], ref["shares1"], ref["landing1"], ref["mine1"])
-            back2 = gather_far(far2, ref["landing2"], ref["mine2"], ref["result2"])
-        else:
-            grad_x.append(copy)
-
-    last2 = gather_mate(back2, ref["result2"])
-    back1 = gather_far(far1, ref["landing1"], ref["mine1"], ref["result1"])
-    out_x.wait_recv()
-    out_b[mine_o] = got_b[...].reshape(per, pairs, half, co)
-
-    def unpack(p, carry):
-        for j in range(per):
+        lax.fori_loop(0, pairs, two_rows, 0, unroll=4)
+        return begin(send_g.at[j], got_g.at[j], (me, o))
+
+    def unpack(j):
+        def line(p, carry):
             out_g[o * per + j, 2 * p] = got_g[j, p, :, 0:width]
             out_g[o * per + j, 2 * p + 1] = got_g[j, p, :, width:TILE]
-        return carry
-
-    for copy in grad_x:
-        copy.wait_recv()
-    lax.fori_loop(0, pairs, unpack, 0)
-
-    last1 = gather_mate(back1, ref["result1"])
+            return carry
+
+        grad_x[j].wait_recv()
+        lax.fori_loop(0, pairs, line, 0, unroll=4)
+
+    back_products(0)
+    far1 = sum_far(sum1, wire1, ref["got1"], ref["shares1"], ref["landing1"], ref["mine1"])
+    grad_x = [input_rows(0)]
+    back2 = gather_far(far2, ref["landing2"], ref["mine2"], ref["result2"])
+    for j in range(1, per):
+        back_products(j)
+        grad_x.append(input_rows(j))
 
     def own_half(row):
         return jnp.where(c == 0, row[:, 0:co], row[:, co:cout])
@@ -846,38 +899,76 @@
     def compact(row, size, padded):
         return jnp.concatenate([row[:, t * padded : t * padded + size] for t in range(9)], axis=1)
 
-    def lines_of(result):
-        share = result.shape[2]
-        return [result[chip_at, :, 0:share].astype(F32) for chip_at in range(n_chips)]
-
+    def turned(part, out, at):
+        some = part.shape[1]
+        if some < TILE:
+            part = jnp.concatenate([part, jnp.zeros((co, TILE - some), F32)], axis=1)
+        part = jnp.concatenate([part, jnp.zeros((TILE - co, TILE), F32)], axis=0)
+        out[at : at + some] = jnp.transpose(part)[0:some, 0:co]
+
+    def outer(left, right, out):
+        columns = column_of(right)
+        for at in range(0, left.shape[1], TILE):
+            some = min(TILE, left.shape[1] - at)
+            turned(columns[:, 0:some] * left[:, at : at + some], out, at)
+
+    def flat_of(result):
+        return jnp.concatenate([result[at].astype(F32) for at in range(n_chips)], axis=1)
+
+    corr1, corr2, corr0 = ref["corr1"], ref["corr2"], ref["corr0"]
+    outer(compact(left1_ref[0:1], cin, TILE), right1 * (scale1 * scale1), corr1)
+    outer(compact(left2_ref[0:1], cout, op), right2 * (scale2 * scale2), corr2)
+    outer(left0_ref[0:1, 0:cin], right0 * (scale0 * scale0), corr0)
+    back1 = gather_far(far1, ref["landing1"], ref["mine1"], ref["result1"])
+    last2 = gather_mate(back2, ref["result2"])
+    out_x.wait_recv()
+    out_b[mine_o] = got_b[...]
+    unpack(0)
+    last2.wait_recv()
+    flat2 = flat_of(ref["result2"])
+    out_k1, out_k2, out_k0 = ref["out_k1"], ref["out_k2"], ref["out_k0"]
+    for at in range(0, n2, TILE):
+        turned(flat2[:, at : min(at + TILE, n2)] * scale2, out_k2, at)
+    turned(flat2[:, n2 : n2 + cin] * scale0, out_k0, 0)
+    last1 = gather_mate(back1, ref["result1"])
+    for j in range(1, per):
+        unpack(j)
     last1.wait_recv()
-    flat1 = jnp.concatenate(lines_of(ref["result1"]), axis=1)
-    extra = flat1[:, 9 * cin : 9 * cin + 10]
+    flat1 = flat_of(ref["result1"])
+    extra = flat1[:, n1 : n1 + 10]
     dot_values = [extra[0:1, 4 + 2 * i : 5 + 2 * i] + extra[0:1, 5 + 2 * i : 6 + 2 * i] for i in range(3)]
     biases = jnp.concatenate([extra, jnp.zeros((co, TILE - 10), F32)], axis=1)
     biases = jnp.transpose(jnp.concatenate([biases, jnp.zeros((TILE - co, TILE), F32)], axis=0))
     ref["out_b1"][...] = biases[0:1, 0:co] + biases[1:2, 0:co]
     ref["out_b2"][...] = biases[2:3, 0:co] + biases[3:4, 0:co]
-
-    def finish(flat, left, right, scale, value, out):
-        columns = column_of(right) * (value * scale * scale)
-        size = flat.shape[1]
-        for at in range(0, size, TILE):
-            some = min(TILE, size - at)
-            part = flat[:, at : at + some] * scale - columns[:, 0:some] * left[:, at : at + some]
-            if some < TILE:
-                part = jnp.concatenate([part, jnp.zeros((co, TILE - some), F32)], axis=1)
-            part = jnp.concatenate([part, jnp.zeros((TILE - co, TILE), F32)], axis=0)
-            out[at : at + some] = jnp.transpose(part)[0:some, 0:co]
-
-    finish(flat1[:, 0 : 9 * cin], compact(left1_ref[0:1], cin, TILE), right1, scale1, dot_values[0], ref["out_k1"])
-    last2.wait_recv()
-    flat2 = jnp.concatenate(lines_of(ref["result2"]), axis=1)
-    finish(flat2[:, 0 : 9 * cout], compact(left2_ref[0:1], cout, op), right2, scale2, dot_values[1], ref["out_k2"])
-    finish(flat2[:, 9 * cout : 9 * cout + cin], left0_ref[0:1, 0:cin], right0, scale0, dot_values[2], ref["out_k0"])
+    for at in range(0, n1, TILE):
+        turned(flat1[:, at : min(at + TILE, n1)] * scale1, out_k1, at)
+    for out, corr, value in ((out_k1, corr1, 0), (out_k2, corr2, 1), (out_k0, corr0, 2)):
+        out[...] = out[...] - corr[...] * dot_values[value]
 
     for copy in sends:
         copy.wait_send()
+
+
+def hand_over(arrays):
+    number = len(arrays)
+
+    def copy_all(*refs):
+        sem = refs[-1]
+        copies = [pltpu.make_async_copy(refs[i], refs[number + i], sem.at[i]) for i in range(number)]
+        for copy in copies:
+            copy.start()
+        for copy in copies:
+            copy.wait()
+
+    return pl.pallas_call(
+        copy_all,
+        out_shape=[jax.ShapeDtypeStruct(a.shape, a.dtype) for a in arrays],
+        in_specs=[pl.BlockSpec(memory_space=pltpu.VMEM)] * number,
+        out_specs=[pl.BlockSpec(memory_space=pl.ANY)] * number,
+        scratch_shapes=[pltpu.SemaphoreType.DMA((number,))],
+        name="hand_over",
+    )(*[pltpu.with_memory_space_constraint(a, pltpu.VMEM) for a in arrays])
 
 
 def fused(n_rows, arrays):
@@ -893,6 +984,9 @@
     lanes_two = -(-(9 * cout + cin) // step) * step
     lanes_one = -(-(9 * cin + 10) // step) * step
     seg_out = rows // 2 + 1
+    bits = 3 if n_rows % 8 == 0 else 2
+    share1 = -(-(10 * cin) // 64) * 16
+    share2 = -(-(9 * cout) // (16 * 2**bits)) * 16
     inputs = {
         "vh": valid_h,
         "vw": valid_w,
@@ -918,12 +1012,15 @@
     }
     vm = pltpu.VMEM
     scratch = {
+        "img_v": vm((micros, rows, ci, width), BF16),
+        "cot_v": vm(cotangent.shape, BF16),
+        "k10_v": vm((4 * share1, co), BF16),
+        "k2_v": vm((2**bits * share2, co), BF16),
+        "k10h": vm((4 * share1, co), BF16),
+        "k2h": vm((2**bits * share2, co), BF16),
         "imgr": vm((per, 2, pairs + 2, ci, TILE), BF16),
         "sendp": vm((per, pairs, ci, TILE), BF16),
         "vec": vm((2, 8, TILE), F32),
-        "k1h": vm((9 * cin, co), BF16),
-        "k2h": vm((9 * cout, co), BF16),
-        "k0h": vm((cin, co), BF16),
         "cotr": vm((per, 2, pairs + 2, half, co), BF16),
         "perm_in": vm((8 * half, TILE), BF16),
         "perm_x": vm((5 * half, TILE), BF16),
@@ -941,7 +1038,6 @@
         "cols": vm((per, 3, 2 * seg_out, half, op), F32),
         "box": vm((per, pairs, half, 9 * op), BF16),
         "quart": vm((per, pairs + 2, half, op), BF16),
-        "acc2": vm((cout, 9 * op), F32),
         "acc0": vm((cout, TILE), F32),
         "acc1": vm((cout, 9 * TILE), F32),
         "taps_sum": vm((3, 2, pairs + 2, half, op), F32),
@@ -953,6 +1049,8 @@
         "send_g": vm((per, pairs, ci, TILE), BF16),
         "got_g": vm((per, pairs, ci, TILE), BF16),
     }
+    for name, size in (("corr1", 9 * cin), ("corr2", 9 * cout), ("corr0", cin)):
+        scratch[name] = vm((size, co), F32)
     for name, lanes in (("1", lanes_one), ("2", lanes_two)):
         share = lanes // n_chips
         scratch["wire" + name] = vm((2, co, lanes), BF16)
@@ -961,25 +1059,29 @@
         scratch["landing" + name] = vm((2 * n_chips - 1, co // 2, share), BF16)
         scratch["mine" + name] = vm((co // 2, share), F32)
         scratch["result" + name] = vm((n_chips, co, share), BF16)
-    copies = 18 + per * 2 + 2 * (1 + 2 * n_chips - 1 + n_chips - 1 + 1)
+    copies = 12 + bits + 6 * per + 2 * (1 + 2 * n_chips - 1 + n_chips - 1 + 1)
+    scratch["lsem"] = pltpu.SemaphoreType.DMA((5,))
     scratch["ssem"] = pltpu.SemaphoreType.DMA((copies,))
     scratch["rsem"] = pltpu.SemaphoreType.DMA((copies,))
     names = list(inputs) + list(outputs) + list(scratch)
-    dims = (micros, rows, width, ci, co, lanes_two, lanes_one)
+    dims = (micros, rows, width, ci, co, lanes_two, lanes_one, bits, share1, share2)
     smem = pl.BlockSpec(memory_space=pltpu.SMEM)
     vmem = pl.BlockSpec(memory_space=pltpu.VMEM)
+    hbm = pl.BlockSpec(memory_space=pltpu.HBM)
+    large = ("img", "k1", "k2", "k0", "cot")
+    small = ("b1", "b2", "q1", "q2", "q0")
     results = pl.pallas_call(
         functools.partial(fused_kernel, names, n_rows, dims),
-        out_shape=list(outputs.values()),
-        in_specs=[smem, smem] + [vmem] * (len(inputs) - 2),
+        out_shape=[pltpu.VMEM(a.shape, a.dtype) for a in outputs.values()],
+        in_specs=[smem, smem] + [vmem if n in small else hbm for n in list(inputs)[2:]],
         out_specs=[vmem] * len(outputs),
         scratch_shapes=list(scratch.values()),
         compiler_params=pltpu.CompilerParams(
-            collective_id=0, has_side_effects=True, vmem_limit_bytes=60 * 1024 * 1024
+            collective_id=0, has_side_effects=True, vmem_limit_bytes=48 * 1024 * 1024
         ),
         name="down_block",
-    )(*inputs.values())
-    out_b, out_g, out_k1, out_k2, out_k0, out_b1, out_b2 = results
+    )(*[pltpu.with_memory_space_constraint(a, pltpu.HBM) if n in large else a for n, a in inputs.items()])
+    out_b, out_g, out_k1, out_k2, out_k0, out_b1, out_b2 = hand_over(results)
     return (
         out_b,
         jnp.transpose(out_g, (0, 1, 3, 2)),

time: 70.7 us -> 56.9 us (0.80)
  Pallas kernels: 61.7 us -> 54.8 us
  local copies, waits for them, and re-layouts: 7.28 us -> 0.69 us
    pallas_call x1, Pallas kernels: 61.7 us -> 53.3 us  [fused(): pl.pallas_call(functools.partial(fused_kernel, names, n_rows, dims), out_...]
    unnamed x17 -> x14, local copies, waits for them, and re-layouts: 7.28 us -> 0.69 us
    pallas_call x0 -> x1, Pallas kernels: none -> 1.47 us  [hand_over(): pl.pallas_call(copy_all, out_shape=[jax.ShapeDtypeStruct(a.shape, a.dtype...]
where the time goes in v2:
time: 56.9 us; the launch traced here: 56.2 us
  Pallas kernels  54.8 us (96%)
  between operations  0.7 us (1%)
  local copies, waits for them, and re-layouts  0.69 us (1%)
    pallas_call x1, Pallas kernels, fused(): pl.pallas_call(functools.partial(fused_kernel, names, n_rows, dims), out_...  53.3 us
    pallas_call x1, Pallas kernels, hand_over(): pl.pallas_call(copy_all, out_shape=[jax.ShapeDtypeStruct(a.shape, a.dtype...  1.47 us

profile of v2, /device:TPU:0, one launch (start us, length us, event | category | flops | bytes accessed | tf_op | source)
XLA Modules:
  0.0 56.2 jit_solution(4458540688929926207)
XLA Ops:
  0.6 0.0 copy-start.5
  0.6 0.0 copy-start.6
  0.7 0.0 copy-start.1
  0.7 0.0 copy-start
  0.7 0.0 copy-start.2
  0.7 0.0 copy-start.3
  0.7 0.0 copy-start.4
  0.7 0.6 %copy-done.5 = f32[96]{0:T(128)S(1)} copy-done((f32[96]{0:T(128)S(1)}, f32[96]{0:T(128)}, u32[]{:S(2)}) %copy-start.5) | copy-done | bytes 408
  1.3 0.0 copy-done.6
  1.3 0.0 copy-done.1
  1.4 0.0 copy-done
  1.4 0.0 copy-done.2
  1.4 0.0 copy-done.3
  1.4 0.0 copy-done.4
  1.4 53.3 %down_block.1 = (bf16[4,8,32,96]{3,2,1,0:T(8,128)(2,1)S(1)}, bf16[4,16,48,64]{3,2,1,0:T(8,128)(2,1)S(1)}, f32[864,96]{1,0:T(8,128)S(1)}, f32[1728,96]{1,0:T(8,12...) custom-call(s32[4,4]{1,0:T(4,128)S(1)} %copy-done, s32[4,4]{1,0:T(4,128)S(1)} %copy-done.1, ...), custom_call_target="tpu_custom_call" | custom-call | tf_op jit(solution)/shard_map/down_block/pallas_call | solution.py:1073
  54.7 1.5 %hand_over.1 = (bf16[4,8,32,96]{3,2,1,0:T(8,128)(2,1)}, bf16[4,16,48,64]{3,2,1,0:T(8,128)(2,1)}, f32[864,96]{1,0:T(8,128)}, f32[1728,96]{1,0:T(8,128)}, f32[96,9...) custom-call(bf16[4,8,32,96]{3,2,1,0:T(8,128)(2,1)S(1)} %get-tuple-element.21.refs_0_, ...), custom_call_target="tpu_custom_call" | custom-call | tf_op jit(solution)/shard_map/hand_over/pallas_call | solution.py:964
Async XLA Ops:
  0.6 0.7 %copy-start.5 = (f32[96]{0:T(128)S(1)}, f32[96]{0:T(128)}, u32[]{:S(2)}) copy-start(f32[96]{0:T(128)} %param.21) | copy-start | bytes 1156
  0.6 0.7 %copy-start.6 = (f32[96]{0:T(128)S(1)}, f32[96]{0:T(128)}, u32[]{:S(2)}) copy-start(f32[96]{0:T(128)} %param.22) | copy-start | bytes 1156
  0.7 0.7 %copy-start.1 = (s32[4,4]{1,0:T(4,128)S(1)}, s32[4,4]{1,0:T(4,128)}, u32[]{:S(2)}) copy-start(s32[4,4]{1,0:T(4,128)} %refs_1_.1) | copy-start | bytes 196
  0.7 0.7 %copy-start = (s32[4,4]{1,0:T(4,128)S(1)}, s32[4,4]{1,0:T(4,128)}, u32[]{:S(2)}) copy-start(s32[4,4]{1,0:T(4,128)} %refs_0_.1) | copy-start | bytes 196
  0.7 0.7 %copy-start.2 = (bf16[96]{0:T(256)(128)(2,1)S(1)}, bf16[96]{0:T(256)(128)(2,1)}, u32[]{:S(2)}) copy-start(bf16[96]{0:T(256)(128)(2,1)} %param.18) | copy-start | bytes 580
  0.7 0.7 %copy-start.3 = (bf16[96]{0:T(256)(128)(2,1)S(1)}, bf16[96]{0:T(256)(128)(2,1)}, u32[]{:S(2)}) copy-start(bf16[96]{0:T(256)(128)(2,1)} %param.19) | copy-start | bytes 580
  0.7 0.7 %copy-start.4 = (f32[96]{0:T(128)S(1)}, f32[96]{0:T(128)}, u32[]{:S(2)}) copy-start(f32[96]{0:T(128)} %param.20) | copy-start | bytes 1156

commit v3 on v2

--- a/solution.py
+++ b/solution.py
@@ -243,8 +243,9 @@
     return (
         n_ch == 2
         and micros % 2 == 0
-        and n_rows % 2 == 0
         and n_rows >= 4
+        and n_rows % min(8, n_rows) == 0
+        and n_rows % 4 == 0
         and rows_dev % 8 == 0
         and SHIFT % rows_dev == rows_dev // 2
         and IMG % rows_dev == 0
@@ -294,7 +295,7 @@
 
 
 def fused_kernel(names, n_rows, dims, *refs):
-    micros, rows, width, ci, co, lanes_two, lanes_one, bits, share1, share2 = dims
+    micros, rows, width, ci, co, lanes_each, bits, share1, share2 = dims
     ref = dict(zip(names, refs))
     half = width // 2
     per = micros // 2
@@ -320,14 +321,25 @@
     up = lax.rem(me + n_rows - 1, n_rows)
     down = lax.rem(me + 1, n_rows)
     my_id = c * n_chips + chip
+    sub = min(4, n_chips)
+    cubes = n_chips // sub
+    spot_in, cube = lax.rem(chip, sub), chip // sub
+    my_id = c * sub + spot_in
     far = []
-    for delta in range(1, 2 * n_chips):
-        other = lax.rem(my_id + delta, 2 * n_chips)
-        far.append((2 * lax.rem(other, n_chips) + core, other // n_chips))
+    for delta in range(1, 2 * sub):
+        other = lax.rem(my_id + delta, 2 * sub)
+        far.append((2 * (cube * sub + lax.rem(other, sub)) + core, other // sub))
+    across = []
+    for delta in range(1, cubes):
+        across.append((2 * (lax.rem(cube + delta, cubes) * sub + spot_in) + core, c))
+    around = []
+    for delta in range(1, 2 * sub):
+        other = lax.rem(2 * spot_in + core + delta, 2 * sub)
+        around.append((2 * cube * sub + other, c))
     near = [(me, o), (mate, c), (up, c), (up, o), (down, c), (down, o)]
 
     barrier = pltpu.get_barrier_semaphore()
-    for device in near + far:
+    for device in near + far + across + around:
         pl.semaphore_signal(barrier, inc=1, device_id=device, device_id_type=MESH)
 
     count = [0]
@@ -419,7 +431,7 @@
     for load in loads[1:]:
         load.wait()
 
-    pl.semaphore_wait(barrier, len(near) + len(far))
+    pl.semaphore_wait(barrier, len(near + far + across + around))
 
     k10h, k2h, cotr = ref["k10h"], ref["k2h"], ref["cotr"]
     spots = [core] + [lax.rem(me // 2**b, 2) for b in range(1, bits)]
@@ -618,53 +630,63 @@
     def owned(j):
         return quart[j, 1 : pairs + 1].reshape(own_px, op)
 
-    wire2, wire1 = ref["wire2"], ref["wire1"]
     half_rows = co // 2
     kept_rows = pl.ds(core * half_rows, half_rows)
     mate_rows = pl.ds((1 - core) * half_rows, half_rows)
 
-    def sum_mate(wire, got):
-        return begin(wire.at[:, mate_rows], got, (mate, c))
-
-    def sum_far(copy, wire, got, shares, landing, mine):
-        copy.wait_recv()
-        share = shares.shape[-1]
-        for ch in range(2):
-            value = wire[ch, kept_rows].astype(F32) + got[ch].astype(F32)
-            for chip_at in range(n_chips):
-                part = value[:, chip_at * share : (chip_at + 1) * share]
-                shares[ch, chip_at] = part.astype(BF16)
-
-                @pl.when(my_id == ch * n_chips + chip_at)
-                def _():
-                    mine[...] = part
-
-        copies = []
-        for delta in range(1, 2 * n_chips):
-            other = lax.rem(my_id + delta, 2 * n_chips)
-            copies.append(
-                begin(shares.at[other // n_chips, lax.rem(other, n_chips)], landing.at[delta - 1], far[delta - 1])
-            )
-        return copies
-
-    def gather_far(copies, landing, mine, result):
-        value = mine[...]
-        for delta in range(1, 2 * n_chips):
-            copies[delta - 1].wait_recv()
-            value = value + landing[delta - 1].astype(F32)
-        result[chip, kept_rows] = value.astype(BF16)
-        back = []
-        for delta in range(1, n_chips):
-            other = lax.rem(chip + delta, n_chips)
-            back.append(
-                begin(result.at[chip, kept_rows], result.at[chip, kept_rows], (2 * other + core, c))
-            )
-        return back
-
-    def gather_mate(copies, result):
-        for copy in copies:
-            copy.wait_recv()
-        return begin(result.at[:, kept_rows], result.at[:, kept_rows], (mate, c))
+    class Summed:
+        def __init__(self, name):
+            self.wire, self.got, self.shares, self.landing, self.mine, self.mids, self.result = [
+                ref[part + name] for part in ("wire", "got", "shares", "landing", "mine", "mids", "result")
+            ]
+            self.share = self.result.shape[2]
+            self.copies = [begin(self.wire.at[:, mate_rows], self.got, (mate, c))]
+
+        def arrived(self):
+            for copy in self.copies:
+                copy.wait_recv()
+
+        def to_owners(self):
+            self.arrived()
+            for ch in range(2):
+                value = self.wire[ch, kept_rows].astype(F32) + self.got[ch].astype(F32)
+                for at in range(sub):
+                    part = value[:, at * self.share : (at + 1) * self.share]
+                    self.shares[ch, at] = part.astype(BF16)
+
+                    @pl.when(my_id == ch * sub + at)
+                    def _():
+                        self.mine[...] = part
+
+            self.copies = []
+            for delta in range(1, 2 * sub):
+                other = lax.rem(my_id + delta, 2 * sub)
+                self.copies.append(
+                    begin(
+                        self.shares.at[other // sub, lax.rem(other, sub)], self.landing.at[delta - 1], far[delta - 1]
+                    )
+                )
+
+        def to_cubes(self):
+            self.arrived()
+            value = self.mine[...]
+            for delta in range(1, 2 * sub):
+                value = value + self.landing[delta - 1].astype(F32)
+            self.mids[cube] = value.astype(BF16)
+            self.copies = [begin(self.mids.at[cube], self.mids.at[cube], device) for device in across]
+
+        def to_all(self):
+            self.arrived()
+            value = self.mids[0].astype(F32)
+            for at in range(1, cubes):
+                value = value + self.mids[at].astype(F32)
+            self.result[spot_in, kept_rows] = value.astype(BF16)
+            place_at = self.result.at[spot_in, kept_rows]
+            self.copies = [begin(place_at, place_at, device) for device in around]
+
+        def flat(self):
+            self.arrived()
+            return jnp.concatenate([self.result[at].astype(F32) for at in range(sub)], axis=1)
 
     one.turn()
     prepare(0)
@@ -703,17 +725,23 @@
 
     acc0 = ref["acc0"]
     given = jnp.concatenate([owned(j) for j in range(per)], axis=0)[:, 0:cout]
-    value = dot(given, box[...].reshape(per * own_px, 9 * op), TN)
-    skip = dot(given, xb[:, 1 : pairs + 1].reshape(per * own_px, TILE), TN)
-    acc0[...] = skip
-    spare = lanes_two - 9 * cout - cin
-    for ch in range(2):
-        rows_at = slice(ch * co, (ch + 1) * co)
-        parts = [value[rows_at, tap * op : tap * op + cout] for tap in range(9)]
-        parts += [skip[rows_at, 0:cin], jnp.zeros((co, spare), F32)]
-        wire2[ch] = jnp.concatenate(parts, axis=1).astype(BF16)
-    sum2 = sum_mate(wire2, ref["got2"])
-
+    turned_quart = jnp.transpose(given)
+    group_a = None
+    for name, taps in (("a", range(0, 5)), ("b", range(5, 9))):
+        lanes = slice(taps[0] * op, (taps[-1] + 1) * op)
+        value = dot(turned_quart, box[:, :, :, lanes].reshape(per * own_px, len(taps) * op))
+        parts = [value[:, k * op : k * op + cout] for k in range(len(taps))]
+        if name == "b":
+            skip = dot(turned_quart, xb[:, 1 : pairs + 1].reshape(per * own_px, TILE))
+            acc0[...] = skip
+            parts.append(skip[:, 0:cin])
+        parts.append(jnp.zeros((cout, lanes_each - sum(part.shape[1] for part in parts)), F32))
+        flat = jnp.concatenate(parts, axis=1).astype(BF16)
+        for ch in range(2):
+            ref["wire" + name][ch] = flat[ch * co : (ch + 1) * co]
+        if name == "a":
+            group_a = Summed("a")
+    group_b = Summed("b")
     for turn in range(two.level, bits + 1):
         two.turn()
     for tap in range(9):
@@ -758,25 +786,11 @@
 
         return lax.fori_loop(0, pairs + 1, line, dot1, unroll=3)
 
-    dot1 = back_two(0, jnp.zeros((half, op), F32))
-    far2 = sum_far(sum2, wire2, ref["got2"], ref["shares2"], ref["landing2"], ref["mine2"])
-    for j in range(1, per):
+    group_a.to_owners()
+    group_b.to_owners()
+    dot1 = jnp.zeros((half, op), F32)
+    for j in range(per):
         dot1 = back_two(j, dot1)
-
-    out_b, send_b, got_b = ref["out_b"], ref["send_b"], ref["got_b"]
-    dot2 = jnp.zeros((1, op), F32)
-    dot0 = jnp.zeros((1, op), F32)
-    for j in range(per):
-        main = dot(box[j].reshape(own_px, 9 * op), w2[...])
-        skip = dot(xb[j, 1 : pairs + 1].reshape(own_px, TILE), w0[...])
-        given = owned(j).astype(F32)
-        dot2 = dot2 + jnp.sum(given * main, axis=0, keepdims=True)
-        dot0 = dot0 + jnp.sum(given * skip, axis=0, keepdims=True)
-        value = (main * scale2 + skip * scale0) * 0.25 + bias2
-        value = value.astype(BF16)
-        first, second = value[:, 0:co], value[:, co:cout]
-        out_b[c * per + j] = jnp.where(c == 0, first, second).reshape(pairs, half, co)
-        send_b[j] = jnp.where(c == 0, second, first).reshape(pairs, half, co)
 
     acc1 = ref["acc1"]
 
@@ -798,24 +812,31 @@
 
     acc1[...] = jnp.zeros_like(acc1)
     lax.fori_loop(0, 2 * per, kernel_one_grad, 0)
-    spare = lanes_one - 9 * cin - 10
-    dots = [total(dot1), total(dot2), total(dot0)]
+    spare = lanes_each - 9 * cin - 6
 
     def pair_of(column):
         high_part = column.astype(BF16).astype(F32)
         return [high_part, column - high_part]
 
+    parts = [acc1[:, tap * TILE : tap * TILE + cin] for tap in range(9)]
+    parts += pair_of(acc1[:, 4 * TILE + cin : 4 * TILE + cin + 1])
+    parts += pair_of(acc0[:, cin : cin + 1])
+    parts += pair_of(jnp.broadcast_to(total(dot1), (cout, 1)))
+    parts.append(jnp.zeros((cout, spare), F32))
+    flat = jnp.concatenate(parts, axis=1).astype(BF16)
     for ch in range(2):
-        rows_at = slice(ch * co, (ch + 1) * co)
-        parts = [acc1[rows_at, tap * TILE : tap * TILE + cin] for tap in range(9)]
-        parts += pair_of(acc1[rows_at, 4 * TILE + cin : 4 * TILE + cin + 1])
-        parts += pair_of(acc0[rows_at, cin : cin + 1])
-        for value in dots:
-            parts += pair_of(jnp.broadcast_to(value, (co, 1)))
-        parts.append(jnp.zeros((co, spare), F32))
-        wire1[ch] = jnp.concatenate(parts, axis=1).astype(BF16)
-    sum1 = sum_mate(wire1, ref["got1"])
-    out_x = begin(send_b, got_b, (me, o))
+        ref["wirec"][ch] = flat[ch * co : (ch + 1) * co]
+    group_c = Summed("c")
+
+    out_b, send_b, got_b = ref["out_b"], ref["send_b"], ref["got_b"]
+
+    def conv_two(j):
+        main = dot(box[j].reshape(own_px, 9 * op), w2[...])
+        skip = dot(xb[j, 1 : pairs + 1].reshape(own_px, TILE), w0[...])
+        value = ((main * scale2 + skip * scale0) * 0.25 + bias2).astype(BF16)
+        first, second = value[:, 0:co], value[:, co:cout]
+        out_b[c * per + j] = jnp.where(c == 0, first, second).reshape(pairs, half, co)
+        send_b[j] = jnp.where(c == 0, second, first).reshape(pairs, half, co)
 
     taps_in, skip_back = ref["taps_in"], ref["skip_back"]
     pixel_in = iota((half, TILE), 0)
@@ -881,14 +902,19 @@
         grad_x[j].wait_recv()
         lax.fori_loop(0, pairs, line, 0, unroll=4)
 
+    for j in range(per):
+        conv_two(j)
+    group_c.to_owners()
+    out_x = begin(send_b, got_b, (me, o))
     back_products(0)
-    far1 = sum_far(sum1, wire1, ref["got1"], ref["shares1"], ref["landing1"], ref["mine1"])
+    group_a.to_cubes()
     grad_x = [input_rows(0)]
-    back2 = gather_far(far2, ref["landing2"], ref["mine2"], ref["result2"])
+    group_b.to_cubes()
     for j in range(1, per):
         back_products(j)
+        if j == 1:
+            group_a.to_all()
         grad_x.append(input_rows(j))
-
     def own_half(row):
         return jnp.where(c == 0, row[:, 0:co], row[:, co:cout])
 
@@ -912,39 +938,46 @@
             some = min(TILE, left.shape[1] - at)
             turned(columns[:, 0:some] * left[:, at : at + some], out, at)
 
-    def flat_of(result):
-        return jnp.concatenate([result[at].astype(F32) for at in range(n_chips)], axis=1)
-
     corr1, corr2, corr0 = ref["corr1"], ref["corr2"], ref["corr0"]
+    group_c.to_cubes()
+    group_b.to_all()
     outer(compact(left1_ref[0:1], cin, TILE), right1 * (scale1 * scale1), corr1)
-    outer(compact(left2_ref[0:1], cout, op), right2 * (scale2 * scale2), corr2)
-    outer(left0_ref[0:1, 0:cin], right0 * (scale0 * scale0), corr0)
-    back1 = gather_far(far1, ref["landing1"], ref["mine1"], ref["result1"])
-    last2 = gather_mate(back2, ref["result2"])
+    outer(compact(left2_ref[0:1], cout, op), right2 * scale2, corr2)
+    outer(left0_ref[0:1, 0:cin], right0 * scale0, corr0)
+    out_k1, out_k2, out_k0 = ref["out_k1"], ref["out_k2"], ref["out_k0"]
+    group_c.to_all()
+    flat = group_a.flat()
+    for at in range(0, 5 * cout, TILE):
+        turned(flat[:, at : min(at + TILE, 5 * cout)] * scale2, out_k2, at)
+    flat = group_b.flat()
+    for at in range(0, 4 * cout, TILE):
+        turned(flat[:, at : min(at + TILE, 4 * cout)] * scale2, out_k2, 5 * cout + at)
+    turned(flat[:, 4 * cout : 4 * cout + cin] * scale0, out_k0, 0)
+
+    dots = ref["dots"]
+    at = iota((8, TILE), 0)
+    sum2 = total(out_k2[...] * k2[0:n2].astype(F32))
+    sum0 = total(out_k0[...] * k10[n1 : n1 + cin].astype(F32))
+    dots[c] = jnp.where(at == 0, sum2, jnp.where(at == 1, sum0, 0.0))
+    dots_x = begin(dots.at[c], dots.at[c], (me, o))
     out_x.wait_recv()
     out_b[mine_o] = got_b[...]
-    unpack(0)
-    last2.wait_recv()
-    flat2 = flat_of(ref["result2"])
-    out_k1, out_k2, out_k0 = ref["out_k1"], ref["out_k2"], ref["out_k0"]
-    for at in range(0, n2, TILE):
-        turned(flat2[:, at : min(at + TILE, n2)] * scale2, out_k2, at)
-    turned(flat2[:, n2 : n2 + cin] * scale0, out_k0, 0)
-    last1 = gather_mate(back1, ref["result1"])
-    for j in range(1, per):
+    for j in range(per):
         unpack(j)
-    last1.wait_recv()
-    flat1 = flat_of(ref["result1"])
-    extra = flat1[:, n1 : n1 + 10]
-    dot_values = [extra[0:1, 4 + 2 * i : 5 + 2 * i] + extra[0:1, 5 + 2 * i : 6 + 2 * i] for i in range(3)]
-    biases = jnp.concatenate([extra, jnp.zeros((co, TILE - 10), F32)], axis=1)
+    dots_x.wait_recv()
+    both = dots[0] + dots[1]
+    for out, corr, row in ((out_k2, corr2, 0), (out_k0, corr0, 1)):
+        out[...] = out[...] - corr[...] * both[row : row + 1, 0:1]
+    flat = group_c.flat()
+    extra = flat[:, n1 : n1 + 6]
+    sum1 = extra[0:1, 4:5] + extra[0:1, 5:6]
+    biases = jnp.concatenate([extra, jnp.zeros((co, TILE - 6), F32)], axis=1)
     biases = jnp.transpose(jnp.concatenate([biases, jnp.zeros((TILE - co, TILE), F32)], axis=0))
     ref["out_b1"][...] = biases[0:1, 0:co] + biases[1:2, 0:co]
     ref["out_b2"][...] = biases[2:3, 0:co] + biases[3:4, 0:co]
     for at in range(0, n1, TILE):
-        turned(flat1[:, at : min(at + TILE, n1)] * scale1, out_k1, at)
-    for out, corr, value in ((out_k1, corr1, 0), (out_k2, corr2, 1), (out_k0, corr0, 2)):
-        out[...] = out[...] - corr[...] * dot_values[value]
+        turned(flat[:, at : min(at + TILE, n1)] * scale1, out_k1, at)
+    out_k1[...] = out_k1[...] - corr1[...] * sum1
 
     for copy in sends:
         copy.wait_send()
@@ -980,9 +1013,9 @@
     op = 2 * TILE
     n_chips = n_rows // 2
     cin, cout = 2 * ci, 2 * co
-    step = TILE * n_chips
-    lanes_two = -(-(9 * cout + cin) // step) * step
-    lanes_one = -(-(9 * cin + 10) // step) * step
+    sub = min(4, n_chips)
+    cubes = n_chips // sub
+    lanes_each = -(-max(9 * cin + 6, 5 * cout, 4 * cout + cin) // (TILE * sub)) * (TILE * sub)
     seg_out = rows // 2 + 1
     bits = 3 if n_rows % 8 == 0 else 2
     share1 = -(-(10 * cin) // 64) * 16
@@ -1051,20 +1084,22 @@
     }
     for name, size in (("corr1", 9 * cin), ("corr2", 9 * cout), ("corr0", cin)):
         scratch[name] = vm((size, co), F32)
-    for name, lanes in (("1", lanes_one), ("2", lanes_two)):
-        share = lanes // n_chips
-        scratch["wire" + name] = vm((2, co, lanes), BF16)
-        scratch["got" + name] = vm((2, co // 2, lanes), BF16)
-        scratch["shares" + name] = vm((2, n_chips, co // 2, share), BF16)
-        scratch["landing" + name] = vm((2 * n_chips - 1, co // 2, share), BF16)
+    share = lanes_each // sub
+    for name in ("a", "b", "c"):
+        scratch["wire" + name] = vm((2, co, lanes_each), BF16)
+        scratch["got" + name] = vm((2, co // 2, lanes_each), BF16)
+        scratch["shares" + name] = vm((2, sub, co // 2, share), BF16)
+        scratch["landing" + name] = vm((2 * sub - 1, co // 2, share), BF16)
         scratch["mine" + name] = vm((co // 2, share), F32)
-        scratch["result" + name] = vm((n_chips, co, share), BF16)
-    copies = 12 + bits + 6 * per + 2 * (1 + 2 * n_chips - 1 + n_chips - 1 + 1)
+        scratch["mids" + name] = vm((cubes, co // 2, share), BF16)
+        scratch["result" + name] = vm((sub, co, share), BF16)
+    scratch["dots"] = vm((2, 8, TILE), F32)
+    copies = 13 + bits + 6 * per + 3 * (1 + 2 * (2 * sub - 1) + cubes - 1)
     scratch["lsem"] = pltpu.SemaphoreType.DMA((5,))
     scratch["ssem"] = pltpu.SemaphoreType.DMA((copies,))
     scratch["rsem"] = pltpu.SemaphoreType.DMA((copies,))
     names = list(inputs) + list(outputs) + list(scratch)
-    dims = (micros, rows, width, ci, co, lanes_two, lanes_one, bits, share1, share2)
+    dims = (micros, rows, width, ci, co, lanes_each, bits, share1, share2)
     smem = pl.BlockSpec(memory_space=pltpu.SMEM)
     vmem = pl.BlockSpec(memory_space=pltpu.VMEM)
     hbm = pl.BlockSpec(memory_space=pltpu.HBM)

time: 56.9 us -> 51.2 us (0.90); the launches traced: 56.2 us -> 51.1 us
  Pallas kernels: 54.8 us -> 49.7 us
    pallas_call x1, Pallas kernels: 53.3 us -> 48.2 us  [fused(): pl.pallas_call(functools.partial(fused_kernel, names, n_rows, dims), out_...]
where the time goes in v3:
time: 51.2 us; the launch traced here: 51.1 us
  Pallas kernels  49.7 us (97%)
  between operations  0.7 us (1%)
  local copies, waits for them, and re-layouts  0.69 us (1%)
    pallas_call x1, Pallas kernels, fused(): pl.pallas_call(functools.partial(fused_kernel, names, n_rows, dims), out_...  48.2 us
    pallas_call x1, Pallas kernels, hand_over(): pl.pallas_call(copy_all, out_shape=[jax.ShapeDtypeStruct(a.shape, a.dtype...  1.47 us

profile of v3, /device:TPU:0, one launch (start us, length us, event | category | flops | bytes accessed | tf_op | source)
XLA Modules:
  0.0 51.1 jit_solution(10150302905024461909)
XLA Ops:
  0.6 0.0 copy-start.5
  0.6 0.0 copy-start.6
  0.7 0.0 copy-start.1
  0.7 0.0 copy-start
  0.7 0.0 copy-start.2
  0.7 0.0 copy-start.3
  0.7 0.0 copy-start.4
  0.7 0.6 %copy-done.5 = f32[96]{0:T(128)S(1)} copy-done((f32[96]{0:T(128)S(1)}, f32[96]{0:T(128)}, u32[]{:S(2)}) %copy-start.5) | copy-done | bytes 408
  1.3 0.0 copy-done.6
  1.3 0.0 copy-done.1
  1.4 0.0 copy-done
  1.4 0.0 copy-done.2
  1.4 0.0 copy-done.3
  1.4 0.0 copy-done.4
  1.4 48.2 %down_block.1 = (bf16[4,8,32,96]{3,2,1,0:T(8,128)(2,1)S(1)}, bf16[4,16,48,64]{3,2,1,0:T(8,128)(2,1)S(1)}, f32[864,96]{1,0:T(8,128)S(1)}, f32[1728,96]{1,0:T(8,12...) custom-call(s32[4,4]{1,0:T(4,128)S(1)} %copy-done, s32[4,4]{1,0:T(4,128)S(1)} %copy-done.1, ...), custom_call_target="tpu_custom_call" | custom-call | tf_op jit(solution)/shard_map/down_block/pallas_call | solution.py:1108
  49.6 1.5 %hand_over.1 = (bf16[4,8,32,96]{3,2,1,0:T(8,128)(2,1)}, bf16[4,16,48,64]{3,2,1,0:T(8,128)(2,1)}, f32[864,96]{1,0:T(8,128)}, f32[1728,96]{1,0:T(8,128)}, f32[96,9...) custom-call(bf16[4,8,32,96]{3,2,1,0:T(8,128)(2,1)S(1)} %get-tuple-element.21.refs_0_, ...), custom_call_target="tpu_custom_call" | custom-call | tf_op jit(solution)/shard_map/hand_over/pallas_call | solution.py:997
Async XLA Ops:
  0.6 0.7 %copy-start.5 = (f32[96]{0:T(128)S(1)}, f32[96]{0:T(128)}, u32[]{:S(2)}) copy-start(f32[96]{0:T(128)} %param.21) | copy-start | bytes 1156
  0.6 0.7 %copy-start.6 = (f32[96]{0:T(128)S(1)}, f32[96]{0:T(128)}, u32[]{:S(2)}) copy-start(f32[96]{0:T(128)} %param.22) | copy-start | bytes 1156
  0.7 0.7 %copy-start.1 = (s32[4,4]{1,0:T(4,128)S(1)}, s32[4,4]{1,0:T(4,128)}, u32[]{:S(2)}) copy-start(s32[4,4]{1,0:T(4,128)} %refs_1_.1) | copy-start | bytes 196
  0.7 0.7 %copy-start = (s32[4,4]{1,0:T(4,128)S(1)}, s32[4,4]{1,0:T(4,128)}, u32[]{:S(2)}) copy-start(s32[4,4]{1,0:T(4,128)} %refs_0_.1) | copy-start | bytes 196
  0.7 0.7 %copy-start.2 = (bf16[96]{0:T(256)(128)(2,1)S(1)}, bf16[96]{0:T(256)(128)(2,1)}, u32[]{:S(2)}) copy-start(bf16[96]{0:T(256)(128)(2,1)} %param.18) | copy-start | bytes 580
  0.7 0.7 %copy-start.3 = (bf16[96]{0:T(256)(128)(2,1)S(1)}, bf16[96]{0:T(256)(128)(2,1)}, u32[]{:S(2)}) copy-start(bf16[96]{0:T(256)(128)(2,1)} %param.19) | copy-start | bytes 580
  0.7 0.7 %copy-start.4 = (f32[96]{0:T(128)S(1)}, f32[96]{0:T(128)}, u32[]{:S(2)}) copy-start(f32[96]{0:T(128)} %param.20) | copy-start | bytes 1156

commit v4 on v3

--- a/solution.py
+++ b/solution.py
@@ -252,8 +252,7 @@
         and 2 * width == TILE
         and in_local % 16 == 0
         and 2 * in_local < TILE
-        and out_local % 32 == 0
-        and TILE < 2 * out_local <= 2 * TILE
+        and out_local == 3 * TILE // 4
     )
 
 
@@ -363,15 +362,15 @@
         sends.append(copy)
         return copy
 
-    img, cot, k10, k2 = ref["img_v"], ref["cot_v"], ref["k10_v"], ref["k2_v"]
+    img, cot, k1, k20 = ref["img_v"], ref["cot_v"], ref["k1_v"], ref["k20_v"]
     n1, n2 = 9 * cin, 9 * cout
     loads = []
     for i, (src, dst) in enumerate(
         [
             (ref["img"], img),
-            (ref["k1"], k10.at[0:n1]),
-            (ref["k0"], k10.at[n1 : n1 + cin]),
-            (ref["k2"], k2.at[0:n2]),
+            (ref["k1"], k1.at[0:n1]),
+            (ref["k0"], k20.at[n2 : n2 + cin]),
+            (ref["k2"], k20.at[0:n2]),
             (ref["cot"], cot),
         ]
     ):
@@ -431,9 +430,27 @@
     for load in loads[1:]:
         load.wait()
 
+    def packed(value):
+        kept, strip = 3 * value.shape[-2] // 4, co // 3
+        last = value[kept:]
+        beside = jnp.concatenate([last[:, k * strip : (k + 1) * strip] for k in range(3)], axis=0)
+        return jnp.concatenate([value[:kept], beside], axis=1)
+
+    def unpacked(value):
+        part = value.shape[0] // 3
+        last = jnp.concatenate([value[k * part : (k + 1) * part, co:] for k in range(3)], axis=1)
+        return jnp.concatenate([value[:, :co], last], axis=0)
+
+    k1p, k20p, cotp = ref["k1p"], ref["k20p"], ref["cotp"]
+    size1, size20 = 3 * k1.shape[0] // 4, 3 * k20.shape[0] // 4
+    k1p[0:size1] = packed(k1[...])
+    k20p[0:size20] = packed(k20[...])
+    for j in range(per):
+        cotp[j] = packed(cot[o * per + j].reshape(own_px, co))
+
     pl.semaphore_wait(barrier, len(near + far + across + around))
 
-    k10h, k2h, cotr = ref["k10h"], ref["k2h"], ref["cotr"]
+    k1h, k20h, coth, cotr = ref["k1h"], ref["k20h"], ref["coth"], ref["cotr"]
     spots = [core] + [lax.rem(me // 2**b, 2) for b in range(1, bits)]
     mates = [mate] + [me + 2**b * (1 - 2 * spots[b]) for b in range(1, bits)]
 
@@ -472,16 +489,15 @@
         )
 
     vec_x = begin(vec.at[c], vec.at[c], (me, o))
-    one = Shared(k10, k10h, share1, 2)
-    send_image(0)
-    two = Shared(k2, k2h, share2, bits)
-    for j in range(1, per):
+    one = Shared(k1p, k1h, share1, 2)
+    two = Shared(k20p, k20h, share2, bits)
+    for j in range(per):
         send_image(j)
-    cot_x = begin(cot.at[mine_o], cotr.at[:, c, pl.ds(1, pairs)], (me, o))
+    cot_x = [begin(cotp.at[j], coth.at[j], (me, o)) for j in range(per)]
     cot_halo = [
-        begin(cot.at[mine_o, 0], cotr.at[:, c, pairs + 1], (up, o)),
+        begin(cot.at[mine_o, 0], cotr.at[:, c, 1], (up, o)),
         begin(cot.at[mine_o, pairs - 1], cotr.at[:, c, 0], (down, o)),
-        begin(cot.at[mine_c, 0], cotr.at[:, c, pairs + 1], (up, c)),
+        begin(cot.at[mine_c, 0], cotr.at[:, c, 1], (up, c)),
         begin(cot.at[mine_c, pairs - 1], cotr.at[:, c, 0], (down, c)),
     ]
 
@@ -616,16 +632,14 @@
         def put(i, own, other):
             first = jnp.where(c == 0, own, other)
             second = jnp.where(c == 0, other, own)
-            line = jnp.concatenate([first, second, jnp.zeros((half, op - cout), BF16)], axis=1)
-            quart[j, i] = (line.astype(F32) * 0.25).astype(BF16)
-
-        def inner(i, carry):
-            put(i + 1, cot[c * per + j, i], cotr[j, o, i + 1])
-            return carry
-
-        lax.fori_loop(0, pairs, inner, 0, unroll=4)
-        for i in (0, pairs + 1):
-            put(i, cotr[j, c, i], cotr[j, o, i])
+            size = first.shape[0]
+            line = jnp.concatenate([first, second, jnp.zeros((size, op - cout), BF16)], axis=1)
+            line = (line.astype(F32) * 0.25).astype(BF16)
+            quart[j, pl.ds(i, size // half)] = line.reshape(size // half, half, op)
+
+        put(1, cot[c * per + j].reshape(own_px, co), unpacked(coth[j]))
+        for i in (0, 1):
+            put(i * (pairs + 1), cotr[j, c, i], cotr[j, o, i])
 
     def owned(j):
         return quart[j, 1 : pairs + 1].reshape(own_px, op)
@@ -689,35 +703,32 @@
             return jnp.concatenate([self.result[at].astype(F32) for at in range(sub)], axis=1)
 
     one.turn()
+    two.turn()
+    one.turn()
     prepare(0)
     one.turn()
-    two.turn()
-    one.turn()
     vec_x.wait_recv()
+    k1o = unpacked(k1h[0:size1])
     for tap in range(9):
         rows_at = slice(tap * cin, (tap + 1) * cin)
-        place(w1, tap * TILE, k10[rows_at], k10h[rows_at], TILE)
-    rows_at = slice(n1, n1 + cin)
-    place(w0, 0, k10[rows_at], k10h[rows_at], TILE)
+        place(w1, tap * TILE, k1[rows_at], k1o[rows_at], TILE)
     left1, right1, sigma1 = power(row_of(0), w1[...])
-    left0, right0, sigma0 = power(row_of(2), w0[...])
-    scale1, scale0 = 1.0 / sigma1, 1.0 / sigma0
+    scale1 = 1.0 / sigma1
     bias1, bias2 = row_of(3), row_of(4)
     left1_ref, left2_ref, left0_ref = ref["left1"], ref["left2"], ref["left0"]
     left1_ref[0:1] = left1
-    left0_ref[0:1] = left0
     conv_one(0)
+    two.turn()
     activate(0)
-    two.turn()
     boxes(0)
     for j in range(1, per):
         prepare(j)
         conv_one(j)
-        if j == 1:
-            two.turn()
         activate(j)
         boxes(j)
-    cot_x.wait_recv()
+    two.turn()
+    for copy in cot_x:
+        copy.wait_recv()
     for copy in cot_halo:
         copy.wait_recv()
     for j in range(per):
@@ -744,11 +755,16 @@
     group_b = Summed("b")
     for turn in range(two.level, bits + 1):
         two.turn()
+    k20o = unpacked(k20h[0:size20])
     for tap in range(9):
         rows_at = slice(tap * cout, (tap + 1) * cout)
-        place(w2, tap * op, k2[rows_at], k2h[rows_at], op)
+        place(w2, tap * op, k20[rows_at], k20o[rows_at], op)
+    rows_at = slice(n2, n2 + cin)
+    place(w0, 0, k20[rows_at], k20o[rows_at], TILE)
     left2, right2, sigma2 = power(row_of(1), w2[...])
-    scale2 = 1.0 / sigma2
+    left0, right0, sigma0 = power(row_of(2), w0[...])
+    scale2, scale0 = 1.0 / sigma2, 1.0 / sigma0
+    left0_ref[0:1] = left0
     left2_ref[0:1] = left2
 
     taps_sum = ref["taps_sum"]
@@ -792,26 +808,30 @@
     for j in range(per):
         dot1 = back_two(j, dot1)
 
-    acc1 = ref["acc1"]
-
-    def kernel_one_grad(step, carry):
-        j, seg = step // 2, lax.rem(step, 2)
+    def kernel_one_grad(taps_u):
         value = None
         for b in range(2):
-            given = g_pre[j, b, pl.ds(seg * cut + 1, cut)].reshape(cut * half, op)[:, 0:cout]
-            taps = [
-                b_in[j, pl.ds(seg * (cut + 2) + 1 + u, cut), :, b * TILE : (b + 3) * TILE].reshape(
-                    cut * half, 3 * TILE
-                )
-                for u in range(3)
-            ]
-            part = dot(given, jnp.concatenate(taps, axis=1), TN)
+            given, lines = [], []
+            for j in range(per):
+                for seg in range(2):
+                    given.append(g_pre[j, b, seg * cut + 1 : (seg + 1) * cut + 1].reshape(cut * half, op)[:, 0:cout])
+                    first = seg * (cut + 2) + 1
+                    lines.append(
+                        jnp.concatenate(
+                            [
+                                b_in[j, first + u : first + u + cut, :, b * TILE : (b + 3) * TILE].reshape(
+                                    cut * half, 3 * TILE
+                                )
+                                for u in taps_u
+                            ],
+                            axis=1,
+                        )
+                    )
+            part = dot(jnp.concatenate(given, axis=0), jnp.concatenate(lines, axis=0), TN)
             value = part if value is None else value + part
-        acc1[...] = acc1[...] + value
-        return carry
-
-    acc1[...] = jnp.zeros_like(acc1)
-    lax.fori_loop(0, 2 * per, kernel_one_grad, 0)
+        return value
+
+    acc1 = kernel_one_grad(range(3))
     spare = lanes_each - 9 * cin - 6
 
     def pair_of(column):
@@ -956,8 +976,8 @@
 
     dots = ref["dots"]
     at = iota((8, TILE), 0)
-    sum2 = total(out_k2[...] * k2[0:n2].astype(F32))
-    sum0 = total(out_k0[...] * k10[n1 : n1 + cin].astype(F32))
+    sum2 = total(out_k2[...] * k20[0:n2].astype(F32))
+    sum0 = total(out_k0[...] * k20[n2 : n2 + cin].astype(F32))
     dots[c] = jnp.where(at == 0, sum2, jnp.where(at == 1, sum0, 0.0))
     dots_x = begin(dots.at[c], dots.at[c], (me, o))
     out_x.wait_recv()
@@ -1018,8 +1038,10 @@
     lanes_each = -(-max(9 * cin + 6, 5 * cout, 4 * cout + cin) // (TILE * sub)) * (TILE * sub)
     seg_out = rows // 2 + 1
     bits = 3 if n_rows % 8 == 0 else 2
-    share1 = -(-(10 * cin) // 64) * 16
-    share2 = -(-(9 * cout) // (16 * 2**bits)) * 16
+    size1 = -(-(9 * cin) // 64) * 64
+    size20 = -(-(9 * cout + cin) // 64) * 64
+    share1 = -(-(3 * size1 // 4) // 64) * 16
+    share2 = -(-(3 * size20 // 4) // (16 * 2**bits)) * 16
     inputs = {
         "vh": valid_h,
         "vw": valid_w,
@@ -1047,14 +1069,18 @@
     scratch = {
         "img_v": vm((micros, rows, ci, width), BF16),
         "cot_v": vm(cotangent.shape, BF16),
-        "k10_v": vm((4 * share1, co), BF16),
-        "k2_v": vm((2**bits * share2, co), BF16),
-        "k10h": vm((4 * share1, co), BF16),
-        "k2h": vm((2**bits * share2, co), BF16),
+        "k1_v": vm((size1, co), BF16),
+        "k20_v": vm((size20, co), BF16),
+        "k1p": vm((4 * share1, TILE), BF16),
+        "k20p": vm((2**bits * share2, TILE), BF16),
+        "k1h": vm((4 * share1, TILE), BF16),
+        "k20h": vm((2**bits * share2, TILE), BF16),
+        "cotp": vm((per, 3 * pairs * half // 4, TILE), BF16),
+        "coth": vm((per, 3 * pairs * half // 4, TILE), BF16),
         "imgr": vm((per, 2, pairs + 2, ci, TILE), BF16),
         "sendp": vm((per, pairs, ci, TILE), BF16),
         "vec": vm((2, 8, TILE), F32),
-        "cotr": vm((per, 2, pairs + 2, half, co), BF16),
+        "cotr": vm((per, 2, 2, half, co), BF16),
         "perm_in": vm((8 * half, TILE), BF16),
         "perm_x": vm((5 * half, TILE), BF16),
         "w1": vm((9 * TILE, op), BF16),
@@ -1072,7 +1098,6 @@
         "box": vm((per, pairs, half, 9 * op), BF16),
         "quart": vm((per, pairs + 2, half, op), BF16),
         "acc0": vm((cout, TILE), F32),
-        "acc1": vm((cout, 9 * TILE), F32),
         "taps_sum": vm((3, 2, pairs + 2, half, op), F32),
         "g_pre": vm((per, 2, 2 * seg_out, half, op), BF16),
         "taps_in": vm((2, 2 * seg_out, half, 9 * TILE), F32),
@@ -1094,7 +1119,7 @@
         scratch["mids" + name] = vm((cubes, co // 2, share), BF16)
         scratch["result" + name] = vm((sub, co, share), BF16)
     scratch["dots"] = vm((2, 8, TILE), F32)
-    copies = 13 + bits + 6 * per + 3 * (1 + 2 * (2 * sub - 1) + cubes - 1)
+    copies = 12 + bits + 7 * per + 3 * (1 + 2 * (2 * sub - 1) + cubes - 1)
     scratch["lsem"] = pltpu.SemaphoreType.DMA((5,))
     scratch["ssem"] = pltpu.SemaphoreType.DMA((copies,))
     scratch["rsem"] = pltpu.SemaphoreType.DMA((copies,))

time: 51.2 us -> 47.6 us (0.930)
  Pallas kernels: 49.7 us -> 45.9 us
    pallas_call x1, Pallas kernels: 48.2 us -> 44.4 us  [fused(): pl.pallas_call(functools.partial(fused_kernel, names, n_rows, dims), out_...]
where the time goes in v4:
time: 47.6 us; the launch traced here: 47.5 us
  Pallas kernels  45.9 us (96%)
  between operations  0.86 us (2%)
  local copies, waits for them, and re-layouts  0.69 us (1%)
    pallas_call x1, Pallas kernels, fused(): pl.pallas_call(functools.partial(fused_kernel, names, n_rows, dims), out_...  44.4 us
    pallas_call x1, Pallas kernels, hand_over(): pl.pallas_call(copy_all, out_shape=[jax.ShapeDtypeStruct(a.shape, a.dtype...  1.47 us

profile of v4, /device:TPU:0, one launch (start us, length us, event | category | flops | bytes accessed | tf_op | source)
XLA Modules:
  0.0 47.5 jit_solution(13479909687945978728)
XLA Ops:
  0.6 0.0 copy-start.5
  0.6 0.0 copy-start.6
  0.7 0.0 copy-start.1
  0.7 0.0 copy-start
  0.7 0.0 copy-start.2
  0.7 0.0 copy-start.3
  0.7 0.0 copy-start.4
  0.7 0.6 %copy-done.5 = f32[96]{0:T(128)S(1)} copy-done((f32[96]{0:T(128)S(1)}, f32[96]{0:T(128)}, u32[]{:S(2)}) %copy-start.5) | copy-done | bytes 408
  1.3 0.0 copy-done.6
  1.3 0.0 copy-done.1
  1.4 0.0 copy-done
  1.4 0.0 copy-done.2
  1.4 0.0 copy-done.3
  1.4 0.0 copy-done.4
  1.4 44.4 %down_block.1 = (bf16[4,8,32,96]{3,2,1,0:T(8,128)(2,1)S(1)}, bf16[4,16,48,64]{3,2,1,0:T(8,128)(2,1)S(1)}, f32[864,96]{1,0:T(8,128)S(1)}, f32[1728,96]{1,0:T(8,12...) custom-call(s32[4,4]{1,0:T(4,128)S(1)} %copy-done, s32[4,4]{1,0:T(4,128)S(1)} %copy-done.1, ...), custom_call_target="tpu_custom_call" | custom-call | tf_op jit(solution)/shard_map/down_block/pallas_call | solution.py:1133
  45.8 1.5 %hand_over.1 = (bf16[4,8,32,96]{3,2,1,0:T(8,128)(2,1)}, bf16[4,16,48,64]{3,2,1,0:T(8,128)(2,1)}, f32[864,96]{1,0:T(8,128)}, f32[1728,96]{1,0:T(8,128)}, f32[96,9...) custom-call(bf16[4,8,32,96]{3,2,1,0:T(8,128)(2,1)S(1)} %get-tuple-element.21.refs_0_, ...), custom_call_target="tpu_custom_call" | custom-call | tf_op jit(solution)/shard_map/hand_over/pallas_call | solution.py:1017
Async XLA Ops:
  0.6 0.7 %copy-start.5 = (f32[96]{0:T(128)S(1)}, f32[96]{0:T(128)}, u32[]{:S(2)}) copy-start(f32[96]{0:T(128)} %param.21) | copy-start | bytes 1156
  0.6 0.7 %copy-start.6 = (f32[96]{0:T(128)S(1)}, f32[96]{0:T(128)}, u32[]{:S(2)}) copy-start(f32[96]{0:T(128)} %param.22) | copy-start | bytes 1156
  0.7 0.7 %copy-start.1 = (s32[4,4]{1,0:T(4,128)S(1)}, s32[4,4]{1,0:T(4,128)}, u32[]{:S(2)}) copy-start(s32[4,4]{1,0:T(4,128)} %refs_1_.1) | copy-start | bytes 196
  0.7 0.7 %copy-start = (s32[4,4]{1,0:T(4,128)S(1)}, s32[4,4]{1,0:T(4,128)}, u32[]{:S(2)}) copy-start(s32[4,4]{1,0:T(4,128)} %refs_0_.1) | copy-start | bytes 196
  0.7 0.7 %copy-start.2 = (bf16[96]{0:T(256)(128)(2,1)S(1)}, bf16[96]{0:T(256)(128)(2,1)}, u32[]{:S(2)}) copy-start(bf16[96]{0:T(256)(128)(2,1)} %param.18) | copy-start | bytes 580
  0.7 0.7 %copy-start.3 = (bf16[96]{0:T(256)(128)(2,1)S(1)}, bf16[96]{0:T(256)(128)(2,1)}, u32[]{:S(2)}) copy-start(bf16[96]{0:T(256)(128)(2,1)} %param.19) | copy-start | bytes 580
  0.7 0.7 %copy-start.4 = (f32[96]{0:T(128)S(1)}, f32[96]{0:T(128)}, u32[]{:S(2)}) copy-start(f32[96]{0:T(128)} %param.20) | copy-start | bytes 1156

commit v5 on v4

--- a/solution.py
+++ b/solution.py
@@ -294,7 +294,7 @@
 
 
 def fused_kernel(names, n_rows, dims, *refs):
-    micros, rows, width, ci, co, lanes_each, bits, share1, share2 = dims
+    micros, rows, width, ci, co, lanes_one, lanes_two, bits, share1, share2 = dims
     ref = dict(zip(names, refs))
     half = width // 2
     per = micros // 2
@@ -372,6 +372,13 @@
             (ref["k0"], k20.at[n2 : n2 + cin]),
             (ref["k2"], k20.at[0:n2]),
             (ref["cot"], cot),
+            (ref["vh"], ref["vh_s"]),
+            (ref["vw"], ref["vw_s"]),
+            (ref["b1"], ref["b1_v"]),
+            (ref["b2"], ref["b2_v"]),
+            (ref["q1"], ref["q1_v"]),
+            (ref["q2"], ref["q2_v"]),
+            (ref["q0"], ref["q0_v"]),
         ]
     ):
         load = pltpu.make_async_copy(src, dst, lsem.at[i])
@@ -392,6 +399,10 @@
     at, lane = iota(shape, 0), iota(shape, 1)
     perm_x[4 * half : 5 * half] = jnp.where(lax.rem(lane, width) // 2 == at, 1.0, 0.0).astype(BF16)
 
+    eye = ref["eye"]
+    shape = (op, op)
+    eye[...] = jnp.where(iota(shape, 0) == iota(shape, 1), 1.0, 0.0).astype(BF16)
+
     def rem_pos(value, by):
         return lax.rem(lax.rem(value, by) + by, by)
 
@@ -400,17 +411,8 @@
     base = [lax.rem(first_a, IMG), lax.rem(first_b, IMG) - cut]
     image_a, image_b = first_a // IMG, first_b // IMG
     keep = jnp.where(base[1] < 0, 0.0, 1.0).astype(F32)
-    vh, vw = ref["vh"], ref["vw"]
-    high = [[vh[c * per + j, image] for image in (image_a, image_b)] for j in range(per)]
-    wide = [[vw[c * per + j, image] for image in (image_a, image_b)] for j in range(per)]
-
     def choose(seg, two):
         return jnp.where(seg == 0, two[0], two[1])
-
-    vec = ref["vec"]
-    vec[c] = jnp.zeros(vec.shape[1:], F32)
-    for i, name in enumerate(("q1", "q2", "q0", "b1", "b2")):
-        vec[c, i : i + 1, 0:co] = ref[name][...].astype(F32)
 
     imgr, sendp = ref["imgr"], ref["sendp"]
     loads[0].wait()
@@ -429,6 +431,14 @@
             lax.fori_loop(0, pairs, pack, 0, unroll=4)
     for load in loads[1:]:
         load.wait()
+    vh, vw = ref["vh_s"], ref["vw_s"]
+    high = [[vh[c * per + j, image] for image in (image_a, image_b)] for j in range(per)]
+    wide = [[vw[c * per + j, image] for image in (image_a, image_b)] for j in range(per)]
+
+    vec = ref["vec"]
+    vec[c] = jnp.zeros(vec.shape[1:], F32)
+    for i, name in enumerate(("q1", "q2", "q0", "b1", "b2")):
+        vec[c, i : i + 1, 0:co] = ref[name + "_v"][...].astype(F32)
 
     def packed(value):
         kept, strip = 3 * value.shape[-2] // 4, co // 3
@@ -452,26 +462,35 @@
 
     k1h, k20h, coth, cotr = ref["k1h"], ref["k20h"], ref["coth"], ref["cotr"]
     spots = [core] + [lax.rem(me // 2**b, 2) for b in range(1, bits)]
-    mates = [mate] + [me + 2**b * (1 - 2 * spots[b]) for b in range(1, bits)]
-
-    def piece(rows_each, level, depth):
+
+    def part_of(rows_each, depth, bits_at):
         first = 0
-        for b in range(depth - level):
-            first = first * 2 + spots[b]
-        return pl.ds(first * (2**level * rows_each), 2**level * rows_each)
+        for b in range(depth):
+            first = first * 2 + bits_at[b]
+        return pl.ds(first * rows_each, rows_each)
 
     class Shared:
         def __init__(self, own, got, rows_each, depth):
             self.got, self.rows_each, self.depth, self.level = got, rows_each, depth, 0
-            at = piece(rows_each, 0, depth)
-            self.copy = begin(own.at[at], got.at[at], (me, o))
+            at = part_of(rows_each, depth, spots)
+            self.copies = [begin(own.at[at], got.at[at], (me, o))]
 
         def turn(self):
-            self.copy.wait_recv()
-            if self.level < self.depth:
-                at = piece(self.rows_each, self.level, self.depth)
-                device = (mates[self.depth - 1 - self.level], c)
-                self.copy = begin(self.got.at[at], self.got.at[at], device)
+            for copy in self.copies:
+                copy.wait_recv()
+            self.copies = []
+            if self.level == 0:
+                at = self.got.at[part_of(self.rows_each, self.depth, spots)]
+                for mask in range(1, 2 ** (self.depth - 1)):
+                    other = me
+                    for b in range(1, self.depth):
+                        if mask >> (b - 1) & 1:
+                            other = other + 2**b * (1 - 2 * spots[b])
+                    self.copies.append(begin(at, at, (other, c)))
+            if self.level == 1:
+                size = 2 ** (self.depth - 1) * self.rows_each
+                at = self.got.at[pl.ds(core * size, size)]
+                self.copies.append(begin(at, at, (mate, c)))
             self.level += 1
 
     mine_c, mine_o = pl.ds(c * per, per), pl.ds(o * per, per)
@@ -559,27 +578,24 @@
         b_in[j, seg_slots - 1] = (b_in[j, seg_slots + 1].astype(F32) * keep).astype(BF16)
         b_in[j, seg_slots] = (b_in[j, seg_slots - 2].astype(F32) * keep).astype(BF16)
 
-    raw1, grad1 = ref["raw1"], ref["grad1"]
+    raw1, grad1, act1 = ref["raw1"], ref["grad1"], ref["act1"]
 
     def conv_one(j):
-        def segment(seg, carry):
-            parts = []
+        parts = []
+        for seg in range(2):
             for b in range(2):
+                first = seg * seg_slots
                 taps = [
-                    b_in[j, pl.ds(seg * seg_slots + u, seg_out), :, b * TILE : (b + 3) * TILE].reshape(
+                    b_in[j, first + u : first + u + seg_out, :, b * TILE : (b + 3) * TILE].reshape(
                         seg_out * half, 3 * TILE
                     )
                     for u in range(3)
                 ]
                 parts.append(jnp.concatenate(taps, axis=1))
-            result = dot(jnp.concatenate(parts, axis=0), w1[...])
+        result = dot(jnp.concatenate(parts, axis=0), w1[...]).reshape(2, 2, seg_out, half, op)
+        for seg in range(2):
             for b in range(2):
-                raw1[j, b, pl.ds(seg * seg_out, seg_out)] = result[
-                    b * seg_out * half : (b + 1) * seg_out * half
-                ].reshape(seg_out, half, op)
-            return carry
-
-        lax.fori_loop(0, 2, segment, 0)
+                raw1[j, b, seg * seg_out : (seg + 1) * seg_out] = result[seg, b]
 
     cols = ref["cols"]
     pixel = iota((half, op), 0)
@@ -595,7 +611,9 @@
                 mask = 2 * pixel + b < broad
                 lift = pre * gate
                 grad1[j, b, i] = jnp.where(mask, gate + lift * (1.0 - gate), 0.0)
-                acts.append(jnp.where(mask, lift, 0.0).astype(BF16).astype(F32))
+                act = jnp.where(mask, lift, 0.0).astype(BF16)
+                act1[j, b, i] = act
+                acts.append(act.astype(F32))
             even, odd = acts
             before = jnp.where(pixel == 0, 0.0, pltpu.roll(odd, 1, 0))
             after = jnp.where(pixel == half - 1, 0.0, pltpu.roll(even, half - 1, 0))
@@ -665,13 +683,9 @@
             for ch in range(2):
                 value = self.wire[ch, kept_rows].astype(F32) + self.got[ch].astype(F32)
                 for at in range(sub):
-                    part = value[:, at * self.share : (at + 1) * self.share]
-                    self.shares[ch, at] = part.astype(BF16)
-
-                    @pl.when(my_id == ch * sub + at)
-                    def _():
-                        self.mine[...] = part
-
+                    self.shares[ch, at] = value[:, at * self.share : (at + 1) * self.share].astype(BF16)
+            lanes = pl.ds(pl.multiple_of(spot_in * self.share, TILE), self.share)
+            self.mine[...] = self.wire[c, kept_rows, lanes].astype(F32) + self.got[c, :, lanes].astype(F32)
             self.copies = []
             for delta in range(1, 2 * sub):
                 other = lax.rem(my_id + delta, 2 * sub)
@@ -698,9 +712,16 @@
             place_at = self.result.at[spot_in, kept_rows]
             self.copies = [begin(place_at, place_at, device) for device in around]
 
-        def flat(self):
+        def turned(self, scale, out, first, size):
             self.arrived()
-            return jnp.concatenate([self.result[at].astype(F32) for at in range(sub)], axis=1)
+            for at in range(0, sub * self.share, op):
+                piece, lanes = at // self.share, at % self.share
+                value = dot(eye[...], self.result[piece, :, lanes : lanes + op], NT)
+                some = min(op, size - at)
+                if some > 0:
+                    out[first + at : first + at + some] = value[0:some] * scale
+                if some < op:
+                    return value[some:]
 
     one.turn()
     two.turn()
@@ -718,15 +739,14 @@
     left1_ref, left2_ref, left0_ref = ref["left1"], ref["left2"], ref["left0"]
     left1_ref[0:1] = left1
     conv_one(0)
+    activate(0)
     two.turn()
-    activate(0)
     boxes(0)
     for j in range(1, per):
         prepare(j)
         conv_one(j)
         activate(j)
         boxes(j)
-    two.turn()
     for copy in cot_x:
         copy.wait_recv()
     for copy in cot_halo:
@@ -737,6 +757,7 @@
     acc0 = ref["acc0"]
     given = jnp.concatenate([owned(j) for j in range(per)], axis=0)[:, 0:cout]
     turned_quart = jnp.transpose(given)
+    sums0 = ref["sums0"]
     group_a = None
     for name, taps in (("a", range(0, 5)), ("b", range(5, 9))):
         lanes = slice(taps[0] * op, (taps[-1] + 1) * op)
@@ -745,16 +766,16 @@
         if name == "b":
             skip = dot(turned_quart, xb[:, 1 : pairs + 1].reshape(per * own_px, TILE))
             acc0[...] = skip
+            sums0[...] = skip.astype(BF16)
             parts.append(skip[:, 0:cin])
-        parts.append(jnp.zeros((cout, lanes_each - sum(part.shape[1] for part in parts)), F32))
+        parts.append(jnp.zeros((cout, lanes_two - sum(part.shape[1] for part in parts)), F32))
         flat = jnp.concatenate(parts, axis=1).astype(BF16)
         for ch in range(2):
             ref["wire" + name][ch] = flat[ch * co : (ch + 1) * co]
         if name == "a":
             group_a = Summed("a")
     group_b = Summed("b")
-    for turn in range(two.level, bits + 1):
-        two.turn()
+    two.turn()
     k20o = unpacked(k20h[0:size20])
     for tap in range(9):
         rows_at = slice(tap * cout, (tap + 1) * cout)
@@ -768,85 +789,110 @@
     left2_ref[0:1] = left2
 
     taps_sum = ref["taps_sum"]
-    spot = iota((all_px, op), 0)
+    spot = iota((per * all_px, op), 0)
     at_left = lax.rem(spot, half) == 0
     at_right = lax.rem(spot, half) == half - 1
     g_pre = ref["g_pre"]
 
-    def back_two(j, dot1):
-        given = quart[j].reshape(all_px, op)
+    def back_taps():
+        given = quart[...].reshape(per * all_px, op)
         for u in range(3):
             t0, t1, t2 = [
                 dot(given, w2[(3 * u + w) * op : (3 * u + w + 1) * op], NT) for w in range(3)
             ]
             even = t0 + t1 + jnp.where(at_left, 0.0, pltpu.roll(t2, 1, 0))
-            odd = t1 + t2 + jnp.where(at_right, 0.0, pltpu.roll(t0, all_px - 1, 0))
-            taps_sum[u, 0] = even.reshape(pairs + 2, half, op)
-            taps_sum[u, 1] = odd.reshape(pairs + 2, half, op)
-
+            odd = t1 + t2 + jnp.where(at_right, 0.0, pltpu.roll(t0, per * all_px - 1, 0))
+            taps_sum[u, 0] = even.reshape(per, pairs + 2, half, op)
+            taps_sum[u, 1] = odd.reshape(per, pairs + 2, half, op)
+
+    def back_two(j, dots):
         def line(i, carry):
             hold = jnp.where(i == cut // 2, keep, 1.0)
             own_even = jnp.where(i < pairs, 1.0, 0.0)
             own_odd = jnp.where(i > 0, 1.0, 0.0)
+            one, two = carry
             for b in range(2):
-                upper, lower = taps_sum[2, b, i], taps_sum[0, b, i + 1]
-                even = lower + taps_sum[1, b, i + 1] + hold * upper
-                odd = taps_sum[1, b, i] + upper + hold * lower
+                upper, lower = taps_sum[2, b, j, i], taps_sum[0, b, j, i + 1]
+                even = lower + taps_sum[1, b, j, i + 1] + hold * upper
+                odd = taps_sum[1, b, j, i] + upper + hold * lower
+                two = two + own_even * even * act1[j, b, 2 * i + 1].astype(F32)
+                two = two + own_odd * odd * act1[j, b, 2 * i].astype(F32)
                 even = (even * scale2 * grad1[j, b, 2 * i + 1]).astype(BF16)
                 odd = (odd * scale2 * grad1[j, b, 2 * i]).astype(BF16)
                 g_pre[j, b, 2 * i + 1] = even
                 g_pre[j, b, 2 * i] = odd
-                carry = carry + own_even * even.astype(F32) * raw1[j, b, 2 * i + 1]
-                carry = carry + own_odd * odd.astype(F32) * raw1[j, b, 2 * i]
-            return carry
-
-        return lax.fori_loop(0, pairs + 1, line, dot1, unroll=3)
-
+                one = one + own_even * even.astype(F32) * raw1[j, b, 2 * i + 1]
+                one = one + own_odd * odd.astype(F32) * raw1[j, b, 2 * i]
+            return one, two
+
+        return lax.fori_loop(0, pairs + 1, line, dots, unroll=3)
+
+    back_taps()
     group_a.to_owners()
+    dots = (jnp.zeros((half, op), F32), jnp.zeros((half, op), F32))
+    dots = back_two(0, dots)
     group_b.to_owners()
-    dot1 = jnp.zeros((half, op), F32)
-    for j in range(per):
-        dot1 = back_two(j, dot1)
-
-    def kernel_one_grad(taps_u):
+    for j in range(1, per):
+        dots = back_two(j, dots)
+    dot1, dot2 = dots
+
+    turned_grad = []
+    for b in range(2):
+        lines = [g_pre[j, b, 1 : rows + 1].reshape(rows * half, op) for j in range(per)]
+        turned_grad.append(jnp.concatenate(lines, axis=0)[:, 0:cout])
+
+    def kernel_one_grad(taps):
         value = None
         for b in range(2):
-            given, lines = [], []
+            lines = []
             for j in range(per):
                 for seg in range(2):
-                    given.append(g_pre[j, b, seg * cut + 1 : (seg + 1) * cut + 1].reshape(cut * half, op)[:, 0:cout])
                     first = seg * (cut + 2) + 1
-                    lines.append(
-                        jnp.concatenate(
-                            [
-                                b_in[j, first + u : first + u + cut, :, b * TILE : (b + 3) * TILE].reshape(
-                                    cut * half, 3 * TILE
-                                )
-                                for u in taps_u
-                            ],
-                            axis=1,
-                        )
-                    )
-            part = dot(jnp.concatenate(given, axis=0), jnp.concatenate(lines, axis=0), TN)
+                    blocks = []
+                    for u in range(3):
+                        cols_at = [w for w in range(3) if 3 * u + w in taps]
+                        if cols_at:
+                            block = b_in[
+                                j,
+                                first + u : first + u + cut,
+                                :,
+                                (b + cols_at[0]) * TILE : (b + cols_at[-1] + 1) * TILE,
+                            ]
+                            blocks.append(block.reshape(cut * half, len(cols_at) * TILE))
+                    lines.append(jnp.concatenate(blocks, axis=1))
+            part = dot(turned_grad[b], jnp.concatenate(lines, axis=0), TN)
             value = part if value is None else value + part
         return value
-
-    acc1 = kernel_one_grad(range(3))
-    spare = lanes_each - 9 * cin - 6
 
     def pair_of(column):
         high_part = column.astype(BF16).astype(F32)
         return [high_part, column - high_part]
 
-    parts = [acc1[:, tap * TILE : tap * TILE + cin] for tap in range(9)]
-    parts += pair_of(acc1[:, 4 * TILE + cin : 4 * TILE + cin + 1])
-    parts += pair_of(acc0[:, cin : cin + 1])
-    parts += pair_of(jnp.broadcast_to(total(dot1), (cout, 1)))
-    parts.append(jnp.zeros((cout, spare), F32))
-    flat = jnp.concatenate(parts, axis=1).astype(BF16)
-    for ch in range(2):
-        ref["wirec"][ch] = flat[ch * co : (ch + 1) * co]
-    group_c = Summed("c")
+    def trace_of(partial, kernel):
+        product = dot(partial, kernel)
+        eye = iota(product.shape, 0) == iota(product.shape, 1)
+        return total(jnp.where(eye, product, 0.0))
+
+    def send_one(name, taps, extras):
+        value = kernel_one_grad(taps)
+        parts = [value[:, k * TILE : k * TILE + cin] for k in range(len(taps))]
+        rest = extras(value)
+        spare = lanes_one - len(taps) * cin - len(rest)
+        parts.append(jnp.concatenate(rest + [jnp.zeros((cout, spare), F32)], axis=1))
+        flat = jnp.concatenate(parts, axis=1).astype(BF16)
+        for ch in range(2):
+            ref["wire" + name][ch] = flat[ch * co : (ch + 1) * co]
+        return Summed(name)
+
+    def extras_c(value):
+        at = 4 * TILE + cin
+        return pair_of(value[:, at : at + 1]) + pair_of(acc0[:, cin : cin + 1])
+
+    def extras_d(value):
+        sums_at = [total(dot1), total(dot2), trace_of(sums0[...], w0[...])]
+        return [part for at in sums_at for part in pair_of(jnp.broadcast_to(at, (cout, 1)))]
+
+    group_c = send_one("c", range(0, 9), lambda value: extras_c(value) + extras_d(value))
 
     out_b, send_b, got_b = ref["out_b"], ref["send_b"], ref["got_b"]
 
@@ -865,15 +911,8 @@
     def back_products(j):
         skip_back[...] = (dot(owned(j), w0[...], NT) * scale0).reshape(pairs, half, TILE)
 
-        def some(step, carry):
-            b, part = step // 2, lax.rem(step, 2)
-            given = g_pre[j, b, pl.ds(part * seg_out, seg_out)].reshape(seg_out * half, op)
-            taps_in[b, pl.ds(part * seg_out, seg_out)] = dot(given, w1[...], NT).reshape(
-                seg_out, half, 9 * TILE
-            )
-            return carry
-
-        lax.fori_loop(0, 4, some, 0)
+        given = g_pre[j].reshape(4 * seg_out * half, op)
+        taps_in[...] = dot(given, w1[...], NT).reshape(2, 2 * seg_out, half, 9 * TILE)
 
     def input_rows(j):
         def two_rows(p, carry):
@@ -922,7 +961,8 @@
         grad_x[j].wait_recv()
         lax.fori_loop(0, pairs, line, 0, unroll=4)
 
-    for j in range(per):
+    conv_two(0)
+    for j in range(1, per):
         conv_two(j)
     group_c.to_owners()
     out_x = begin(send_b, got_b, (me, o))
@@ -933,8 +973,10 @@
     for j in range(1, per):
         back_products(j)
         if j == 1:
+            group_c.to_cubes()
             group_a.to_all()
         grad_x.append(input_rows(j))
+
     def own_half(row):
         return jnp.where(c == 0, row[:, 0:co], row[:, co:cout])
 
@@ -959,45 +1001,26 @@
             turned(columns[:, 0:some] * left[:, at : at + some], out, at)
 
     corr1, corr2, corr0 = ref["corr1"], ref["corr2"], ref["corr0"]
-    group_c.to_cubes()
     group_b.to_all()
     outer(compact(left1_ref[0:1], cin, TILE), right1 * (scale1 * scale1), corr1)
-    outer(compact(left2_ref[0:1], cout, op), right2 * scale2, corr2)
-    outer(left0_ref[0:1, 0:cin], right0 * scale0, corr0)
+    outer(compact(left2_ref[0:1], cout, op), right2 * (scale2 * scale2), corr2)
+    outer(left0_ref[0:1, 0:cin], right0 * (scale0 * scale0), corr0)
     out_k1, out_k2, out_k0 = ref["out_k1"], ref["out_k2"], ref["out_k0"]
     group_c.to_all()
-    flat = group_a.flat()
-    for at in range(0, 5 * cout, TILE):
-        turned(flat[:, at : min(at + TILE, 5 * cout)] * scale2, out_k2, at)
-    flat = group_b.flat()
-    for at in range(0, 4 * cout, TILE):
-        turned(flat[:, at : min(at + TILE, 4 * cout)] * scale2, out_k2, 5 * cout + at)
-    turned(flat[:, 4 * cout : 4 * cout + cin] * scale0, out_k0, 0)
-
-    dots = ref["dots"]
-    at = iota((8, TILE), 0)
-    sum2 = total(out_k2[...] * k20[0:n2].astype(F32))
-    sum0 = total(out_k0[...] * k20[n2 : n2 + cin].astype(F32))
-    dots[c] = jnp.where(at == 0, sum2, jnp.where(at == 1, sum0, 0.0))
-    dots_x = begin(dots.at[c], dots.at[c], (me, o))
+    group_a.turned(scale2, out_k2, 0, 5 * cout)
     out_x.wait_recv()
     out_b[mine_o] = got_b[...]
-    for j in range(per):
+    unpack(0)
+    rest = group_b.turned(scale2, out_k2, 5 * cout, 4 * cout)
+    out_k0[...] = rest[0:cin] * scale0
+    for j in range(1, per):
         unpack(j)
-    dots_x.wait_recv()
-    both = dots[0] + dots[1]
-    for out, corr, row in ((out_k2, corr2, 0), (out_k0, corr0, 1)):
-        out[...] = out[...] - corr[...] * both[row : row + 1, 0:1]
-    flat = group_c.flat()
-    extra = flat[:, n1 : n1 + 6]
-    sum1 = extra[0:1, 4:5] + extra[0:1, 5:6]
-    biases = jnp.concatenate([extra, jnp.zeros((co, TILE - 6), F32)], axis=1)
-    biases = jnp.transpose(jnp.concatenate([biases, jnp.zeros((TILE - co, TILE), F32)], axis=0))
-    ref["out_b1"][...] = biases[0:1, 0:co] + biases[1:2, 0:co]
-    ref["out_b2"][...] = biases[2:3, 0:co] + biases[3:4, 0:co]
-    for at in range(0, n1, TILE):
-        turned(flat[:, at : min(at + TILE, n1)] * scale1, out_k1, at)
-    out_k1[...] = out_k1[...] - corr1[...] * sum1
+    extra = group_c.turned(scale1, out_k1, 0, n1)
+    ref["out_b1"][...] = extra[0:1] + extra[1:2]
+    ref["out_b2"][...] = extra[2:3] + extra[3:4]
+    for at, (out, corr) in enumerate(((out_k1, corr1), (out_k2, corr2), (out_k0, corr0))):
+        value = extra[4 + 2 * at : 5 + 2 * at, 0:1] + extra[5 + 2 * at : 6 + 2 * at, 0:1]
+        out[...] = out[...] - corr[...] * value
 
     for copy in sends:
         copy.wait_send()
@@ -1035,7 +1058,9 @@
     cin, cout = 2 * ci, 2 * co
     sub = min(4, n_chips)
     cubes = n_chips // sub
-    lanes_each = -(-max(9 * cin + 6, 5 * cout, 4 * cout + cin) // (TILE * sub)) * (TILE * sub)
+    unit = op * sub
+    lanes_two = -(-max(5 * cout, 4 * cout + cin) // unit) * unit
+    lanes_one = -(-(9 * cin + 10) // unit) * unit
     seg_out = rows // 2 + 1
     bits = 3 if n_rows % 8 == 0 else 2
     size1 = -(-(9 * cin) // 64) * 64
@@ -1067,6 +1092,13 @@
     }
     vm = pltpu.VMEM
     scratch = {
+        "vh_s": pltpu.SMEM(valid_h.shape, jnp.int32),
+        "vw_s": pltpu.SMEM(valid_w.shape, jnp.int32),
+        "b1_v": vm((1, co), BF16),
+        "b2_v": vm((1, co), BF16),
+        "q1_v": vm((1, co), F32),
+        "q2_v": vm((1, co), F32),
+        "q0_v": vm((1, co), F32),
         "img_v": vm((micros, rows, ci, width), BF16),
         "cot_v": vm(cotangent.shape, BF16),
         "k1_v": vm((size1, co), BF16),
@@ -1081,6 +1113,7 @@
         "sendp": vm((per, pairs, ci, TILE), BF16),
         "vec": vm((2, 8, TILE), F32),
         "cotr": vm((per, 2, 2, half, co), BF16),
+        "eye": vm((op, op), BF16),
         "perm_in": vm((8 * half, TILE), BF16),
         "perm_x": vm((5 * half, TILE), BF16),
         "w1": vm((9 * TILE, op), BF16),
@@ -1094,11 +1127,13 @@
         "xb": vm((per, pairs + 2, half, TILE), BF16),
         "raw1": vm((per, 2, 2 * seg_out, half, op), F32),
         "grad1": vm((per, 2, 2 * seg_out, half, op), F32),
+        "act1": vm((per, 2, 2 * seg_out, half, op), BF16),
         "cols": vm((per, 3, 2 * seg_out, half, op), F32),
         "box": vm((per, pairs, half, 9 * op), BF16),
         "quart": vm((per, pairs + 2, half, op), BF16),
         "acc0": vm((cout, TILE), F32),
-        "taps_sum": vm((3, 2, pairs + 2, half, op), F32),
+        "sums0": vm((cout, TILE), BF16),
+        "taps_sum": vm((3, 2, per, pairs + 2, half, op), F32),
         "g_pre": vm((per, 2, 2 * seg_out, half, op), BF16),
         "taps_in": vm((2, 2 * seg_out, half, 9 * TILE), F32),
         "skip_back": vm((pairs, half, TILE), F32),
@@ -1109,8 +1144,8 @@
     }
     for name, size in (("corr1", 9 * cin), ("corr2", 9 * cout), ("corr0", cin)):
         scratch[name] = vm((size, co), F32)
-    share = lanes_each // sub
-    for name in ("a", "b", "c"):
+    for name, lanes_each in (("a", lanes_two), ("b", lanes_two), ("c", lanes_one)):
+        share = lanes_each // sub
         scratch["wire" + name] = vm((2, co, lanes_each), BF16)
         scratch["got" + name] = vm((2, co // 2, lanes_each), BF16)
         scratch["shares" + name] = vm((2, sub, co // 2, share), BF16)
@@ -1118,29 +1153,25 @@
         scratch["mine" + name] = vm((co // 2, share), F32)
         scratch["mids" + name] = vm((cubes, co // 2, share), BF16)
         scratch["result" + name] = vm((sub, co, share), BF16)
-    scratch["dots"] = vm((2, 8, TILE), F32)
-    copies = 12 + bits + 7 * per + 3 * (1 + 2 * (2 * sub - 1) + cubes - 1)
-    scratch["lsem"] = pltpu.SemaphoreType.DMA((5,))
+    copies = 11 + 2 ** (bits - 1) + 7 * per + 3 * (1 + 2 * (2 * sub - 1) + cubes - 1)
+    scratch["lsem"] = pltpu.SemaphoreType.DMA((12,))
     scratch["ssem"] = pltpu.SemaphoreType.DMA((copies,))
     scratch["rsem"] = pltpu.SemaphoreType.DMA((copies,))
     names = list(inputs) + list(outputs) + list(scratch)
-    dims = (micros, rows, width, ci, co, lanes_each, bits, share1, share2)
-    smem = pl.BlockSpec(memory_space=pltpu.SMEM)
+    dims = (micros, rows, width, ci, co, lanes_one, lanes_two, bits, share1, share2)
     vmem = pl.BlockSpec(memory_space=pltpu.VMEM)
     hbm = pl.BlockSpec(memory_space=pltpu.HBM)
-    large = ("img", "k1", "k2", "k0", "cot")
-    small = ("b1", "b2", "q1", "q2", "q0")
     results = pl.pallas_call(
         functools.partial(fused_kernel, names, n_rows, dims),
         out_shape=[pltpu.VMEM(a.shape, a.dtype) for a in outputs.values()],
-        in_specs=[smem, smem] + [vmem if n in small else hbm for n in list(inputs)[2:]],
+        in_specs=[hbm] * len(inputs),
         out_specs=[vmem] * len(outputs),
         scratch_shapes=list(scratch.values()),
         compiler_params=pltpu.CompilerParams(
             collective_id=0, has_side_effects=True, vmem_limit_bytes=48 * 1024 * 1024
         ),
         name="down_block",
-    )(*[pltpu.with_memory_space_constraint(a, pltpu.HBM) if n in large else a for n, a in inputs.items()])
+    )(*[pltpu.with_memory_space_constraint(a, pltpu.HBM) for a in inputs.values()])
     out_b, out_g, out_k1, out_k2, out_k0, out_b1, out_b2 = hand_over(results)
     return (
         out_b,

time: 47.6 us -> 46.3 us (0.973)
  local copies, waits for them, and re-layouts: 0.69 us -> 0 us
    unnamed x14 -> x0, local copies, waits for them, and re-layouts: 0.69 us -> none
where the time goes in v5:
time: 46.3 us; the launch traced here: 46.2 us
  Pallas kernels  45.5 us (98%)
  between operations  0.65 us (1%)
    pallas_call x1, Pallas kernels, fused(): pl.pallas_call(functools.partial(fused_kernel, names, n_rows, dims), out_...  44 us
    pallas_call x1, Pallas kernels, hand_over(): pl.pallas_call(copy_all, out_shape=[jax.ShapeDtypeStruct(a.shape, a.dtype...  1.47 us

profile of v5, /device:TPU:0, one launch (start us, length us, event | category | flops | bytes accessed | tf_op | source)
XLA Modules:
  0.0 46.2 jit_solution(2931419514723783231)
XLA Ops:
  0.6 44.0 %down_block.1 = (bf16[4,8,32,96]{3,2,1,0:T(8,128)(2,1)S(1)}, bf16[4,16,48,64]{3,2,1,0:T(8,128)(2,1)S(1)}, f32[864,96]{1,0:T(8,128)S(1)}, f32[1728,96]{1,0:T(8,12...) custom-call(s32[4,4]{1,0:T(4,128)} %refs_0_.1, s32[4,4]{1,0:T(4,128)} %refs_1_.1, ...), custom_call_target="tpu_custom_call" | custom-call | tf_op jit(solution)/shard_map/down_block/pallas_call | solution.py:1164
  44.7 1.5 %hand_over.1 = (bf16[4,8,32,96]{3,2,1,0:T(8,128)(2,1)}, bf16[4,16,48,64]{3,2,1,0:T(8,128)(2,1)}, f32[864,96]{1,0:T(8,128)}, f32[1728,96]{1,0:T(8,128)}, f32[96,9...) custom-call(bf16[4,8,32,96]{3,2,1,0:T(8,128)(2,1)S(1)} %get-tuple-element.21.refs_0_, ...), custom_call_target="tpu_custom_call" | custom-call | tf_op jit(solution)/shard_map/hand_over/pallas_call | solution.py:1040

commit v6 on v5

--- a/solution.py
+++ b/solution.py
@@ -288,8 +288,12 @@
     return left, image * scale, square * scale
 
 
+def sigmoid(value):
+    return 0.5 * jnp.tanh(0.5 * value) + 0.5
+
+
 def slope(value):
-    gate = 1.0 / (1.0 + jnp.exp(-value))
+    gate = sigmoid(value)
     return gate + value * gate * (1.0 - gate)
 
 
@@ -556,7 +560,7 @@
                     (choose(seg, base) + row < choose(seg, high[j])) & (column < choose(seg, wide[j])), 1.0, 0.0
                 )
                 x = jnp.concatenate([imgr[j, 0, p], imgr[j, 1, p]], axis=0).astype(F32) * mask
-                act = x / (1.0 + jnp.exp(-x))
+                act = x * sigmoid(x)
                 acts += [act.astype(BF16), ones]
                 plain += [x.astype(BF16), ones]
                 slots.append(2 * p + 2 * seg)
@@ -607,7 +611,7 @@
             acts = []
             for b in range(2):
                 pre = raw1[j, b, i] * scale1 + bias1
-                gate = 1.0 / (1.0 + jnp.exp(-pre))
+                gate = sigmoid(pre)
                 mask = 2 * pixel + b < broad
                 lift = pre * gate
                 grad1[j, b, i] = jnp.where(mask, gate + lift * (1.0 - gate), 0.0)
@@ -622,7 +626,7 @@
             cols[j, 2, i] = odd + after
             return carry
 
-        lax.fori_loop(0, 2 * seg_out, line, 0, unroll=2)
+        lax.fori_loop(0, 2 * seg_out, line, 0, unroll=True)
 
     box = ref["box"]
 
@@ -642,7 +646,7 @@
                     box[j, i, :, tap * op : (tap + 1) * op] = (upper + lower).astype(BF16)
             return carry
 
-        lax.fori_loop(0, pairs, line, 0, unroll=2)
+        lax.fori_loop(0, pairs, line, 0, unroll=True)
 
     quart = ref["quart"]
 
@@ -825,7 +829,7 @@
                 one = one + own_odd * odd.astype(F32) * raw1[j, b, 2 * i]
             return one, two
 
-        return lax.fori_loop(0, pairs + 1, line, dots, unroll=3)
+        return lax.fori_loop(0, pairs + 1, line, dots, unroll=True)
 
     back_taps()
     group_a.to_owners()
@@ -949,7 +953,7 @@
             send_g[j, p] = other
             return carry
 
-        lax.fori_loop(0, pairs, two_rows, 0, unroll=4)
+        lax.fori_loop(0, pairs, two_rows, 0, unroll=True)
         return begin(send_g.at[j], got_g.at[j], (me, o))
 
     def unpack(j):

time: 46.3 us -> 45.2 us (0.976)
  Pallas kernels: 45.5 us -> 44.2 us
    pallas_call x1, Pallas kernels: 44 us -> 42.7 us  [fused(): pl.pallas_call(functools.partial(fused_kernel, names, n_rows, dims), out_...]
where the time goes in v6:
time: 45.2 us; the launch traced here: 45 us
  Pallas kernels  44.2 us (98%)
  between operations  0.81 us (2%)
    pallas_call x1, Pallas kernels, fused(): pl.pallas_call(functools.partial(fused_kernel, names, n_rows, dims), out_...  42.7 us
    pallas_call x1, Pallas kernels, hand_over(): pl.pallas_call(copy_all, out_shape=[jax.ShapeDtypeStruct(a.shape, a.dtype...  1.47 us

profile of v6, /device:TPU:0, one launch (start us, length us, event | category | flops | bytes accessed | tf_op | source)
XLA Modules:
  0.0 45.0 jit_solution(1814096736856658013)
XLA Ops:
  0.6 42.7 %down_block.1 = (bf16[4,8,32,96]{3,2,1,0:T(8,128)(2,1)S(1)}, bf16[4,16,48,64]{3,2,1,0:T(8,128)(2,1)S(1)}, f32[864,96]{1,0:T(8,128)S(1)}, f32[1728,96]{1,0:T(8,12...) custom-call(s32[4,4]{1,0:T(4,128)} %refs_0_.1, s32[4,4]{1,0:T(4,128)} %refs_1_.1, ...), custom_call_target="tpu_custom_call" | custom-call | tf_op jit(solution)/shard_map/down_block/pallas_call | solution.py:1168
  43.4 1.5 %hand_over.1 = (bf16[4,8,32,96]{3,2,1,0:T(8,128)(2,1)}, bf16[4,16,48,64]{3,2,1,0:T(8,128)(2,1)}, f32[864,96]{1,0:T(8,128)}, f32[1728,96]{1,0:T(8,128)}, f32[96,9...) custom-call(bf16[4,8,32,96]{3,2,1,0:T(8,128)(2,1)S(1)} %get-tuple-element.21.refs_0_, ...), custom_call_target="tpu_custom_call" | custom-call | tf_op jit(solution)/shard_map/hand_over/pallas_call | solution.py:1044

commit v7 on v6

--- a/solution.py
+++ b/solution.py
@@ -339,6 +339,7 @@
     for delta in range(1, 2 * sub):
         other = lax.rem(2 * spot_in + core + delta, 2 * sub)
         around.append((2 * cube * sub + other, c))
+    same_core = [(2 * (cube * sub + lax.rem(spot_in + delta, sub)) + core, c) for delta in range(1, sub)]
     near = [(me, o), (mate, c), (up, c), (up, o), (down, c), (down, o)]
 
     barrier = pltpu.get_barrier_semaphore()
@@ -707,14 +708,19 @@
             self.mids[cube] = value.astype(BF16)
             self.copies = [begin(self.mids.at[cube], self.mids.at[cube], device) for device in across]
 
-        def to_all(self):
+        def forward(self):
+            self.arrived()
+            place_at = self.result.at[:, kept_rows]
+            self.copies = [begin(place_at, place_at, (mate, c))]
+
+        def to_all(self, direct=True):
             self.arrived()
             value = self.mids[0].astype(F32)
             for at in range(1, cubes):
                 value = value + self.mids[at].astype(F32)
             self.result[spot_in, kept_rows] = value.astype(BF16)
             place_at = self.result.at[spot_in, kept_rows]
-            self.copies = [begin(place_at, place_at, device) for device in around]
+            self.copies = [begin(place_at, place_at, device) for device in (around if direct else same_core)]
 
         def turned(self, scale, out, first, size):
             self.arrived()
@@ -969,18 +975,10 @@
     for j in range(1, per):
         conv_two(j)
     group_c.to_owners()
+    back_products(0)
     out_x = begin(send_b, got_b, (me, o))
-    back_products(0)
     group_a.to_cubes()
     grad_x = [input_rows(0)]
-    group_b.to_cubes()
-    for j in range(1, per):
-        back_products(j)
-        if j == 1:
-            group_c.to_cubes()
-            group_a.to_all()
-        grad_x.append(input_rows(j))
-
     def own_half(row):
         return jnp.where(c == 0, row[:, 0:co], row[:, co:cout])
 
@@ -1005,12 +1003,22 @@
             turned(columns[:, 0:some] * left[:, at : at + some], out, at)
 
     corr1, corr2, corr0 = ref["corr1"], ref["corr2"], ref["corr0"]
-    group_b.to_all()
     outer(compact(left1_ref[0:1], cin, TILE), right1 * (scale1 * scale1), corr1)
     outer(compact(left2_ref[0:1], cout, op), right2 * (scale2 * scale2), corr2)
     outer(left0_ref[0:1, 0:cin], right0 * (scale0 * scale0), corr0)
+    for j in range(1, per):
+        back_products(j)
+        if j == 1:
+            group_b.to_cubes()
+            group_a.to_all(False)
+        grad_x.append(input_rows(j))
+    group_c.to_cubes()
+
+    group_b.to_all(False)
     out_k1, out_k2, out_k0 = ref["out_k1"], ref["out_k2"], ref["out_k0"]
+    group_a.forward()
     group_c.to_all()
+    group_b.forward()
     group_a.turned(scale2, out_k2, 0, 5 * cout)
     out_x.wait_recv()
     out_b[mine_o] = got_b[...]

time: 45.2 us -> 44.6 us (0.987)
  Pallas kernels: 44.2 us -> 43.6 us
    pallas_call x1, Pallas kernels: 42.7 us -> 42.2 us  [fused(): pl.pallas_call(functools.partial(fused_kernel, names, n_rows, dims), out_...]
where the time goes in v7:
time: 44.6 us; the launch traced here: 44.4 us
  Pallas kernels  43.6 us (98%)
  between operations  0.81 us (2%)
    pallas_call x1, Pallas kernels, fused(): pl.pallas_call(functools.partial(fused_kernel, names, n_rows, dims), out_...  42.2 us
    pallas_call x1, Pallas kernels, hand_over(): pl.pallas_call(copy_all, out_shape=[jax.ShapeDtypeStruct(a.shape, a.dtype...  1.47 us

profile of v7, /device:TPU:0, one launch (start us, length us, event | category | flops | bytes accessed | tf_op | source)
XLA Modules:
  0.0 44.4 jit_solution(15193115861192969407)
XLA Ops:
  0.6 42.2 %down_block.1 = (bf16[4,8,32,96]{3,2,1,0:T(8,128)(2,1)S(1)}, bf16[4,16,48,64]{3,2,1,0:T(8,128)(2,1)S(1)}, f32[864,96]{1,0:T(8,128)S(1)}, f32[1728,96]{1,0:T(8,12...) custom-call(s32[4,4]{1,0:T(4,128)} %refs_0_.1, s32[4,4]{1,0:T(4,128)} %refs_1_.1, ...), custom_call_target="tpu_custom_call" | custom-call | tf_op jit(solution)/shard_map/down_block/pallas_call | solution.py:1176
  42.8 1.5 %hand_over.1 = (bf16[4,8,32,96]{3,2,1,0:T(8,128)(2,1)}, bf16[4,16,48,64]{3,2,1,0:T(8,128)(2,1)}, f32[864,96]{1,0:T(8,128)}, f32[1728,96]{1,0:T(8,128)}, f32[96,9...) custom-call(bf16[4,8,32,96]{3,2,1,0:T(8,128)(2,1)S(1)} %get-tuple-element.21.refs_0_, ...), custom_call_target="tpu_custom_call" | custom-call | tf_op jit(solution)/shard_map/hand_over/pallas_call | solution.py:1052

commit v8 on v7

--- a/solution.py
+++ b/solution.py
@@ -340,10 +340,11 @@
         other = lax.rem(2 * spot_in + core + delta, 2 * sub)
         around.append((2 * cube * sub + other, c))
     same_core = [(2 * (cube * sub + lax.rem(spot_in + delta, sub)) + core, c) for delta in range(1, sub)]
-    near = [(me, o), (mate, c), (up, c), (up, o), (down, c), (down, o)]
 
     barrier = pltpu.get_barrier_semaphore()
-    for device in near + far + across + around:
+    plane = [(2 * (cube * sub + lax.rem(spot_in + delta, sub)) + core, o) for delta in range(sub)]
+    greeted = [(up, o), (down, o), (up, c), (down, c)] + across + plane + around
+    for device in greeted:
         pl.semaphore_signal(barrier, inc=1, device_id=device, device_id_type=MESH)
 
     count = [0]
@@ -463,7 +464,7 @@
     for j in range(per):
         cotp[j] = packed(cot[o * per + j].reshape(own_px, co))
 
-    pl.semaphore_wait(barrier, len(near + far + across + around))
+    pl.semaphore_wait(barrier, len(greeted))
 
     k1h, k20h, coth, cotr = ref["k1h"], ref["k20h"], ref["coth"], ref["cotr"]
     spots = [core] + [lax.rem(me // 2**b, 2) for b in range(1, bits)]

time: 44.6 us -> 44.7 us (level)
  no operation moved by 1% of the time
where the time goes in v8:
time: 44.7 us; the launch traced here: 44.5 us
  Pallas kernels  43.7 us (98%)
  between operations  0.81 us (2%)
    pallas_call x1, Pallas kernels, fused(): pl.pallas_call(functools.partial(fused_kernel, names, n_rows, dims), out_...  42.2 us
    pallas_call x1, Pallas kernels, hand_over(): pl.pallas_call(copy_all, out_shape=[jax.ShapeDtypeStruct(a.shape, a.dtype...  1.47 us

profile of v8, /device:TPU:0, one launch (start us, length us, event | category | flops | bytes accessed | tf_op | source)
XLA Modules:
  0.0 44.5 jit_solution(14194671650002196962)
XLA Ops:
  0.6 42.2 %down_block.1 = (bf16[4,8,32,96]{3,2,1,0:T(8,128)(2,1)S(1)}, bf16[4,16,48,64]{3,2,1,0:T(8,128)(2,1)S(1)}, f32[864,96]{1,0:T(8,128)S(1)}, f32[1728,96]{1,0:T(8,12...) custom-call(s32[4,4]{1,0:T(4,128)} %refs_0_.1, s32[4,4]{1,0:T(4,128)} %refs_1_.1, ...), custom_call_target="tpu_custom_call" | custom-call | tf_op jit(solution)/shard_map/down_block/pallas_call | solution.py:1177
  42.9 1.5 %hand_over.1 = (bf16[4,8,32,96]{3,2,1,0:T(8,128)(2,1)}, bf16[4,16,48,64]{3,2,1,0:T(8,128)(2,1)}, f32[864,96]{1,0:T(8,128)}, f32[1728,96]{1,0:T(8,128)}, f32[96,9...) custom-call(bf16[4,8,32,96]{3,2,1,0:T(8,128)(2,1)S(1)} %get-tuple-element.21.refs_0_, ...), custom_call_target="tpu_custom_call" | custom-call | tf_op jit(solution)/shard_map/hand_over/pallas_call | solution.py:1053
